TPU v7x, 32 devices: a whole 2x2x4 slice. The times are simulated.
32 devices in a mesh: dp: 8 (over z, x), tensor: 4 (over y, core).
Axes of the slice: x: 2, y: 2, z: 4, core: 2. Of those that a mesh axis runs over, the one named last changes fastest.
Arguments:
- image: bfloat16 [16, 1024, 1536], P('dp', 'tensor'), may hold values from -6 to 6
- text: bfloat16 [16, 152, 1536], P('dp', 'tensor'), may hold values from -6 to 6
- cond: bfloat16 [16, 1536], P('dp'), may hold values from -6 to 6
- teacher_image: bfloat16 [16, 1024, 1536], P('dp', 'tensor'), may hold values from -8 to 8
- teacher_text: bfloat16 [16, 152, 1536], P('dp', 'tensor'), may hold values from -8 to 8
- grad_image: bfloat16 [16, 1024, 1536], P('dp', 'tensor'), may hold values from -8 to 8
- grad_text: bfloat16 [16, 152, 1536], P('dp', 'tensor'), may hold values from -8 to 8
- live: int32 [16], P('dp'), may hold values from 0 to 1, as said below
- w_mod: bfloat16 [2, 1536, 9216], P(None, 'dp', 'tensor'), may hold values from -0.15625 to 0.15625
- w_qkv: bfloat16 [2, 3, 24, 64, 1536], P(None, None, 'tensor', 'dp'), may hold values from -0.15625 to 0.15625
- w_out: bfloat16 [2, 24, 64, 1536], P(None, 'tensor', 'dp'), may hold values from -3 to 3
- w_up: bfloat16 [2, 1536, 6144], P(None, 'dp', 'tensor'), may hold values from -0.15625 to 0.15625
- w_down: bfloat16 [2, 1536, 6144], P(None, 'dp', 'tensor'), may hold values from -0.078125 to 0.078125
Outputs:
- loss: float32 [], replicated
- grad_mod: float32 [2, 1536, 9216], P(None, 'dp', 'tensor')
- grad_qkv: float32 [2, 3, 24, 64, 1536], P(None, None, 'tensor', 'dp')
- grad_out: float32 [2, 24, 64, 1536], P(None, 'tensor', 'dp')
- grad_up: float32 [2, 1536, 6144], P(None, 'dp', 'tensor')
- grad_down: float32 [2, 1536, 6144], P(None, 'dp', 'tensor')
- grad_image_in: float32 [16, 1024, 1536], P('dp', 'tensor')
- grad_text_in: float32 [16, 152, 1536], P('dp', 'tensor')
- grad_cond: float32 [16, 1536], P('dp')
Inputs may be any that keep to these rules, and one draw needn't show every extreme that they name: Slot 2 * r + j lies on data rank r. On each rank the live slots are the first ones, 1 to 2 of them. Rank r and rank r + 8 / 2 together hold 3 live slots, so some rank has all 2 live.
All inputs are finite; a program needn't handle non-finite values.
Results may differ from a plain program's by a relative error of at most 0.0085.
The roundings to bfloat16 on the way count: a program that leaves them out, or rounds other values in their place, can miss the bound.
Values may be sent and summed in bfloat16 or wider, within the bound.
A program may use at most 384 MiB of HBM per device.

v0:
```python
from functools import partial

import jax
import jax.numpy as jnp
from jax import lax
from jax.sharding import PartitionSpec as P

norm_eps = 1e-06


def project(rows, weight):
    flat = rows.reshape(-1, rows.shape[-1])
    result = jnp.dot(flat, weight, preferred_element_type=jnp.float32)
    return result.reshape(rows.shape[:-1] + (weight.shape[-1],))


def project_back(rows, weight):
    flat = rows.reshape(-1, rows.shape[-1])
    result = lax.dot_general(
        flat, weight, (((1,), (1,)), ((), ())), preferred_element_type=jnp.float32
    )
    return result.reshape(rows.shape[:-1] + (weight.shape[0],))


def outer_sum(left, right):
    flat_left = left.reshape(-1, left.shape[-1])
    flat_right = right.reshape(-1, right.shape[-1])
    return lax.dot_general(
        flat_left, flat_right, (((0,), (0,)), ((), ())), preferred_element_type=jnp.float32
    )


def norm_forward(values):
    center = jnp.mean(values, -1, keepdims=True)
    spread = jnp.mean(jnp.square(values - center), -1, keepdims=True)
    rstd = lax.rsqrt(spread + norm_eps)
    return ((values - center) * rstd, rstd)


def norm_backward(grads, hats, rstd):
    first = jnp.mean(grads, -1, keepdims=True)
    second = jnp.mean(grads * hats, -1, keepdims=True)
    return rstd * (grads - first - hats * second)


def gather_rows(pair):
    return (
        lax.all_gather(pair[0], "tensor", axis=1, tiled=True),
        lax.all_gather(pair[1], "tensor", axis=1, tiled=True),
    )


def scatter_rows(pair):
    return (
        lax.psum_scatter(pair[0], "tensor", scatter_dimension=1, tiled=True),
        lax.psum_scatter(pair[1], "tensor", scatter_dimension=1, tiled=True),
    )


def gather_grads(pair):
    return (
        lax.all_gather(pair[0], "tensor", axis=1, tiled=True),
        lax.all_gather(pair[1], "tensor", axis=1, tiled=True),
    )


def scatter_grads(pair):
    return (
        lax.psum_scatter(pair[0], "tensor", scatter_dimension=1, tiled=True),
        lax.psum_scatter(pair[1], "tensor", scatter_dimension=1, tiled=True),
    )


def attend(item):
    query, key, value = item
    factor = query.shape[-1] ** (-0.5)
    scores = (
        lax.dot_general(query, key, (((1,), (1,)), ((), ())), preferred_element_type=jnp.float32)
        * factor
    )
    top = jnp.max(scores, -1, keepdims=True)
    expd = jnp.exp(scores - top)
    total = jnp.sum(expd, -1, keepdims=True)
    probs = (expd / total).astype(jnp.bfloat16)
    result = jnp.dot(probs, value, preferred_element_type=jnp.float32).astype(jnp.bfloat16)
    return (result, (top + jnp.log(total))[:, 0])


def attend_back(item):
    query, key, value, logsum, grad_result = item
    factor = query.shape[-1] ** (-0.5)
    scores = (
        lax.dot_general(query, key, (((1,), (1,)), ((), ())), preferred_element_type=jnp.float32)
        * factor
    )
    probs = jnp.exp(scores - logsum[:, None])
    grad_probs = lax.dot_general(
        grad_result, value, (((1,), (1,)), ((), ())), preferred_element_type=jnp.float32
    )
    grad_value = lax.dot_general(
        probs.astype(jnp.bfloat16),
        grad_result,
        (((0,), (0,)), ((), ())),
        preferred_element_type=jnp.float32,
    )
    grad_scores = (probs * (grad_probs - jnp.sum(grad_probs * probs, -1, keepdims=True))).astype(
        jnp.bfloat16
    )
    grad_query = (jnp.dot(grad_scores, key, preferred_element_type=jnp.float32) * factor).astype(
        jnp.bfloat16
    )
    grad_key = (
        lax.dot_general(
            grad_scores, query, (((0,), (0,)), ((), ())), preferred_element_type=jnp.float32
        )
        * factor
    ).astype(jnp.bfloat16)
    return (grad_query, grad_key, grad_value.astype(jnp.bfloat16))


def on_device(
    image,
    text,
    cond,
    teacher_image,
    teacher_text,
    grad_image,
    grad_text,
    live,
    w_mod,
    w_qkv,
    w_out,
    w_up,
    w_down,
):
    f_mod, f_qkv, f_out, f_up, f_down = (
        lax.all_gather(w_mod, "dp", axis=1, tiled=True),
        lax.all_gather(w_qkv, "dp", axis=3, tiled=True),
        lax.all_gather(w_out, "dp", axis=2, tiled=True),
        lax.all_gather(w_up, "dp", axis=1, tiled=True),
        lax.all_gather(w_down, "dp", axis=1, tiled=True),
    )
    slots, width = cond.shape
    heads_local = f_qkv.shape[2]
    head_size = f_qkv.shape[3]
    inner_width = heads_local * head_size
    cond_f = cond.astype(jnp.float32)
    act = jax.nn.silu(cond_f).astype(jnp.bfloat16)
    mod_full = (
        lax.all_gather(project(act, f_mod[0]), "tensor", axis=1, tiled=True),
        lax.all_gather(project(act, f_mod[1]), "tensor", axis=1, tiled=True),
    )
    mods = [mod_full[s].reshape(slots, 6, width) for s in range(2)]
    inputs = (text.astype(jnp.float32), image.astype(jnp.float32))
    first_norm = [norm_forward(inputs[s]) for s in range(2)]
    hat_one = [first_norm[s][0] for s in range(2)]
    rstd_one = [first_norm[s][1] for s in range(2)]
    h_one = gather_rows(
        tuple(
            (
                (hat_one[s] * (1.0 + mods[s][:, 1][:, None]) + mods[s][:, 0][:, None]).astype(
                    jnp.bfloat16
                )
                for s in range(2)
            )
        )
    )
    text_len = h_one[0].shape[1]
    seq_len = text_len + h_one[1].shape[1]
    partial_count = jnp.sum(live).astype(jnp.float32) * seq_len
    count = lax.psum(partial_count, "dp")
    qkv = [
        project_back(h_one[s], f_qkv[s].reshape(3 * inner_width, width)).astype(jnp.bfloat16)
        for s in range(2)
    ]
    joined = jnp.concatenate(qkv, 1).reshape(slots, seq_len, 3, heads_local, head_size)
    items = joined.transpose(2, 0, 3, 1, 4).reshape(3, slots * heads_local, seq_len, head_size)
    attended, logsum = lax.map(attend, (items[0], items[1], items[2]))
    att_rows = (
        attended.reshape(slots, heads_local, seq_len, head_size)
        .transpose(0, 2, 1, 3)
        .reshape(slots, seq_len, inner_width)
    )
    att_pair = (att_rows[:, :text_len], att_rows[:, text_len:])
    y_pair = scatter_rows(
        tuple((project(att_pair[s], f_out[s].reshape(inner_width, width)) for s in range(2)))
    )
    middle = [inputs[s] + mods[s][:, 2][:, None] * y_pair[s] for s in range(2)]
    second_norm = [norm_forward(middle[s]) for s in range(2)]
    hat_two = [second_norm[s][0] for s in range(2)]
    rstd_two = [second_norm[s][1] for s in range(2)]
    h_two = gather_rows(
        tuple(
            (
                (hat_two[s] * (1.0 + mods[s][:, 4][:, None]) + mods[s][:, 3][:, None]).astype(
                    jnp.bfloat16
                )
                for s in range(2)
            )
        )
    )
    before = [project(h_two[s], f_up[s]) for s in range(2)]
    hidden = [jax.nn.gelu(before[s], approximate=True).astype(jnp.bfloat16) for s in range(2)]
    m_pair = scatter_rows(tuple((project_back(hidden[s], f_down[s]) for s in range(2))))
    outputs = [middle[s] + mods[s][:, 5][:, None] * m_pair[s] for s in range(2)]
    mask = live.astype(jnp.float32)[:, None, None]
    teachers = (teacher_text, teacher_image)
    givens = (grad_text, grad_image)
    errors = [outputs[s] - teachers[s].astype(jnp.float32) for s in range(2)]
    partial_loss = jnp.sum(mask * errors[0] * errors[0]) + jnp.sum(mask * errors[1] * errors[1])
    total = lax.psum(partial_loss, ("dp", "tensor"))
    loss = total / (count * width)
    cot = [mask * (givens[s].astype(jnp.float32) + 2.0 * errors[s]) for s in range(2)]
    grad_gate_two = [jnp.sum(cot[s] * m_pair[s], 1) for s in range(2)]
    grad_m = gather_grads(
        tuple(((cot[s] * mods[s][:, 5][:, None]).astype(jnp.bfloat16) for s in range(2)))
    )
    g_down = [outer_sum(grad_m[s], hidden[s]) for s in range(2)]
    grad_pre = []
    for s in range(2):
        grad_hidden = project(grad_m[s], f_down[s])
        unused, pull = jax.vjp(partial(jax.nn.gelu, approximate=True), before[s])
        grad_pre.append(pull(grad_hidden)[0].astype(jnp.bfloat16))
    g_up = [outer_sum(h_two[s], grad_pre[s]) for s in range(2)]
    grad_h_two = scatter_grads(tuple((project_back(grad_pre[s], f_up[s]) for s in range(2))))
    grad_shift_two = [jnp.sum(grad_h_two[s], 1) for s in range(2)]
    grad_scale_two = [jnp.sum(grad_h_two[s] * hat_two[s], 1) for s in range(2)]
    back_two = [
        norm_backward(grad_h_two[s] * (1.0 + mods[s][:, 4][:, None]), hat_two[s], rstd_two[s])
        for s in range(2)
    ]
    grad_mid = [cot[s] + back_two[s] for s in range(2)]
    grad_gate_one = [jnp.sum(grad_mid[s] * y_pair[s], 1) for s in range(2)]
    grad_y = gather_grads(
        tuple(((grad_mid[s] * mods[s][:, 2][:, None]).astype(jnp.bfloat16) for s in range(2)))
    )
    g_out = [
        outer_sum(att_pair[s], grad_y[s]).reshape(heads_local, head_size, width) for s in range(2)
    ]
    grad_att = [
        project_back(grad_y[s], f_out[s].reshape(inner_width, width)).astype(jnp.bfloat16)
        for s in range(2)
    ]
    grad_items = (
        jnp.concatenate(grad_att, 1)
        .reshape(slots, seq_len, heads_local, head_size)
        .transpose(0, 2, 1, 3)
        .reshape(slots * heads_local, seq_len, head_size)
    )
    grad_query, grad_key, grad_value = lax.map(
        attend_back, (items[0], items[1], items[2], logsum, grad_items)
    )
    grad_qkv = (
        jnp.stack((grad_query, grad_key, grad_value))
        .reshape(3, slots, heads_local, seq_len, head_size)
        .transpose(1, 3, 0, 2, 4)
        .reshape(slots, seq_len, 3 * inner_width)
    )
    grad_qkv_pair = (grad_qkv[:, :text_len], grad_qkv[:, text_len:])
    g_qkv = [
        outer_sum(grad_qkv_pair[s], h_one[s]).reshape(3, heads_local, head_size, width)
        for s in range(2)
    ]
    grad_h_one = scatter_grads(
        tuple(
            (project(grad_qkv_pair[s], f_qkv[s].reshape(3 * inner_width, width)) for s in range(2))
        )
    )
    grad_shift_one = [jnp.sum(grad_h_one[s], 1) for s in range(2)]
    grad_scale_one = [jnp.sum(grad_h_one[s] * hat_one[s], 1) for s in range(2)]
    back_one = [
        norm_backward(grad_h_one[s] * (1.0 + mods[s][:, 1][:, None]), hat_one[s], rstd_one[s])
        for s in range(2)
    ]
    grad_inputs = [grad_mid[s] + back_one[s] for s in range(2)]
    mod_terms = tuple(
        (
            jnp.stack(
                (
                    grad_shift_one[s],
                    grad_scale_one[s],
                    grad_gate_one[s],
                    grad_shift_two[s],
                    grad_scale_two[s],
                    grad_gate_two[s],
                ),
                1,
            ).reshape(slots, -1)
            for s in range(2)
        )
    )
    mod_summed = (
        lax.psum_scatter(mod_terms[0], "tensor", scatter_dimension=1, tiled=True),
        lax.psum_scatter(mod_terms[1], "tensor", scatter_dimension=1, tiled=True),
    )
    g_mod = []
    cond_part = jnp.zeros((slots, width), jnp.float32)
    for s in range(2):
        grad_mods = mod_summed[s].astype(jnp.bfloat16)
        g_mod.append(outer_sum(act, grad_mods))
        cond_part = cond_part + project_back(grad_mods, f_mod[s])
    cond_total = lax.psum(cond_part, "tensor")
    unused_value, silu_pull = jax.vjp(jax.nn.silu, cond_f)
    grad_cond = silu_pull(cond_total)[0]
    done_mod, done_qkv, done_out, done_up, done_down = (
        lax.psum_scatter(jnp.stack(g_mod), "dp", scatter_dimension=1, tiled=True),
        lax.psum_scatter(jnp.stack(g_qkv), "dp", scatter_dimension=3, tiled=True),
        lax.psum_scatter(jnp.stack(g_out), "dp", scatter_dimension=2, tiled=True),
        lax.psum_scatter(jnp.stack(g_up), "dp", scatter_dimension=1, tiled=True),
        lax.psum_scatter(jnp.stack(g_down), "dp", scatter_dimension=1, tiled=True),
    )
    return (
        loss,
        done_mod,
        done_qkv,
        done_out,
        done_up,
        done_down,
        grad_inputs[1],
        grad_inputs[0],
        grad_cond,
    )


def solution(mesh):
    return jax.shard_map(
        on_device,
        mesh=mesh,
        in_specs=(
            P("dp", "tensor", None),
            P("dp", "tensor", None),
            P("dp", None),
            P("dp", "tensor", None),
            P("dp", "tensor", None),
            P("dp", "tensor", None),
            P("dp", "tensor", None),
            P("dp"),
            P(None, "dp", "tensor"),
            P(None, None, "tensor", "dp", None),
            P(None, "tensor", "dp", None),
            P(None, "dp", "tensor"),
            P(None, "dp", "tensor"),
        ),
        out_specs=(
            P(),
            P(None, "dp", "tensor"),
            P(None, None, "tensor", "dp", None),
            P(None, "tensor", "dp", None),
            P(None, "dp", "tensor"),
            P(None, "dp", "tensor"),
            P("dp", "tensor", None),
            P("dp", "tensor", None),
            P("dp", None),
        ),
        check_vma=False,
    )
```

profile of v0, /device:TPU:0, one launch (start us, length us, event | category | flops | bytes accessed | tf_op | source)
XLA Modules:
  0.0 3349.2 jit_solution(584314777867812505)
XLA Ops:
  10.3 198.2 %all-gather.10.cloned.1.call-done = bf16[2,1536,2304]{2,1,0:T(8,128)(2,1)} async-done(((bf16[2,192,2304]{2,1,0:T(8,128)(2,1)}), bf16[2,1536,2304]{2,1,0:T(8,128)(2,1)}) %all-gather.10.cloned.1.call-update) | async-done | bytes 14155792 | tf_op jit(solution)/shard_map/all_gather | solution.py:137
  222.7 38.3 %all-gather.16.cloned.1.call-done = bf16[2,6,64,1536]{3,2,1,0:T(8,128)(2,1)} async-done(((bf16[2,6,8,1536]{3,2,1,0:T(8,128)(2,1)}), bf16[2,6,64,1536]{3,2,1,0:T(8,128)(2,1)}) %all-gather.16.cloned.1.call-update) | async-done | bytes 2359312 | tf_op jit(solution)/shard_map/all_gather | solution.py:139
  264.3 106.3 %all-gather.12.cloned.1.call-done = bf16[2,3,6,64,1536]{4,3,2,1,0:T(8,128)(2,1)} async-done(((bf16[2,3,6,8,1536]{4,3,2,1,0:T(8,128)(2,1)}), bf16[2,3,6,64,1536]{4,3,2,1,0:T(8,128)(2,1)}) %all-gather.12.cloned.1.call-update) | async-done | bytes 7077904 | tf_op jit(solution)/shard_map/all_gather | solution.py:138
  463.6 130.1 %while.26 = (s32[]{:T(128)}, bf16[12,1176,64]{1,2,0:T(8,128)(2,1)S(1)}, f32[12,1176]{1,0:T(8,128)}, bf16[12,1176,64]{2,1,0:T(8,128)(2,1)}, bf16[12,1176,64]{2,1,...) while((s32[]{:T(128)}, bf16[12,1176,64]{1,2,0:T(8,128)(2,1)S(1)}, ...), condition=%wide.region_7.8_spmd, body=%wide.region_4.7_spmd.sunk | while | flops 363796768 | bytes 40345140 | solution.py:178
  601.8 97.8 %reduce-scatter.16.cloned.1.call-done = f32[2,256,1536]{2,1,0:T(8,128)} async-done(((f32[2,1024,1536]{2,1,0:T(8,128)}), f32[2,256,1536]{2,1,0:T(8,128)}) %reduce-scatter.16.cloned.1.call-update) | async-done | bytes 3145744 | tf_op jit(solution)/shard_map/reduce_scatter | solution.py:56
  705.7 134.1 %all-gather.18.cloned.1.call-done = bf16[2,1536,1536]{2,1,0:T(8,128)(2,1)} async-done(((bf16[2,192,1536]{2,1,0:T(8,128)(2,1)}), bf16[2,1536,1536]{2,1,0:T(8,128)(2,1)}) %all-gather.18.cloned.1.call-update) | async-done | bytes 9437200 | tf_op jit(solution)/shard_map/all_gather | solution.py:140
  839.8 46.7 %all-gather.22.cloned.1.call-done = bf16[2,1024,1536]{2,1,0:T(8,128)(2,1)} async-done(((bf16[2,256,1536]{2,1,0:T(8,128)(2,1)}), bf16[2,1024,1536]{2,1,0:T(8,128)(2,1)}) %all-gather.22.cloned.1.call-update) | async-done | bytes 6291472 | tf_op jit(solution)/shard_map/all_gather | solution.py:49
  902.5 124.3 %all-gather.20.cloned.1.call-done = bf16[2,1536,1536]{2,1,0:T(8,128)(2,1)} async-done(((bf16[2,192,1536]{2,1,0:T(8,128)(2,1)}), bf16[2,1536,1536]{2,1,0:T(8,128)(2,1)}) %all-gather.20.cloned.1.call-update) | async-done | bytes 9437200 | tf_op jit(solution)/shard_map/all_gather | solution.py:141
  1050.1 91.8 %reduce-scatter.18.cloned.1.call-done = f32[2,256,1536]{2,1,0:T(8,128)} async-done(((f32[2,1024,1536]{2,1,0:T(8,128)}), f32[2,256,1536]{2,1,0:T(8,128)}) %reduce-scatter.18.cloned.1.call-update) | async-done | bytes 3145744 | tf_op jit(solution)/shard_map/reduce_scatter | solution.py:56
  1149.7 42.7 %all-reduce.9.cloned.1.call-done = f32[2,152,1536]{2,0,1:T(2,128)} async-done(((f32[2,152,1536]{2,0,1:T(2,128)}), f32[2,152,1536]{2,0,1:T(2,128)}) %all-reduce.9.cloned.1.call-update) | async-done | bytes 1867792
  1216.7 24.3 all-gather.24.cloned.1.call-done
  1241.0 22.1 fusion.58
  1319.0 74.3 %reduce-scatter.20.cloned.1.call-done = f32[2,256,1536]{2,1,0:T(8,128)} async-done(((f32[2,1024,1536]{2,1,0:T(8,128)}), f32[2,256,1536]{2,1,0:T(8,128)}) %reduce-scatter.20.cloned.1.call-update) | async-done | bytes 3145744 | tf_op jit(solution)/shard_map/reduce_scatter | solution.py:70
  1406.0 37.8 %all-reduce.13.cloned.1.call-done = f32[2,152,1536]{2,0,1:T(2,128)} async-done(((f32[2,152,1536]{2,0,1:T(2,128)}), f32[2,152,1536]{2,0,1:T(2,128)}) %all-reduce.13.cloned.1.call-update) | async-done | bytes 1867792
  1463.3 30.3 all-gather.26.cloned.1.call-done
  1505.6 155.7 %while.27 = (s32[]{:T(128)}, bf16[12,1176,64]{1,2,0:T(8,128)(2,1)S(1)}, bf16[12,1176,64]{1,2,0:T(8,128)(2,1)}, bf16[12,1176,64]{1,2,0:T(8,128)(2,1)}, bf16[12,11...) while((s32[]{:T(128)}, ...), condition=%wide.region_29.30_spmd, body=%wide.region_27.29_spmd.sunk | while | flops 896543552 | bytes 44087112 | solution.py:250
  1725.4 95.8 %reduce-scatter.22.cloned.1.call-done = f32[2,256,1536]{2,1,0:T(8,128)} async-done(((f32[2,1024,1536]{2,1,0:T(8,128)}), f32[2,256,1536]{2,1,0:T(8,128)}) %reduce-scatter.22.cloned.1.call-update) | async-done | bytes 3145744 | tf_op jit(solution)/shard_map/reduce_scatter | solution.py:70
  1972.6 23.1 psum.22
  1998.7 40.0 %psum.21 = f32[]{:T(128)} all-reduce(f32[]{:T(128)S(6)} %add.234), channel_id=1, replica_groups=mesh['dp'=8,'tensor'=4] {'dp','tensor'}, use_global_device_ids=true, to_apply=%region_18.19 | all-reduce | flops 1 | bytes 8 | tf_op jit(solution)/shard_map/psum | solution.py:211
  2066.6 173.7 %reduce-scatter.32.cloned.1.call-done = f32[2,192,1536]{2,1,0:T(8,128)} async-done(((f32[2,1536,1536]{2,1,0:T(8,128)}), f32[2,192,1536]{2,1,0:T(8,128)}) %reduce-scatter.32.cloned.1.call-update) | async-done | bytes 2359312 | tf_op jit(solution)/shard_map/reduce_scatter | solution.py:310
  2240.3 316.4 %reduce-scatter.30.cloned.1.call-done = f32[2,192,1536]{2,1,0:T(8,128)} async-done(((f32[2,1536,1536]{2,1,0:T(8,128)}), f32[2,192,1536]{2,1,0:T(8,128)}) %reduce-scatter.30.cloned.1.call-update) | async-done | bytes 2359312 | tf_op jit(solution)/shard_map/reduce_scatter | solution.py:309
  2556.7 98.7 %reduce-scatter.28.cloned.1.call-done = f32[2,6,8,1536]{3,2,1,0:T(8,128)} async-done(((f32[2,6,64,1536]{3,2,1,0:T(8,128)}), f32[2,6,8,1536]{3,2,1,0:T(8,128)}) %reduce-scatter.28.cloned.1.call-update) | async-done | bytes 589840 | tf_op jit(solution)/shard_map/reduce_scatter | solution.py:308
  2655.4 233.2 %reduce-scatter.26.cloned.1.call-done = f32[2,3,6,8,1536]{4,3,2,1,0:T(8,128)} async-done(((f32[2,3,6,64,1536]{4,3,2,1,0:T(8,128)}), f32[2,3,6,8,1536]{4,3,2,1,0:T(8,128)}) %reduce-scatter.26.cloned.1.call-update) | async-done | bytes 1769488 | tf_op jit(solution)/shard_map/reduce_scatter | solution.py:307
  2888.6 452.2 %reduce-scatter.24.cloned.1.call-done = f32[2,192,2304]{2,1,0:T(8,128)} async-done(((f32[2,1536,2304]{2,1,0:T(8,128)}), f32[2,192,2304]{2,1,0:T(8,128)}) %reduce-scatter.24.cloned.1.call-update) | async-done | bytes 3538960 | tf_op jit(solution)/shard_map/reduce_scatter | solution.py:306
  (569 shorter events, 825.1 us)
Async XLA Ops:
  7.2 201.4 %all-gather.10.cloned.1.call-start = ((), (), s32[]{:S(2)}) async-start(), calls=%async_computation.11 | async-start | bytes 15925248 | tf_op jit(solution)/shard_map/all_gather | solution.py:137
  7.9 253.1 %all-gather.16.cloned.1.call-start = ((), (), s32[]{:S(2)}) async-start(), calls=%async_computation.14 | async-start | bytes 2654208 | tf_op jit(solution)/shard_map/all_gather | solution.py:139
  8.7 362.0 %all-gather.12.cloned.1.call-start = ((), (), s32[]{:S(2)}) async-start(), calls=%async_computation.12 | async-start | bytes 7962624 | tf_op jit(solution)/shard_map/all_gather | solution.py:138
  9.4 413.2 %all-gather.14.cloned.1.call-start = ((), (), s32[]{:S(2)}) async-start(), calls=%async_computation.13 | async-start | bytes 7864320 | tf_op jit(solution)/shard_map/all_gather | solution.py:49
  221.2 478.5 %reduce-scatter.16.cloned.1.call-start = ((), (), s32[]{:S(2)}) async-start(), calls=%async_computation.17 | async-start | bytes 15728640 | tf_op jit(solution)/shard_map/reduce_scatter | solution.py:56
  600.6 239.2 %all-gather.18.cloned.1.call-start = ((), (), s32[]{:S(2)}) async-start(), calls=%async_computation.15 | async-start | bytes 10616832 | tf_op jit(solution)/shard_map/all_gather | solution.py:140
  601.2 285.3 %all-gather.22.cloned.1.call-start = ((), (), s32[]{:S(2)}) async-start(), calls=%async_computation.18 | async-start | bytes 7864320 | tf_op jit(solution)/shard_map/all_gather | solution.py:49
  704.9 321.9 %all-gather.20.cloned.1.call-start = ((), (), s32[]{:S(2)}) async-start(), calls=%async_computation.16 | async-start | bytes 10616832 | tf_op jit(solution)/shard_map/all_gather | solution.py:141
  705.7 436.2 %reduce-scatter.18.cloned.1.call-start = ((), (), s32[]{:S(2)}) async-start(), calls=%async_computation.19 | async-start | bytes 15728640 | tf_op jit(solution)/shard_map/reduce_scatter | solution.py:56
  1044.5 147.9 %all-reduce.9.cloned.1.call-start = ((), (), s32[]{:S(2)}) async-start(), calls=%async_computation.31 | async-start | bytes 3735552
  1049.3 191.7 %all-gather.24.cloned.1.call-start = ((), (), s32[]{:S(2)}) async-start(), calls=%async_computation.20 | async-start | bytes 7864320 | tf_op jit(solution)/shard_map/all_gather | solution.py:63
  1148.1 143.4 %all-reduce.11.cloned.1.call-start = ((), (), s32[]{:S(2)}) async-start(), calls=%async_computation.32 | async-start | bytes 3735552
  1216.6 176.7 %reduce-scatter.20.cloned.1.call-start = ((), (), s32[]{:S(2)}) async-start(), calls=%async_computation.21 | async-start | bytes 15728640 | tf_op jit(solution)/shard_map/reduce_scatter | solution.py:70
  1281.0 162.9 %all-reduce.13.cloned.1.call-start = ((), (), s32[]{:S(2)}) async-start(), calls=%async_computation.33 | async-start | bytes 3735552
  1319.0 174.7 %all-gather.26.cloned.1.call-start = ((), (), s32[]{:S(2)}) async-start(), calls=%async_computation.22 | async-start | bytes 7864320 | tf_op jit(solution)/shard_map/all_gather | solution.py:63
  1405.9 313.7 %all-reduce.15.cloned.1.call-start = ((), (), s32[]{:S(2)}) async-start(), calls=%async_computation.34 | async-start | bytes 3735552
  1671.4 149.8 %reduce-scatter.22.cloned.1.call-start = ((), (), s32[]{:S(2)}) async-start(), calls=%async_computation.23 | async-start | bytes 15728640 | tf_op jit(solution)/shard_map/reduce_scatter | solution.py:70
  1685.4 261.0 %reduce-scatter.34.cloned.1.call-start = ((), (), s32[]{:S(2)}) async-start(), calls=%async_computation.29 | async-start | bytes 5898240
  1725.4 229.8 %reduce-scatter.36.cloned.1.call-start = ((), (), s32[]{:S(2)}) async-start(), calls=%async_computation.30 | async-start | bytes 5898240
  1828.1 412.2 %reduce-scatter.32.cloned.1.call-start = ((), (), s32[]{:S(2)}) async-start(), calls=%async_computation.28 | async-start | bytes 21233664 | tf_op jit(solution)/shard_map/reduce_scatter | solution.py:310
  1843.9 712.8 %reduce-scatter.30.cloned.1.call-start = ((), (), s32[]{:S(2)}) async-start(), calls=%async_computation.27 | async-start | bytes 21233664 | tf_op jit(solution)/shard_map/reduce_scatter | solution.py:309
  1869.0 786.4 %reduce-scatter.28.cloned.1.call-start = ((), (), s32[]{:S(2)}) async-start(), calls=%async_computation.26 | async-start | bytes 5308416 | tf_op jit(solution)/shard_map/reduce_scatter | solution.py:308
  1888.1 1000.5 %reduce-scatter.26.cloned.1.call-start = ((), (), s32[]{:S(2)}) async-start(), calls=%async_computation.25 | async-start | bytes 15925248 | tf_op jit(solution)/shard_map/reduce_scatter | solution.py:307
  1946.1 1394.7 %reduce-scatter.24.cloned.1.call-start = ((), (), s32[]{:S(2)}) async-start(), calls=%async_computation.24 | async-start | bytes 31850496 | tf_op jit(solution)/shard_map/reduce_scatter | solution.py:306
  (104 other events, 3063.8 us)
Sparse Core Ops, SparseCore 0:
  10.2 198.3 all-gather.9
  210.8 50.2 all-gather.15
  263.3 107.3 all-gather.11
  372.6 49.9 all-gather.13
  600.8 98.8 reduce-scatter.15
  701.7 138.0 all-gather.17
  841.9 44.5 all-gather.21
  888.7 138.0 all-gather.19
  1044.6 97.2 reduce-scatter.17
  1144.7 47.6 all-reduce.8
  1194.5 46.4 all-gather.23
  1243.8 47.6 all-reduce.10
  1294.1 99.2 reduce-scatter.19
  1396.1 47.6 all-reduce.12
  1445.8 47.7 all-gather.25
  1671.5 48.0 all-reduce.14
  1722.1 99.1 reduce-scatter.21
  1823.6 47.8 reduce-scatter.33
  1874.2 47.8 reduce-scatter.35
  1926.4 313.9 reduce-scatter.31
  2244.8 311.8 reduce-scatter.29
  2560.9 94.4 reduce-scatter.27
  2659.6 228.9 reduce-scatter.25
  2892.9 447.7 reduce-scatter.23
where the time goes:
time: 3360 us; the launch traced here: 3350 us
  waiting for transfers between devices  2450 us (73%)
  matrix products  430 us (13%)
  local copies, waits for them, and re-layouts  181 us (5%)
  other arithmetic  131 us (4%)
  blocking collectives  131 us (4%)
    reduce_scatter x1, waiting for transfers between devices, on_device(): lax.psum_scatter(jnp.stack(g_mod), 'dp', scatter_dimension=1, tiled=True)  452 us
    reduce_scatter x1, waiting for transfers between devices, on_device(): lax.psum_scatter(jnp.stack(g_up), 'dp', scatter_dimension=1, tiled=True)  316 us
    reduce_scatter x1, waiting for transfers between devices, on_device(): lax.psum_scatter(jnp.stack(g_qkv), 'dp', scatter_dimension=3, tiled=True)  233 us
    all_gather x1, waiting for transfers between devices, on_device(): lax.all_gather(w_mod, 'dp', axis=1, tiled=True)  198 us
    reduce_scatter x2, waiting for transfers between devices, scatter_rows(): lax.psum_scatter(pair[1], 'tensor', scatter_dimension=1, tiled=True)  190 us
    reduce_scatter x1, waiting for transfers between devices, on_device(): lax.psum_scatter(jnp.stack(g_down), 'dp', scatter_dimension=1, tiled=True)  174 us
    reduce_scatter x2, waiting for transfers between devices, scatter_grads(): lax.psum_scatter(pair[1], 'tensor', scatter_dimension=1, tiled=True)  170 us
    all_gather x1, waiting for transfers between devices, on_device(): lax.all_gather(w_up, 'dp', axis=1, tiled=True)  134 us
  transfers between devices with their start and end apart: 24, of which 22 were waited for; matrix products, arithmetic and copies ran while one was open for 10% of the time, Pallas kernels for 0%

commit v1 on v0

v1 whole, which is shorter than its diff:
```python
import math
from functools import partial

import jax
import jax.numpy as jnp
from jax import lax
from jax.experimental import pallas as pl
from jax.experimental.pallas import tpu as pltpu
from jax.sharding import PartitionSpec as P

norm_eps = 1e-06

LOG2E = math.log2(math.e)
HEAD = 64


def nt(a, b):
    return lax.dot_general(a, b, (((1,), (1,)), ((), ())), preferred_element_type=jnp.float32)


def nn(a, b):
    return jnp.dot(a, b, preferred_element_type=jnp.float32)


def query_blocks(rows_img, rows_txt):
    step = 256 if rows_img % 256 == 0 else rows_img
    return [(0, s, step) for s in range(0, rows_img, step)] + [(1, 0, rows_txt)]


def pad_bias(rows, block, valid):
    place = lax.broadcasted_iota(jnp.int32, (rows, 1), 0)
    return jnp.where(lax.rem(place, block) < valid, 0.0, -1e30).astype(jnp.float32)


def attend_kernel(block, valid, qi, ki, vi, qt, kt, vt, oi, ot, lse):
    factor = HEAD**-0.5
    low = lax.broadcasted_iota(jnp.int32, (1, 2 * HEAD), 1) < HEAD
    zero = jnp.zeros((), jnp.bfloat16)
    bias = pad_bias(qt.shape[0], block, valid)
    vit, vtt = vi[...].T, vt[...].T
    keys = []
    for h in range(2):
        mask = low if h == 0 else ~low
        keys.append((jnp.where(mask, ki[...], zero), jnp.where(mask, kt[...], zero)))
    at = 0
    for which, start, size in query_blocks(qi.shape[0], qt.shape[0]):
        src, dst = (qi, oi) if which == 0 else (qt, ot)
        q = src[start : start + size, :]
        parts = []
        for h in range(2):
            s_i = nt(keys[h][0], q)
            s_t = nt(keys[h][1], q) + bias
            top = jnp.maximum(
                jnp.max(s_i, 0, keepdims=True), jnp.max(s_t, 0, keepdims=True)
            )
            e_i = jnp.exp2((s_i - top) * (factor * LOG2E))
            e_t = jnp.exp2((s_t - top) * (factor * LOG2E))
            total = jnp.sum(e_i, 0, keepdims=True) + jnp.sum(e_t, 0, keepdims=True)
            inv = 1.0 / total
            p_i = (e_i * inv).astype(jnp.bfloat16)
            p_t = (e_t * inv).astype(jnp.bfloat16)
            rows = slice(h * HEAD, (h + 1) * HEAD)
            parts.append(nn(vit[rows], p_i) + nn(vtt[rows], p_t))
            lse[0, h : h + 1, at : at + size] = top * (factor * LOG2E) + jnp.log2(total)
        dst[start : start + size, :] = jnp.concatenate(parts, 0).T.astype(jnp.bfloat16)
        at += size


def back_kernel(block, valid, qi, ki, vi, qt, kt, vt, gi, gt, lse,
                dqi, dki, dvi, dqt, dkt, dvt, aki, avi, akt, avt):
    factor = HEAD**-0.5
    low = lax.broadcasted_iota(jnp.int32, (1, 2 * HEAD), 1) < HEAD
    zero = jnp.zeros((), jnp.bfloat16)
    bias = pad_bias(qt.shape[0], block, valid)
    kit, ktt = ki[...].T, kt[...].T
    masks = [low, ~low]
    at = 0
    first = True
    for which, start, size in query_blocks(qi.shape[0], qt.shape[0]):
        q_ref, g_ref, d_ref = (qi, gi, dqi) if which == 0 else (qt, gt, dqt)
        q, g = q_ref[start : start + size, :], g_ref[start : start + size, :]
        parts = []
        for h in range(2):
            q_h, g_h = jnp.where(masks[h], q, zero), jnp.where(masks[h], g, zero)
            stat = lse[0, h : h + 1, at : at + size]
            p_i = jnp.exp2(nt(ki[...], q_h) * (factor * LOG2E) - stat)
            p_t = jnp.exp2((nt(kt[...], q_h) + bias) * (factor * LOG2E) - stat)
            d_i, d_t = nt(vi[...], g_h), nt(vt[...], g_h)
            delta = jnp.sum(d_i * p_i, 0, keepdims=True) + jnp.sum(d_t * p_t, 0, keepdims=True)
            s_i = (p_i * (d_i - delta)).astype(jnp.bfloat16)
            s_t = (p_t * (d_t - delta)).astype(jnp.bfloat16)
            v_i = nn(p_i.astype(jnp.bfloat16), g_h)
            v_t = nn(p_t.astype(jnp.bfloat16), g_h)
            k_i = nn(s_i, q_h)
            k_t = nn(s_t, q_h)
            if first:
                avi[...], avt[...], aki[...], akt[...] = v_i, v_t, k_i, k_t
                first = False
            else:
                avi[...] += v_i
                avt[...] += v_t
                aki[...] += k_i
                akt[...] += k_t
            rows = slice(h * HEAD, (h + 1) * HEAD)
            parts.append(nn(kit[rows], s_i) + nn(ktt[rows], s_t))
        d_ref[start : start + size, :] = (jnp.concatenate(parts, 0).T * factor).astype(jnp.bfloat16)
        at += size
    dki[...] = (aki[...] * factor).astype(jnp.bfloat16)
    dkt[...] = (akt[...] * factor).astype(jnp.bfloat16)
    dvi[...] = avi[...].astype(jnp.bfloat16)
    dvt[...] = avt[...].astype(jnp.bfloat16)


def kind_specs(rows, pairs, heads_first):
    return [pl.BlockSpec((rows, 2 * HEAD), partial(lambda k, p: (0, k * pairs + p), k)) for k in range(3)]


def attend(qkv_img, qkv_txt, block, valid):
    n_i, n_t = qkv_img.shape[0], qkv_txt.shape[0]
    inner = qkv_img.shape[1] // 3
    pairs = inner // (2 * HEAD)
    col = lambda rows: pl.BlockSpec((rows, 2 * HEAD), lambda p: (0, p))
    return pl.pallas_call(
        partial(attend_kernel, block, valid),
        grid=(pairs,),
        in_specs=kind_specs(n_i, pairs, 0) + kind_specs(n_t, pairs, 0),
        out_specs=[col(n_i), col(n_t), pl.BlockSpec((1, 2, n_i + n_t), lambda p: (p, 0, 0))],
        out_shape=[
            jax.ShapeDtypeStruct((n_i, inner), jnp.bfloat16),
            jax.ShapeDtypeStruct((n_t, inner), jnp.bfloat16),
            jax.ShapeDtypeStruct((pairs, 2, n_i + n_t), jnp.float32),
        ],
        compiler_params=pltpu.CompilerParams(vmem_limit_bytes=40 << 20),
        cost_estimate=pl.CostEstimate(flops=4 * (n_i + n_t) ** 2 * inner * 4, bytes_accessed=8 * (n_i + n_t) * inner, transcendentals=0),
    )(*([qkv_img] * 3 + [qkv_txt] * 3))


def attend_back(qkv_img, qkv_txt, g_img, g_txt, lse, block, valid):
    n_i, n_t = qkv_img.shape[0], qkv_txt.shape[0]
    inner = qkv_img.shape[1] // 3
    pairs = inner // (2 * HEAD)
    col = lambda rows: pl.BlockSpec((rows, 2 * HEAD), lambda p: (0, p))
    outs = [jax.ShapeDtypeStruct((n_i, inner), jnp.bfloat16)] * 3 + [jax.ShapeDtypeStruct((n_t, inner), jnp.bfloat16)] * 3
    res = pl.pallas_call(
        partial(back_kernel, block, valid),
        grid=(pairs,),
        in_specs=kind_specs(n_i, pairs, 0) + kind_specs(n_t, pairs, 0) + [col(n_i), col(n_t), pl.BlockSpec((1, 2, n_i + n_t), lambda p: (p, 0, 0))],
        out_specs=[col(n_i)] * 3 + [col(n_t)] * 3,
        out_shape=outs,
        scratch_shapes=[pltpu.VMEM((n, 2 * HEAD), jnp.float32) for n in (n_i, n_i, n_t, n_t)],
        compiler_params=pltpu.CompilerParams(vmem_limit_bytes=40 << 20),
        cost_estimate=pl.CostEstimate(flops=10 * (n_i + n_t) ** 2 * inner * 4, bytes_accessed=16 * (n_i + n_t) * inner, transcendentals=0),
    )(*([qkv_img] * 3 + [qkv_txt] * 3 + [g_img, g_txt, lse]))
    return res[:3], res[3:]


def tn(a, b):
    return lax.dot_general(a, b, (((0,), (0,)), ((), ())), preferred_element_type=jnp.float32)


def norm_forward(values):
    center = jnp.mean(values, -1, keepdims=True)
    spread = jnp.mean(jnp.square(values - center), -1, keepdims=True)
    rstd = lax.rsqrt(spread + norm_eps)
    return ((values - center) * rstd, rstd)


def norm_backward(grads, hats, rstd):
    first = jnp.mean(grads, -1, keepdims=True)
    second = jnp.mean(grads * hats, -1, keepdims=True)
    return rstd * (grads - first - hats * second)


class Group:
    def __init__(self, size):
        self.size = size
        self.evens = [2 * k for k in range(size // 2)]
        self.odds = [2 * k + 1 for k in range(size // 2)]
        self.order = self.evens + self.odds

    def send(self, value, flip):
        return lax.ppermute(value, "tensor", [(t, t ^ flip) for t in range(self.size)])

    def gather(self, own):
        evens = [own] + [self.send(own, flip) for flip in self.evens[1:]]
        return evens + [self.send(value, 1) for value in evens]


def on_device(
    n_dp,
    group,
    image,
    text,
    cond,
    teacher_image,
    teacher_text,
    grad_image,
    grad_text,
    live,
    w_mod,
    w_qkv,
    w_out,
    w_up,
    w_down,
):
    slots, width = cond.shape
    rows_i, rows_t = image.shape[1], text.shape[1]
    pad_t = -(-rows_t // 8) * 8
    size = group.size
    f_qkv, f_out, f_up, f_down = (
        lax.all_gather(w_qkv, "dp", axis=3, tiled=True),
        lax.all_gather(w_out, "dp", axis=2, tiled=True),
        lax.all_gather(w_up, "dp", axis=1, tiled=True),
        lax.all_gather(w_down, "dp", axis=1, tiled=True),
    )
    heads = f_qkv.shape[2]
    inner = heads * HEAD
    odd = heads % 2
    if odd:
        f_qkv = jnp.pad(f_qkv, ((0, 0), (0, 0), (0, 1), (0, 0), (0, 0)))
        f_out = jnp.pad(f_out, ((0, 0), (0, 1), (0, 0), (0, 0)))
    inner_p = inner + odd * HEAD
    f_qkv = f_qkv.reshape(2, 3 * inner_p, width)
    f_out = f_out.reshape(2, inner_p, width)
    here = lax.axis_index("dp")
    cond_f = cond.astype(jnp.float32)

    part = w_mod.shape[1]
    cond_all = lax.all_gather(cond, "dp", axis=0, tiled=True).astype(jnp.float32)
    act_all = jax.nn.silu(cond_all).astype(jnp.bfloat16)
    act_own = lax.dynamic_slice_in_dim(act_all, here * part, part, 1)
    mod_part = jnp.stack([nn(act_own, w_mod[s]) for s in range(2)], 1)
    mod_sum = lax.psum_scatter(mod_part, "dp", scatter_dimension=0, tiled=True)
    mod_full = lax.all_gather(mod_sum, "tensor", axis=2, tiled=True)
    mods = mod_full.reshape(slots, 2, 6, width)

    is_image = (lax.broadcasted_iota(jnp.int32, (rows_i + pad_t, 1), 0) < rows_i)
    is_real = (lax.broadcasted_iota(jnp.int32, (rows_i + pad_t, 1), 0) < rows_i + rows_t)

    def merged(img, txt, j):
        return jnp.concatenate([img[j], jnp.pad(txt[j], ((0, pad_t - rows_t), (0, 0)))], 0)

    def pick(j, span):
        return jnp.where(is_image, mods[j, 1, span][None], mods[j, 0, span][None])

    def token_sums(values):
        return jnp.stack([jnp.sum(values[rows_i:], 0), jnp.sum(values[:rows_i], 0)])

    def spread(blocks):
        return (
            jnp.concatenate([b[:rows_i] for b in blocks], 0),
            jnp.concatenate([b[rows_i:] for b in blocks], 0),
        )

    half_i, half_t = size // 2 * rows_i, size // 2 * pad_t

    def scatter(make_img, make_txt):
        top_i, top_t = slice(half_i, 2 * half_i), slice(half_t, 2 * half_t)
        sent_i = group.send(make_img(top_i).astype(jnp.bfloat16), 1)
        sent_t = group.send(make_txt(top_t).astype(jnp.bfloat16), 1)
        own_i = make_img(slice(0, half_i))
        own_t = make_txt(slice(0, half_t))
        blocks = []
        for k in range(size // 2):
            cut_i, cut_t = slice(k * rows_i, (k + 1) * rows_i), slice(k * pad_t, (k + 1) * pad_t)
            blocks.append(
                jnp.concatenate(
                    [
                        own_i[cut_i] + sent_i[cut_i].astype(jnp.float32),
                        own_t[cut_t] + sent_t[cut_t].astype(jnp.float32),
                    ],
                    0,
                )
            )
        total = blocks[0]
        for k in range(1, size // 2):
            total = total + group.send(blocks[k].astype(jnp.bfloat16), 2 * k).astype(jnp.float32)
        return total

    count = 3.0 * (n_dp // 2) * size * (rows_i + rows_t)

    slot = [dict() for j in range(slots)]
    for j in range(slots):
        v = slot[j]
        v["x"] = merged(image, text, j).astype(jnp.float32)
        v["hat1"], v["rstd1"] = norm_forward(v["x"])
        h1 = (v["hat1"] * (1.0 + pick(j, 1)) + pick(j, 0)).astype(jnp.bfloat16)
        v["h1_i"], v["h1_t"] = spread(group.gather(h1))
    for j in range(slots):
        v = slot[j]
        v["qkv_i"] = nt(v["h1_i"], f_qkv[1]).astype(jnp.bfloat16)
        v["qkv_t"] = nt(v["h1_t"], f_qkv[0]).astype(jnp.bfloat16)
        v["att_i"], v["att_t"], v["lse"] = attend(v["qkv_i"], v["qkv_t"], pad_t, rows_t)
        v["y"] = scatter(lambda r: nn(v["att_i"][r], f_out[1]), lambda r: nn(v["att_t"][r], f_out[0]))
        v["mid"] = v["x"] + pick(j, 2) * v["y"]
        v["hat2"], v["rstd2"] = norm_forward(v["mid"])
        h2 = (v["hat2"] * (1.0 + pick(j, 4)) + pick(j, 3)).astype(jnp.bfloat16)
        v["h2_i"], v["h2_t"] = spread(group.gather(h2))
    for j in range(slots):
        v = slot[j]
        v["pre_i"], v["pre_t"] = nn(v["h2_i"], f_up[1]), nn(v["h2_t"], f_up[0])
        v["hid_i"] = jax.nn.gelu(v["pre_i"], approximate=True).astype(jnp.bfloat16)
        v["hid_t"] = jax.nn.gelu(v["pre_t"], approximate=True).astype(jnp.bfloat16)
        v["m"] = scatter(lambda r: nt(v["hid_i"][r], f_down[1]), lambda r: nt(v["hid_t"][r], f_down[0]))
        out = v["mid"] + pick(j, 5) * v["m"]
        mask = jnp.where(is_real, live[j].astype(jnp.float32), 0.0)
        err = mask * (out - merged(teacher_image, teacher_text, j).astype(jnp.float32))
        v["loss"] = jnp.sum(err * err)
        v["cot"] = mask * merged(grad_image, grad_text, j).astype(jnp.float32) + 2.0 * err
        v["dgate2"] = token_sums(v["cot"] * v["m"])
        dm = (v["cot"] * pick(j, 5)).astype(jnp.bfloat16)
        v["dm_i"], v["dm_t"] = spread(group.gather(dm))
    loss = lax.psum(sum(v["loss"] for v in slot), ("dp", "tensor")) / (count * width)

    def reduced(make, axis, shape=None):
        g = jnp.stack([make("_t"), make("_i")]).astype(jnp.bfloat16)
        if shape is not None:
            g = g.reshape(shape)
        return lax.psum_scatter(g, "dp", scatter_dimension=axis, tiled=True).astype(jnp.float32)

    done_down = reduced(lambda e: sum(tn(v["dm" + e], v["hid" + e]) for v in slot), 1)
    for j in range(slots):
        v = slot[j]
        for s, e in enumerate(("_t", "_i")):
            dhid = nn(v["dm" + e], f_down[s])
            unused, pull = jax.vjp(partial(jax.nn.gelu, approximate=True), v["pre" + e])
            v["dpre" + e] = pull(dhid)[0].astype(jnp.bfloat16)
        v["dh2"] = scatter(lambda r: nt(v["dpre_i"][r], f_up[1]), lambda r: nt(v["dpre_t"][r], f_up[0]))
    done_up = reduced(lambda e: sum(tn(v["h2" + e], v["dpre" + e]) for v in slot), 1)
    for j in range(slots):
        v = slot[j]
        v["dshift2"] = token_sums(v["dh2"])
        v["dscale2"] = token_sums(v["dh2"] * v["hat2"])
        v["dmid"] = v["cot"] + norm_backward(v["dh2"] * (1.0 + pick(j, 4)), v["hat2"], v["rstd2"])
        v["dgate1"] = token_sums(v["dmid"] * v["y"])
        dy = (v["dmid"] * pick(j, 2)).astype(jnp.bfloat16)
        v["dy_i"], v["dy_t"] = spread(group.gather(dy))
    out_shape = (2, heads + odd, HEAD, width)
    done_out = reduced(lambda e: sum(tn(v["att" + e], v["dy" + e]) for v in slot), 2, out_shape)
    for j in range(slots):
        v = slot[j]
        g_i = nt(v["dy_i"], f_out[1]).astype(jnp.bfloat16)
        g_t = nt(v["dy_t"], f_out[0]).astype(jnp.bfloat16)
        back_i, back_t = attend_back(v["qkv_i"], v["qkv_t"], g_i, g_t, v["lse"], pad_t, rows_t)
        v["dqkv_i"], v["dqkv_t"] = jnp.concatenate(back_i, 1), jnp.concatenate(back_t, 1)
        v["dh1"] = scatter(lambda r: nn(v["dqkv_i"][r], f_qkv[1]), lambda r: nn(v["dqkv_t"][r], f_qkv[0]))
    qkv_shape = (2, 3, heads + odd, HEAD, width)
    done_qkv = reduced(lambda e: sum(tn(v["dqkv" + e], v["h1" + e]) for v in slot), 3, qkv_shape)
    grad_i, grad_t, terms = [], [], []
    for j in range(slots):
        v = slot[j]
        dshift1 = token_sums(v["dh1"])
        dscale1 = token_sums(v["dh1"] * v["hat1"])
        back = v["dmid"] + norm_backward(v["dh1"] * (1.0 + pick(j, 1)), v["hat1"], v["rstd1"])
        grad_i.append(back[:rows_i])
        grad_t.append(back[rows_i : rows_i + rows_t])
        terms.append(
            jnp.stack([dshift1, dscale1, v["dgate1"], v["dshift2"], v["dscale2"], v["dgate2"]], 1)
        )
    dmod = jnp.stack(terms).reshape(slots, 2, size, -1)
    dmod = lax.psum_scatter(dmod, "tensor", scatter_dimension=2, tiled=False).astype(jnp.bfloat16)
    dmod_all = lax.all_gather(dmod, "dp", axis=0, tiled=True)
    done_mod = jnp.stack([tn(act_own, dmod_all[:, s]) for s in range(2)])
    cond_part = nt(dmod_all[:, 0], w_mod[0]) + nt(dmod_all[:, 1], w_mod[1])
    cond_sum = lax.psum(cond_part, "tensor")
    cond_rows = lax.all_gather(cond_sum, "dp", axis=1, tiled=True)
    cond_total = lax.dynamic_slice_in_dim(cond_rows, here * slots, slots, 0)
    unused_value, silu_pull = jax.vjp(jax.nn.silu, cond_f)
    grad_cond = silu_pull(cond_total)[0]
    if odd:
        done_qkv, done_out = done_qkv[:, :, :heads], done_out[:, :heads]
    return (
        loss,
        done_mod,
        done_qkv,
        done_out,
        done_up,
        done_down,
        jnp.stack(grad_i),
        jnp.stack(grad_t),
        grad_cond,
    )


def solution(mesh):
    return jax.shard_map(
        partial(on_device, mesh.shape["dp"], Group(mesh.shape["tensor"])),
        mesh=mesh,
        in_specs=(
            P("dp", "tensor", None),
            P("dp", "tensor", None),
            P("dp", None),
            P("dp", "tensor", None),
            P("dp", "tensor", None),
            P("dp", "tensor", None),
            P("dp", "tensor", None),
            P("dp"),
            P(None, "dp", "tensor"),
            P(None, None, "tensor", "dp", None),
            P(None, "tensor", "dp", None),
            P(None, "dp", "tensor"),
            P(None, "dp", "tensor"),
        ),
        out_specs=(
            P(),
            P(None, "dp", "tensor"),
            P(None, None, "tensor", "dp", None),
            P(None, "tensor", "dp", None),
            P(None, "dp", "tensor"),
            P(None, "dp", "tensor"),
            P("dp", "tensor", None),
            P("dp", "tensor", None),
            P("dp", None),
        ),
        check_vma=False,
    )
```

time: 3360 us -> 1510 us (0.45)
  waiting for transfers between devices: 2450 us -> 722 us
  matrix products: 430 us -> 226 us
  Pallas kernels: 0 us -> 116 us
  local copies, waits for them, and re-layouts: 181 us -> 102 us
  blocking collectives: 131 us -> 197 us
  other arithmetic: 131 us -> 95.2 us
    reduce_scatter x9 -> x2, waiting for transfers between devices: 1630 us -> 193 us  [reduced(): lax.psum_scatter(g, 'dp', scatter_dimension=axis, tiled=True)]
    all_gather x5 -> x0, waiting for transfers between devices: 312 us -> none  [the longest x1 198 us: on_device(): lax.all_gather(w_mod, 'dp', axis=1, tiled=True)]
    ppermute x0 -> x48, waiting for transfers between devices: none -> 219 us  [send(): lax.ppermute(value, 'tensor', [(t, t ^ flip) for t in range(self.size)])]
    dot_general x114 -> x70, matrix products: 430 us -> 226 us  [the longest x26 95.6 us: nn(): return jnp.dot(a, b, preferred_element_type=jnp.float32)]
    all_gather x1, waiting for transfers between devices: 134 us -> 0.01 us  [on_device(): lax.all_gather(w_up, 'dp', axis=1, tiled=True)]
    pallas_call x0 -> x4, Pallas kernels: none -> 116 us  [the longest x2 62.4 us: attend_back(): pl.pallas_call(partial(back_kernel, block, valid), grid=(pairs,), in_spec...]
    all_gather x6 -> x4, blocking collectives: 56.6 us -> 101 us  [the longest x1 32.7 us: on_device(): lax.all_gather(cond, 'dp', axis=0, tiled=True).astype(jnp.float32)]
    while x27 -> x0, local copies, waits for them, and re-layouts: 43 us -> none
  transfers between devices with their start and end apart: 24 -> 57, of which waited for: 22 -> 22; matrix products, arithmetic and copies ran while one was open for 10% -> 24% of each run, Pallas kernels for 0% -> 4%
where the time goes in v1:
time: 1510 us
  waiting for transfers between devices  722 us (48%)
  matrix products  226 us (15%)
  blocking collectives  197 us (13%)
  Pallas kernels  116 us (8%)
  local copies, waits for them, and re-layouts  102 us (7%)
  other arithmetic  95.2 us (6%)
  starting transfers between devices  25 us (2%)
  between operations  23.8 us (2%)
    ppermute x48, waiting for transfers between devices, send(): lax.ppermute(value, 'tensor', [(t, t ^ flip) for t in range(self.size)])  219 us
    reduce_scatter x2, waiting for transfers between devices, reduced(): lax.psum_scatter(g, 'dp', scatter_dimension=axis, tiled=True)  193 us
    all_gather x1, waiting for transfers between devices, on_device(): lax.all_gather(w_down, 'dp', axis=1, tiled=True)  116 us
    all_gather x1, waiting for transfers between devices, on_device(): lax.all_gather(w_qkv, 'dp', axis=3, tiled=True)  107 us
    dot_general x26, matrix products, nn(): return jnp.dot(a, b, preferred_element_type=jnp.float32)  95.6 us
    dot_general x26, matrix products, nt(): lax.dot_general(a, b, (((1,), (1,)), ((), ())), preferred_element_type=jn...  76.8 us
    psum x1, blocking collectives, on_device(): lax.psum(sum((v['loss'] for v in slot)), ('dp', 'tensor')) / (count * width)  72 us
    unnamed x12, waiting for transfers between devices  67.8 us
  transfers between devices with their start and end apart: 57, of which 22 were waited for; matrix products, arithmetic and copies ran while one was open for 24% of the time, Pallas kernels for 4%

profile of v1, /device:TPU:0, one launch (start us, length us, event | category | flops | bytes accessed | tf_op | source)
XLA Modules:
  0.0 1506.7 jit_solution(14691674189554413518)
XLA Ops:
  7.2 32.7 %all-gather.1 = bf16[8,2,1536]{2,1,0:T(2,128)(2,1)S(1)} all-gather(bf16[1,2,1536]{2,1,0:T(2,128)(2,1)} %bitcast.253), channel_id=1, replica_groups=mesh['dp'=8,'tensor'=4] {'dp'}, dimensions={0}, use_global_device_ids=true | all-gather | bytes 55296 | tf_op jit(solution)/shard_map/all_gather | solution.py:229
  50.3 65.3 %all-reduce.11.cloned.1.call-done = f32[16,2,2304]{2,0,1:T(8,128)} async-done(((f32[16,2,2304]{2,0,1:T(8,128)}), f32[16,2,2304]{2,0,1:T(8,128)}) %all-reduce.11.cloned.1.call-update) | async-done | bytes 294928
  125.3 20.9 %collective-permute-done.12 = bf16[296,1536]{1,0:T(8,128)(2,1)S(1)} collective-permute-done((bf16[296,1536]{1,0:T(8,128)(2,1)S(1)}, bf16[296,1536]{1,0:T(8,128)(2,1)S(1)}, u32[]{:S(2)}, u32[]{:S(2)}) %collective-permute-start.12) | collective-permute-done | bytes 909344 | tf_op jit(solution)/shard_map/ppermute | solution.py:182
  149.6 19.5 %all-gather.10.cloned.1.call-done = bf16[2,6,64,1536]{3,2,1,0:T(8,128)(2,1)} async-done(((bf16[2,6,8,1536]{3,2,1,0:T(8,128)(2,1)}), bf16[2,6,64,1536]{3,2,1,0:T(8,128)(2,1)}) %all-gather.10.cloned.1.call-update) | async-done | bytes 2359312 | tf_op jit(solution)/shard_map/all_gather | solution.py:212
  172.3 106.6 %all-gather.8.cloned.1.call-done = bf16[2,3,6,64,1536]{4,3,2,1,0:T(8,128)(2,1)} async-done(((bf16[2,3,6,8,1536]{4,3,2,1,0:T(8,128)(2,1)}), bf16[2,3,6,64,1536]{4,3,2,1,0:T(8,128)(2,1)}) %all-gather.8.cloned.1.call-update) | async-done | bytes 7077904 | tf_op jit(solution)/shard_map/all_gather | solution.py:211
  292.9 26.5 %shard_map.197 = (bf16[1024,384]{1,0:T(8,128)(2,1)S(1)}, bf16[160,384]{1,0:T(8,128)(2,1)S(1)}, f32[3,2,1184]{2,1,0:T(2,128)S(1)}) custom-call(bf16[1024,1152]{1,0:T(8,128)(2,1)S(1)} %convolution_convert_fusion.qi.ki.vi, bf16[1024,1152]{1,0:T(8,128)(2,1)S(1)} %convolution_convert_fusion.qi.ki.vi, bf16[1024,1152]{1,0:T(8,128)(2,1)S(1)} %convolution_convert_fusion.qi.ki.vi, ...), custom_call_target="tpu_custom_call" | custom-call | flops 8613003264 | bytes 3637248 | tf_op jit(solution)/shard_map/pallas_call | solution.py:123
  327.8 19.4 %collective-permute-done.17 = bf16[296,1536]{1,0:T(8,128)(2,1)S(1)} collective-permute-done((bf16[296,1536]{1,0:T(8,128)(2,1)S(1)}, bf16[296,1536]{1,0:T(8,128)(2,1)S(1)}, u32[]{:S(2)}, u32[]{:S(2)}) %collective-permute-start.17) | collective-permute-done | bytes 909344 | tf_op jit(solution)/shard_map/ppermute | solution.py:182
  358.0 15.6 %collective-permute-done = bf16[296,1536]{1,0:T(8,128)(2,1)S(1)} collective-permute-done((bf16[296,1536]{1,0:T(8,128)(2,1)S(1)}, bf16[296,1536]{1,0:T(8,128)(2,1)S(1)}, u32[]{:S(2)}, u32[]{:S(2)}) %collective-permute-start) | collective-permute-done | bytes 909344 | tf_op jit(solution)/shard_map/ppermute | solution.py:182
  402.7 26.9 %shard_map.196 = (bf16[1024,384]{1,0:T(8,128)(2,1)S(1)}, bf16[160,384]{1,0:T(8,128)(2,1)S(1)}, f32[3,2,1184]{2,1,0:T(2,128)S(1)}) custom-call(bf16[1024,1152]{1,0:T(8,128)(2,1)S(1)} %convolution_convert_fusion.1.qi.ki.vi, bf16[1024,1152]{1,0:T(8,128)(2,1)S(1)} %convolution_convert_fusion.1.qi.ki.vi, ...), custom_call_target="tpu_custom_call" | custom-call | flops 8613003264 | bytes 3637248 | tf_op jit(solution)/shard_map/pallas_call | solution.py:123
  439.6 116.5 %all-gather.14.cloned.1.call-done = bf16[2,1536,1536]{2,1,0:T(8,128)(2,1)} async-done(((bf16[2,192,1536]{2,1,0:T(8,128)(2,1)}), bf16[2,1536,1536]{2,1,0:T(8,128)(2,1)}) %all-gather.14.cloned.1.call-update) | async-done | bytes 9437200 | tf_op jit(solution)/shard_map/all_gather | solution.py:214
  586.4 20.1 %collective-permute-done.5 = bf16[296,1536]{1,0:T(8,128)(2,1)S(1)} collective-permute-done((bf16[296,1536]{1,0:T(8,128)(2,1)S(1)}, bf16[296,1536]{1,0:T(8,128)(2,1)S(1)}, u32[]{:S(2)}, u32[]{:S(2)}) %collective-permute-start.5) | collective-permute-done | bytes 909344 | tf_op jit(solution)/shard_map/ppermute | solution.py:182
  607.6 17.5 %collective-permute-done.23 = bf16[296,1536]{1,0:T(8,128)(2,1)S(1)} collective-permute-done((bf16[296,1536]{1,0:T(8,128)(2,1)S(1)}, bf16[296,1536]{1,0:T(8,128)(2,1)S(1)}, u32[]{:S(2)}, u32[]{:S(2)}) %collective-permute-start.23) | collective-permute-done | bytes 909344 | tf_op jit(solution)/shard_map/ppermute | solution.py:182
  631.9 20.9 %collective-permute-done.6 = bf16[296,1536]{1,0:T(8,128)(2,1)S(1)} collective-permute-done((bf16[296,1536]{1,0:T(8,128)(2,1)S(1)}, bf16[296,1536]{1,0:T(8,128)(2,1)S(1)}, u32[]{:S(2)}, u32[]{:S(2)}) %collective-permute-start.6) | collective-permute-done | bytes 909344 | tf_op jit(solution)/shard_map/ppermute | solution.py:182
  653.9 16.5 %collective-permute-done.36 = bf16[296,1536]{1,0:T(8,128)(2,1)S(1)} collective-permute-done((bf16[296,1536]{1,0:T(8,128)(2,1)S(1)}, bf16[296,1536]{1,0:T(8,128)(2,1)S(1)}, u32[]{:S(2)}, u32[]{:S(2)}) %collective-permute-start.36) | collective-permute-done | bytes 909344 | tf_op jit(solution)/shard_map/ppermute | solution.py:182
  797.6 19.4 %collective-permute-done.29 = bf16[296,1536]{1,0:T(8,128)(2,1)S(1)} collective-permute-done((bf16[296,1536]{1,0:T(8,128)(2,1)S(1)}, bf16[296,1536]{1,0:T(8,128)(2,1)S(1)}, u32[]{:S(2)}, u32[]{:S(2)}) %collective-permute-start.29) | collective-permute-done | bytes 909344 | tf_op jit(solution)/shard_map/ppermute | solution.py:182
  831.6 20.6 %collective-permute-done.42 = bf16[296,1536]{1,0:T(8,128)(2,1)S(1)} collective-permute-done((bf16[296,1536]{1,0:T(8,128)(2,1)S(1)}, bf16[296,1536]{1,0:T(8,128)(2,1)S(1)}, u32[]{:S(2)}, u32[]{:S(2)}) %collective-permute-start.42) | collective-permute-done | bytes 909344 | tf_op jit(solution)/shard_map/ppermute | solution.py:182
  852.3 17.6 %collective-permute-done.30 = bf16[296,1536]{1,0:T(8,128)(2,1)S(1)} collective-permute-done((bf16[296,1536]{1,0:T(8,128)(2,1)S(1)}, bf16[296,1536]{1,0:T(8,128)(2,1)S(1)}, u32[]{:S(2)}, u32[]{:S(2)}) %collective-permute-start.30) | collective-permute-done | bytes 909344 | tf_op jit(solution)/shard_map/ppermute | solution.py:182
  884.6 31.2 %shard_map.198 = (bf16[1024,384]{1,0:T(8,128)(2,1)S(1)}, bf16[1024,384]{1,0:T(8,128)(2,1)S(1)}, bf16[1024,384]{1,0:T(8,128)(2,1)S(1)}, bf16[160,384]{1,0:T(8,128...) custom-call(bf16[1024,1152]{1,0:T(8,128)(2,1)S(1)} %copy-done.20, ...), custom_call_target="tpu_custom_call" | custom-call | flops 21532508160 | bytes 7274496 | tf_op jit(solution)/shard_map/pallas_call | solution.py:144
  916.4 31.2 %shard_map.199 = (bf16[1024,384]{1,0:T(8,128)(2,1)S(1)}, bf16[1024,384]{1,0:T(8,128)(2,1)S(1)}, bf16[1024,384]{1,0:T(8,128)(2,1)S(1)}, bf16[160,384]{1,0:T(8,128...) custom-call(bf16[1024,1152]{1,0:T(8,128)(2,1)S(1)} %copy-done.18, ...), custom_call_target="tpu_custom_call" | custom-call | flops 21532508160 | bytes 7274496 | tf_op jit(solution)/shard_map/pallas_call | solution.py:144
  1102.2 72.0 %psum.14 = f32[]{:T(128)} all-reduce(f32[]{:T(128)S(6)} %add.364), channel_id=1, replica_groups=mesh['dp'=8,'tensor'=4] {'dp','tensor'}, use_global_device_ids=true, to_apply=%region_11.12 | all-reduce | flops 1 | bytes 8 | tf_op jit(solution)/shard_map/psum | solution.py:313
  1207.3 32.0 %all-gather = bf16[16,2,1,2304]{3,1,2,0:T(2,128)(2,1)S(1)} all-gather(bf16[2,2,1,2304]{3,1,2,0:T(2,128)(2,1)S(1)} %fusion.189), channel_id=2, replica_groups=mesh['dp'=8,'tensor'=4] {'dp'}, dimensions={0}, use_global_device_ids=true | all-gather | bytes 165888 | tf_op jit(solution)/shard_map/all_gather | solution.py:362
  1253.2 30.8 %all-gather.2 = f32[8,192,16]{1,2,0:T(8,128)S(1)} all-gather(f32[1,192,16]{1,2,0:T(8,128)S(1)} %bitcast.252), channel_id=1, replica_groups=mesh['dp'=8,'tensor'=4] {'dp'}, dimensions={0}, use_global_device_ids=true | all-gather | bytes 110592 | tf_op jit(solution)/shard_map/all_gather | solution.py:366
  1299.9 29.8 %reduce-scatter.10.cloned.1.call-done = bf16[2,192,1536]{2,1,0:T(8,128)(2,1)} async-done(((bf16[2,1536,1536]{2,1,0:T(8,128)(2,1)}), bf16[2,192,1536]{2,1,0:T(8,128)(2,1)}) %reduce-scatter.10.cloned.1.call-update) | async-done | bytes 1179664 | tf_op jit(solution)/shard_map/reduce_scatter | solution.py:319
  1332.6 163.2 %reduce-scatter.12.cloned.1.call-done = bf16[2,192,1536]{2,1,0:T(8,128)(2,1)} async-done(((bf16[2,1536,1536]{2,1,0:T(8,128)(2,1)}), bf16[2,192,1536]{2,1,0:T(8,128)(2,1)}) %reduce-scatter.12.cloned.1.call-update) | async-done | bytes 1179664 | tf_op jit(solution)/shard_map/reduce_scatter | solution.py:319
  (979 shorter events, 510.4 us)
Async XLA Ops:
  7.2 108.4 %all-reduce.11.cloned.1.call-start = ((), (), s32[]{:S(2)}) async-start(), calls=%async_computation.12 | async-start | bytes 589824
  43.7 125.5 %all-gather.10.cloned.1.call-start = ((), (), s32[]{:S(2)}) async-start(), calls=%async_computation.5 | async-start | bytes 2654208 | tf_op jit(solution)/shard_map/all_gather | solution.py:212
  44.4 234.5 %all-gather.8.cloned.1.call-start = ((), (), s32[]{:S(2)}) async-start(), calls=%async_computation.4 | async-start | bytes 7962624 | tf_op jit(solution)/shard_map/all_gather | solution.py:211
  45.2 389.7 %all-gather.12.cloned.1.call-start = ((), (), s32[]{:S(2)}) async-start(), calls=%async_computation.6 | async-start | bytes 10616832 | tf_op jit(solution)/shard_map/all_gather | solution.py:213
  45.8 510.3 %all-gather.14.cloned.1.call-start = ((), (), s32[]{:S(2)}) async-start(), calls=%async_computation.7 | async-start | bytes 10616832 | tf_op jit(solution)/shard_map/all_gather | solution.py:214
  46.3 1246.9 %reduce-scatter.16.cloned.1.call-start = ((), (), s32[]{:S(2)}) async-start(), calls=%async_computation.11 | async-start | bytes 2654208
  357.2 34.3 %collective-permute-start.18 = (bf16[296,1536]{1,0:T(8,128)(2,1)S(1)}, bf16[296,1536]{1,0:T(8,128)(2,1)S(1)}, u32[]{:S(2)}, u32[]{:S(2)}) collective-permute-start(bf16[296,1536]{1,0:T(8,128)(2,1)S(1)} %get-tuple-element.186), channel_id=1, source_target_pairs={{0,2},{1,3},{2,0},{3,1},{4,6},{5,7},{6,4},{7,5},{8,10},{9,11},{10,... | collective-permute-start | bytes 2727944 | tf_op jit(solution)/shard_map/ppermute | solution.py:182
  357.8 34.4 %collective-permute-start.19 = (bf16[296,1536]{1,0:T(8,128)(2,1)S(1)}, bf16[296,1536]{1,0:T(8,128)(2,1)S(1)}, u32[]{:S(2)}, u32[]{:S(2)}) collective-permute-start(bf16[296,1536]{1,0:T(8,128)(2,1)S(1)} %get-tuple-element.186), channel_id=1, source_target_pairs={{0,1},{1,0},{2,3},{3,2},{4,5},{5,4},{6,7},{7,6},{8,9},{9,8},{10,11... | collective-permute-start | bytes 2727944 | tf_op jit(solution)/shard_map/ppermute | solution.py:182
  391.5 41.8 %collective-permute-start.20 = (bf16[296,1536]{1,0:T(8,128)(2,1)S(1)}, bf16[296,1536]{1,0:T(8,128)(2,1)S(1)}, u32[]{:S(2)}, u32[]{:S(2)}) collective-permute-start(bf16[296,1536]{1,0:T(8,128)(2,1)S(1)} %collective-permute-done.18), channel_id=1, source_target_pairs={{0,1},{1,0},{2,3},{3,2},{4,5},{5,4},{6,7},{7,6},{8,9},{9,8},{10,11... | collective-permute-start | bytes 2727944 | tf_op jit(solution)/shard_map/ppermute | solution.py:182
  430.7 149.7 %collective-permute-start.4 = (bf16[80,1536]{1,0:T(8,128)(2,1)}, bf16[80,1536]{1,0:T(8,128)(2,1)}, u32[]{:S(2)}, u32[]{:S(2)}) collective-permute-start(bf16[80,1536]{1,0:T(8,128)(2,1)} %convolution_convert_fusion.19), channel_id=1, source_target_pairs={{0,1},{1,0},{2,3},{3,2},{4,5},{5,4},{6,7},{7,6},{8,9},{9,8},{10,11... | collective-permute-start | bytes 737288 | tf_op jit(solution)/shard_map/ppermute | solution.py:182
  433.3 148.1 %collective-permute-start.3 = (bf16[512,1536]{1,0:T(8,128)(2,1)}, bf16[512,1536]{1,0:T(8,128)(2,1)}, u32[]{:S(2)}, u32[]{:S(2)}) collective-permute-start(bf16[512,1536]{1,0:T(8,128)(2,1)} %convolution_convert_fusion.9), channel_id=1, source_target_pairs={{0,1},{1,0},{2,3},{3,2},{4,5},{5,4},{6,7},{7,6},{8,9},{9,8},{10,11... | collective-permute-start | bytes 4718600 | tf_op jit(solution)/shard_map/ppermute | solution.py:182
  585.8 39.3 %collective-permute-start.23 = (bf16[296,1536]{1,0:T(8,128)(2,1)S(1)}, bf16[296,1536]{1,0:T(8,128)(2,1)S(1)}, u32[]{:S(2)}, u32[]{:S(2)}) collective-permute-start(bf16[296,1536]{1,0:T(8,128)(2,1)S(1)} %pad_maximum_fusion.17), channel_id=1, source_target_pairs={{0,2},{1,3},{2,0},{3,1},{4,6},{5,7},{6,4},{7,5},{8,10},{9,11},{10,... | collective-permute-start | bytes 2727944 | tf_op jit(solution)/shard_map/ppermute | solution.py:182
  631.1 39.3 %collective-permute-start.36 = (bf16[296,1536]{1,0:T(8,128)(2,1)S(1)}, bf16[296,1536]{1,0:T(8,128)(2,1)S(1)}, u32[]{:S(2)}, u32[]{:S(2)}) collective-permute-start(bf16[296,1536]{1,0:T(8,128)(2,1)S(1)} %get-tuple-element.182), channel_id=1, source_target_pairs={{0,2},{1,3},{2,0},{3,1},{4,6},{5,7},{6,4},{7,5},{8,10},{9,11},{10,... | collective-permute-start | bytes 2727944 | tf_op jit(solution)/shard_map/ppermute | solution.py:182
  631.7 38.8 %collective-permute-start.37 = (bf16[296,1536]{1,0:T(8,128)(2,1)S(1)}, bf16[296,1536]{1,0:T(8,128)(2,1)S(1)}, u32[]{:S(2)}, u32[]{:S(2)}) collective-permute-start(bf16[296,1536]{1,0:T(8,128)(2,1)S(1)} %get-tuple-element.182), channel_id=1, source_target_pairs={{0,1},{1,0},{2,3},{3,2},{4,5},{5,4},{6,7},{7,6},{8,9},{9,8},{10,11... | collective-permute-start | bytes 2727944 | tf_op jit(solution)/shard_map/ppermute | solution.py:182
  702.2 56.8 %collective-permute-start.40 = (bf16[80,1536]{1,0:T(8,128)(2,1)S(1)}, bf16[80,1536]{1,0:T(8,128)(2,1)S(1)}, u32[]{:S(2)}, u32[]{:S(2)}) collective-permute-start(bf16[80,1536]{1,0:T(8,128)(2,1)S(1)} %convolution_convert_fusion.13), channel_id=1, source_target_pairs={{0,1},{1,0},{2,3},{3,2},{4,5},{5,4},{6,7},{7,6},{8,9},{9,8},{10,11... | collective-permute-start | bytes 737288 | tf_op jit(solution)/shard_map/ppermute | solution.py:182
  759.6 36.3 %collective-permute-start.41 = (bf16[296,1536]{1,0:T(8,128)(2,1)S(1)}, bf16[296,1536]{1,0:T(8,128)(2,1)S(1)}, u32[]{:S(2)}, u32[]{:S(2)}) collective-permute-start(bf16[296,1536]{1,0:T(8,128)(2,1)S(1)} %pad_maximum_fusion.20), channel_id=1, source_target_pairs={{0,2},{1,3},{2,0},{3,1},{4,6},{5,7},{6,4},{7,5},{8,10},{9,11},{10,... | collective-permute-start | bytes 2727944 | tf_op jit(solution)/shard_map/ppermute | solution.py:182
  830.2 39.7 %collective-permute-start.30 = (bf16[296,1536]{1,0:T(8,128)(2,1)S(1)}, bf16[296,1536]{1,0:T(8,128)(2,1)S(1)}, u32[]{:S(2)}, u32[]{:S(2)}) collective-permute-start(bf16[296,1536]{1,0:T(8,128)(2,1)S(1)} %get-tuple-element.181), channel_id=1, source_target_pairs={{0,2},{1,3},{2,0},{3,1},{4,6},{5,7},{6,4},{7,5},{8,10},{9,11},{10,... | collective-permute-start | bytes 2727944 | tf_op jit(solution)/shard_map/ppermute | solution.py:182
  831.1 38.9 %collective-permute-start.31 = (bf16[296,1536]{1,0:T(8,128)(2,1)S(1)}, bf16[296,1536]{1,0:T(8,128)(2,1)S(1)}, u32[]{:S(2)}, u32[]{:S(2)}) collective-permute-start(bf16[296,1536]{1,0:T(8,128)(2,1)S(1)} %get-tuple-element.181), channel_id=1, source_target_pairs={{0,1},{1,0},{2,3},{3,2},{4,5},{5,4},{6,7},{7,6},{8,9},{9,8},{10,11... | collective-permute-start | bytes 2727944 | tf_op jit(solution)/shard_map/ppermute | solution.py:182
  831.1 39.1 %collective-permute-start.43 = (bf16[296,1536]{1,0:T(8,128)(2,1)S(1)}, bf16[296,1536]{1,0:T(8,128)(2,1)S(1)}, u32[]{:S(2)}, u32[]{:S(2)}) collective-permute-start(bf16[296,1536]{1,0:T(8,128)(2,1)S(1)} %get-tuple-element.180), channel_id=1, source_target_pairs={{0,1},{1,0},{2,3},{3,2},{4,5},{5,4},{6,7},{7,6},{8,9},{9,8},{10,11... | collective-permute-start | bytes 2727944 | tf_op jit(solution)/shard_map/ppermute | solution.py:182
  960.5 335.2 %reduce-scatter.14.cloned.1.call-start = ((), (), s32[]{:S(2)}) async-start(), calls=%async_computation.10 | async-start | bytes 7962624
  1007.1 322.5 %reduce-scatter.10.cloned.1.call-start = ((), (), s32[]{:S(2)}) async-start(), calls=%async_computation.8 | async-start | bytes 10616832 | tf_op jit(solution)/shard_map/reduce_scatter | solution.py:319
  1035.4 460.5 %reduce-scatter.12.cloned.1.call-start = ((), (), s32[]{:S(2)}) async-start(), calls=%async_computation.9 | async-start | bytes 10616832 | tf_op jit(solution)/shard_map/reduce_scatter | solution.py:319
  1097.6 81.3 %collective-permute-start.35 = (bf16[296,1536]{1,0:T(8,128)(2,1)}, bf16[296,1536]{1,0:T(8,128)(2,1)}, u32[]{:S(2)}, u32[]{:S(2)}) collective-permute-start(bf16[296,1536]{1,0:T(8,128)(2,1)} %pad_maximum_fusion.19), channel_id=1, source_target_pairs={{0,2},{1,3},{2,0},{3,1},{4,6},{5,7},{6,4},{7,5},{8,10},{9,11},{10,... | collective-permute-start | bytes 2727944 | tf_op jit(solution)/shard_map/ppermute | solution.py:182
  1101.7 77.2 %collective-permute-start.47 = (bf16[296,1536]{1,0:T(8,128)(2,1)}, bf16[296,1536]{1,0:T(8,128)(2,1)}, u32[]{:S(2)}, u32[]{:S(2)}) collective-permute-start(bf16[296,1536]{1,0:T(8,128)(2,1)} %pad_maximum_fusion.21), channel_id=1, source_target_pairs={{0,2},{1,3},{2,0},{3,1},{4,6},{5,7},{6,4},{7,5},{8,10},{9,11},{10,... | collective-permute-start | bytes 2727944 | tf_op jit(solution)/shard_map/ppermute | solution.py:182
  (297 other events, 6078.4 us)
Sparse Core Ops, SparseCore 0:
  43.8 71.6 all-reduce.10
  118.0 51.1 all-gather.9
  171.6 107.3 all-gather.7
  281.2 136.2 all-gather.11
  419.8 136.2 all-gather.13
  960.6 67.2 reduce-scatter.15
  1032.0 128.9 reduce-scatter.13
  1164.6 165.0 reduce-scatter.9
  1333.3 162.5 reduce-scatter.11

commit v2 on v1

--- a/solution.py
+++ b/solution.py
@@ -186,8 +186,249 @@
         return evens + [self.send(value, 1) for value in evens]
 
 
+MESH = pl.DeviceIdType.MESH
+
+
+def flip_bits(index, flip, size):
+    total, bit = 0, 1
+    while bit < size:
+        digit = lax.rem(lax.div(index, bit), 2)
+        total = total + bit * ((1 - digit) if flip & bit else digit)
+        bit *= 2
+    return total
+
+
+class Data:
+    def __init__(self, size):
+        self.size = size
+        self.nx = math.isqrt(size // 2)
+        self.nz = size // self.nx
+
+    def send(self, value, flip):
+        return lax.ppermute(value, "dp", [(p, p ^ flip) for p in range(self.size)])
+
+    def gather(self, own):
+        blocks = {}
+        for zk in range(self.nz):
+            blocks[zk * self.nx] = self.send(own, zk * self.nx) if zk else own
+        for zk in range(self.nz):
+            for xk in range(1, self.nx):
+                blocks[zk * self.nx + xk] = self.send(blocks[zk * self.nx], xk)
+        return [blocks[k] for k in range(self.size)]
+
+
+def place_kernel(size, *refs):
+    blocks, out, sems = refs[:size], refs[size], refs[size + 1]
+    here = lax.axis_index("dp")
+    part = blocks[0].shape[1]
+    copies = []
+    for k in range(size):
+        start = pl.multiple_of(flip_bits(here, k, size) * part, 16)
+        copies.append(
+            pltpu.make_async_copy(blocks[k], out.at[:, pl.ds(start, part), :], sems.at[k])
+        )
+        copies[-1].start()
+    for copy in copies:
+        copy.wait()
+
+
+def place(blocks):
+    size = len(blocks)
+    two, part, columns = blocks[0].shape
+    return pl.pallas_call(
+        partial(place_kernel, size),
+        in_specs=[pl.BlockSpec(memory_space=pl.ANY)] * size,
+        out_specs=pl.BlockSpec(memory_space=pl.ANY),
+        out_shape=jax.ShapeDtypeStruct((two, size * part, columns), blocks[0].dtype),
+        scratch_shapes=[pltpu.SemaphoreType.DMA((size,))],
+        cost_estimate=pl.CostEstimate(flops=0, bytes_accessed=4 * two * size * part * columns, transcendentals=0),
+    )(*blocks)
+
+
+def greet(n_dp, size):
+    me_d, me_t = lax.axis_index("dp"), lax.axis_index("tensor")
+    barrier = pltpu.get_barrier_semaphore()
+    for k in range(1, n_dp):
+        pl.semaphore_signal(barrier, inc=1, device_id=(flip_bits(me_d, k, n_dp), me_t), device_id_type=MESH)
+    for k in range(1, size):
+        pl.semaphore_signal(barrier, inc=1, device_id=(me_d, flip_bits(me_t, k, size)), device_id_type=MESH)
+    pl.semaphore_wait(barrier, n_dp + size - 2)
+
+
+def to_data(n_dp, source, target, send, recv):
+    me_d, me_t = lax.axis_index("dp"), lax.axis_index("tensor")
+    copies = []
+    for k in range(1, n_dp):
+        peer = flip_bits(me_d, k, n_dp)
+        copy = pltpu.make_async_remote_copy(
+            src_ref=source(peer),
+            dst_ref=target.at[me_d],
+            send_sem=send.at[k - 1],
+            recv_sem=recv.at[k - 1],
+            device_id=(peer, me_t),
+            device_id_type=MESH,
+        )
+        copy.start()
+        copies.append(copy)
+    return copies
+
+
+def to_tensor(size, source, target, send, recv):
+    me_d, me_t = lax.axis_index("dp"), lax.axis_index("tensor")
+    copies = []
+    for k in range(1, size):
+        peer = flip_bits(me_t, k, size)
+        copy = pltpu.make_async_remote_copy(
+            src_ref=source(peer),
+            dst_ref=target.at[me_t],
+            send_sem=send.at[k - 1],
+            recv_sem=recv.at[k - 1],
+            device_id=(me_d, peer),
+            device_id_type=MESH,
+        )
+        copy.start()
+        copies.append(copy)
+    return copies
+
+
+def finish(copies):
+    for copy in copies:
+        copy.wait()
+
+
+def mod_kernel(n_dp, size, cond, w, mod_out, act_out, conds, parts, got, own, sd1, rd1, sd2, rd2, st, rt):
+    me_d, me_t = lax.axis_index("dp"), lax.axis_index("tensor")
+    rows, part, columns = conds.shape[1], w.shape[1], w.shape[2]
+    greet(n_dp, size)
+    copies = to_data(n_dp, lambda peer: cond.at[peer], conds, sd1, rd1)
+    conds[me_d] = cond[me_d]
+    finish(copies)
+    value = conds[...].reshape(n_dp * rows, conds.shape[2])[:, :part]
+    act = (value * jax.nn.sigmoid(value)).astype(jnp.bfloat16)
+    act_out[...] = act
+    place = lax.rem(lax.broadcasted_iota(jnp.int32, (n_dp * rows, 1), 0), rows)
+    mixed = jnp.where(place < rows // 4, nn(act, w[0]), nn(act, w[1]))
+    parts[...] = mixed.reshape(n_dp, rows, columns)
+    copies = to_data(n_dp, lambda peer: parts.at[peer], got, sd2, rd2)
+    got[me_d] = parts[me_d]
+    finish(copies)
+    total = got[0]
+    for p in range(1, n_dp):
+        total = total + got[p]
+    own[...] = total
+    copies = to_tensor(size, lambda peer: own, mod_out, st, rt)
+    mod_out[me_t] = total
+    finish(copies)
+
+
+def mod_forward(n_dp, size, cond, w_mod):
+    slots, width = cond.shape
+    part, columns = w_mod.shape[1:]
+    rows, lanes = 4 * slots, -(-part // 128) * 128
+    laid = cond.astype(jnp.float32).reshape(slots, n_dp, part).transpose(1, 0, 2)
+    laid = jnp.concatenate([laid, laid, jnp.zeros_like(laid), jnp.zeros_like(laid)], 1)
+    laid = jnp.pad(laid, ((0, 0), (0, 0), (0, lanes - part)))
+    dma = pltpu.SemaphoreType.DMA
+    return pl.pallas_call(
+        partial(mod_kernel, n_dp, size),
+        in_specs=[pl.BlockSpec(memory_space=pltpu.VMEM)] * 2,
+        out_specs=[pl.BlockSpec(memory_space=pltpu.VMEM)] * 2,
+        out_shape=[
+            jax.ShapeDtypeStruct((size, rows, columns), jnp.float32),
+            jax.ShapeDtypeStruct((n_dp * rows, part), jnp.bfloat16),
+        ],
+        scratch_shapes=[
+            pltpu.VMEM((n_dp, rows, lanes), jnp.float32),
+            pltpu.VMEM((n_dp, rows, columns), jnp.float32),
+            pltpu.VMEM((n_dp, rows, columns), jnp.float32),
+            pltpu.VMEM((rows, columns), jnp.float32),
+            dma((n_dp - 1,)), dma((n_dp - 1,)), dma((n_dp - 1,)), dma((n_dp - 1,)),
+            dma((size - 1,)), dma((size - 1,)),
+        ],
+        compiler_params=pltpu.CompilerParams(
+            collective_id=0, has_side_effects=True, vmem_limit_bytes=40 << 20
+        ),
+        cost_estimate=pl.CostEstimate(flops=1 << 33, bytes_accessed=1 << 21, transcendentals=0),
+    )(laid, w_mod)
+
+
+def mod_back_kernel(n_dp, size, terms, act, w, grad, cond_out, loss_out, halves, sums, every, cparts, cgot, cfull,
+                    st1, rt1, sd1, rd1, sd2, rd2, st2, rt2):
+    me_d, me_t = lax.axis_index("dp"), lax.axis_index("tensor")
+    rows, columns = terms.shape[1:]
+    part = w.shape[1]
+    greet(n_dp, size)
+    copies = to_tensor(size, lambda peer: terms.at[peer], halves, st1, rt1)
+    halves[me_t] = terms[me_t]
+    finish(copies)
+    total = halves[0]
+    for t in range(1, size):
+        total = total + halves[t]
+    sums[...] = total
+    copies = to_data(n_dp, lambda peer: sums, every, sd1, rd1)
+    every[me_d] = total
+    finish(copies)
+    loss = every[0, rows // 2 : rows // 2 + 1, :128]
+    for p in range(1, n_dp):
+        loss = loss + every[p, rows // 2 : rows // 2 + 1, :128]
+    loss_out[...] = jnp.broadcast_to(loss, loss_out.shape)
+    dmod = every[...].reshape(n_dp * rows, columns).astype(jnp.bfloat16)
+    place = lax.rem(lax.broadcasted_iota(jnp.int32, (n_dp * rows, 1), 0), rows)
+    quarter = rows // 4
+    back = [nt(dmod, w[s]) for s in range(2)]
+    mixed = jnp.where(place < quarter, back[0], jnp.where(place < 2 * quarter, back[1], 0.0))
+    cparts[:, :, :part] = mixed.reshape(n_dp, rows, part)
+    copies = to_data(n_dp, lambda peer: cparts.at[peer], cgot, sd2, rd2)
+    cgot[me_d] = cparts[me_d]
+    for s in range(2):
+        mask = (place >= s * quarter) & (place < (s + 1) * quarter)
+        picked = jnp.where(mask, act[...], jnp.zeros((), jnp.bfloat16))
+        grad[s] = tn(picked, dmod)
+    finish(copies)
+    copies = to_tensor(size, lambda peer: cgot, cfull, st2, rt2)
+    cfull[me_t] = cgot[...]
+    finish(copies)
+    full = cfull[0]
+    for t in range(1, size):
+        full = full + cfull[t]
+    cond_out[...] = full
+
+
+def mod_backward(n_dp, size, terms, act, w_mod):
+    rows, columns = terms.shape[1:]
+    part = w_mod.shape[1]
+    lanes = -(-part // 128) * 128
+    dma = pltpu.SemaphoreType.DMA
+    f32 = jnp.float32
+    return pl.pallas_call(
+        partial(mod_back_kernel, n_dp, size),
+        in_specs=[pl.BlockSpec(memory_space=pltpu.VMEM)] * 3,
+        out_specs=[pl.BlockSpec(memory_space=pltpu.VMEM)] * 3,
+        out_shape=[
+            jax.ShapeDtypeStruct(w_mod.shape, f32),
+            jax.ShapeDtypeStruct((n_dp, rows, lanes), f32),
+            jax.ShapeDtypeStruct((8, 128), f32),
+        ],
+        scratch_shapes=[
+            pltpu.VMEM((size, rows, columns), f32),
+            pltpu.VMEM((rows, columns), f32),
+            pltpu.VMEM((n_dp, rows, columns), f32),
+            pltpu.VMEM((n_dp, rows, lanes), f32),
+            pltpu.VMEM((n_dp, rows, lanes), f32),
+            pltpu.VMEM((size, n_dp, rows, lanes), f32),
+            dma((size - 1,)), dma((size - 1,)),
+            dma((n_dp - 1,)), dma((n_dp - 1,)), dma((n_dp - 1,)), dma((n_dp - 1,)),
+            dma((size - 1,)), dma((size - 1,)),
+        ],
+        compiler_params=pltpu.CompilerParams(
+            collective_id=1, has_side_effects=True, vmem_limit_bytes=40 << 20
+        ),
+        cost_estimate=pl.CostEstimate(flops=1 << 33, bytes_accessed=1 << 21, transcendentals=0),
+    )(terms, act, w_mod)
+
+
 def on_device(
-    n_dp,
+    data,
     group,
     image,
     text,
@@ -207,32 +448,28 @@
     rows_i, rows_t = image.shape[1], text.shape[1]
     pad_t = -(-rows_t // 8) * 8
     size = group.size
-    f_qkv, f_out, f_up, f_down = (
-        lax.all_gather(w_qkv, "dp", axis=3, tiled=True),
-        lax.all_gather(w_out, "dp", axis=2, tiled=True),
-        lax.all_gather(w_up, "dp", axis=1, tiled=True),
-        lax.all_gather(w_down, "dp", axis=1, tiled=True),
+    n_dp = data.size
+    mod_all, act_all = mod_forward(n_dp, size, cond, w_mod)
+    mods = jnp.stack(
+        [
+            jnp.stack([mod_all[:, s * slots + j].reshape(6, width) for s in range(2)])
+            for j in range(slots)
+        ]
     )
-    heads = f_qkv.shape[2]
-    inner = heads * HEAD
+
+    heads = w_qkv.shape[2]
     odd = heads % 2
-    if odd:
-        f_qkv = jnp.pad(f_qkv, ((0, 0), (0, 0), (0, 1), (0, 0), (0, 0)))
-        f_out = jnp.pad(f_out, ((0, 0), (0, 1), (0, 0), (0, 0)))
-    inner_p = inner + odd * HEAD
-    f_qkv = f_qkv.reshape(2, 3 * inner_p, width)
-    f_out = f_out.reshape(2, inner_p, width)
-    here = lax.axis_index("dp")
-    cond_f = cond.astype(jnp.float32)
-
-    part = w_mod.shape[1]
-    cond_all = lax.all_gather(cond, "dp", axis=0, tiled=True).astype(jnp.float32)
-    act_all = jax.nn.silu(cond_all).astype(jnp.bfloat16)
-    act_own = lax.dynamic_slice_in_dim(act_all, here * part, part, 1)
-    mod_part = jnp.stack([nn(act_own, w_mod[s]) for s in range(2)], 1)
-    mod_sum = lax.psum_scatter(mod_part, "dp", scatter_dimension=0, tiled=True)
-    mod_full = lax.all_gather(mod_sum, "tensor", axis=2, tiled=True)
-    mods = mod_full.reshape(slots, 2, 6, width)
+
+    def by_head(blocks, pad):
+        joined = jnp.stack(blocks, -3)
+        if odd:
+            joined = jnp.pad(joined, pad)
+        return joined.reshape(2, -1, width)
+
+    f_qkv = by_head(data.gather(w_qkv), ((0, 0), (0, 0), (0, odd), (0, 0), (0, 0), (0, 0)))
+    f_out = by_head(data.gather(w_out), ((0, 0), (0, odd), (0, 0), (0, 0), (0, 0)))
+    f_up = place(data.gather(w_up))
+    f_down = place(data.gather(w_down))
 
     is_image = (lax.broadcasted_iota(jnp.int32, (rows_i + pad_t, 1), 0) < rows_i)
     is_real = (lax.broadcasted_iota(jnp.int32, (rows_i + pad_t, 1), 0) < rows_i + rows_t)
@@ -310,15 +547,46 @@
         v["dgate2"] = token_sums(v["cot"] * v["m"])
         dm = (v["cot"] * pick(j, 5)).astype(jnp.bfloat16)
         v["dm_i"], v["dm_t"] = spread(group.gather(dm))
-    loss = lax.psum(sum(v["loss"] for v in slot), ("dp", "tensor")) / (count * width)
-
-    def reduced(make, axis, shape=None):
-        g = jnp.stack([make("_t"), make("_i")]).astype(jnp.bfloat16)
-        if shape is not None:
-            g = g.reshape(shape)
-        return lax.psum_scatter(g, "dp", scatter_dimension=axis, tiled=True).astype(jnp.float32)
-
-    done_down = reduced(lambda e: sum(tn(v["dm" + e], v["hid" + e]) for v in slot), 1)
+
+    here = lax.axis_index("dp")
+    here_z, here_x = lax.div(here, data.nx), lax.rem(here, data.nx)
+
+    def exchange(own, for_x, for_z):
+        got = [data.send(for_x(xk), xk) for xk in range(1, data.nx)]
+        total = None
+        sent = []
+        for zk in range(1, data.nz):
+            part = own(zk)
+            for g in got:
+                part = part + for_z(g, zk).astype(jnp.float32)
+            sent.append(data.send(part.astype(jnp.bfloat16), zk * data.nx))
+        total = own(0)
+        for g in got:
+            total = total + for_z(g, 0).astype(jnp.float32)
+        for g in sent:
+            total = total + g.astype(jnp.float32)
+        return total
+
+    def reduced_rows(make):
+        g = [make(e).astype(jnp.bfloat16) for e in ("_t", "_i")]
+        g = [v.reshape(data.nz, data.nx, -1, v.shape[-1]) for v in g]
+        column = lambda v, xk: lax.dynamic_index_in_dim(v, flip_bits(here_x, xk, data.nx), 1, keepdims=False)
+        line = lambda v, zk, axis: lax.dynamic_index_in_dim(v, flip_bits(here_z, zk, data.nz), axis, keepdims=False)
+        return exchange(
+            lambda zk: jnp.stack([line(column(v, 0), zk, 0) for v in g]).astype(jnp.float32),
+            lambda xk: jnp.stack([column(v, xk) for v in g]),
+            lambda v, zk: line(v, zk, 1),
+        )
+
+    def reduced_heads(make, lead):
+        g = [make(e).astype(jnp.bfloat16).reshape(lead, data.nz, data.nx, -1, width) for e in ("_t", "_i")]
+        return exchange(
+            lambda zk: jnp.stack([v[:, zk, 0] for v in g]).astype(jnp.float32),
+            lambda xk: jnp.stack([v[:, :, xk] for v in g]),
+            lambda v, zk: v[:, :, zk],
+        )
+
+    done_down = reduced_rows(lambda e: sum(tn(v["dm" + e], v["hid" + e]) for v in slot))
     for j in range(slots):
         v = slot[j]
         for s, e in enumerate(("_t", "_i")):
@@ -326,7 +594,7 @@
             unused, pull = jax.vjp(partial(jax.nn.gelu, approximate=True), v["pre" + e])
             v["dpre" + e] = pull(dhid)[0].astype(jnp.bfloat16)
         v["dh2"] = scatter(lambda r: nt(v["dpre_i"][r], f_up[1]), lambda r: nt(v["dpre_t"][r], f_up[0]))
-    done_up = reduced(lambda e: sum(tn(v["h2" + e], v["dpre" + e]) for v in slot), 1)
+    done_up = reduced_rows(lambda e: sum(tn(v["h2" + e], v["dpre" + e]) for v in slot))
     for j in range(slots):
         v = slot[j]
         v["dshift2"] = token_sums(v["dh2"])
@@ -335,8 +603,7 @@
         v["dgate1"] = token_sums(v["dmid"] * v["y"])
         dy = (v["dmid"] * pick(j, 2)).astype(jnp.bfloat16)
         v["dy_i"], v["dy_t"] = spread(group.gather(dy))
-    out_shape = (2, heads + odd, HEAD, width)
-    done_out = reduced(lambda e: sum(tn(v["att" + e], v["dy" + e]) for v in slot), 2, out_shape)
+    done_out = reduced_heads(lambda e: sum(tn(v["att" + e], v["dy" + e]) for v in slot), heads + odd)
     for j in range(slots):
         v = slot[j]
         g_i = nt(v["dy_i"], f_out[1]).astype(jnp.bfloat16)
@@ -344,8 +611,8 @@
         back_i, back_t = attend_back(v["qkv_i"], v["qkv_t"], g_i, g_t, v["lse"], pad_t, rows_t)
         v["dqkv_i"], v["dqkv_t"] = jnp.concatenate(back_i, 1), jnp.concatenate(back_t, 1)
         v["dh1"] = scatter(lambda r: nn(v["dqkv_i"][r], f_qkv[1]), lambda r: nn(v["dqkv_t"][r], f_qkv[0]))
-    qkv_shape = (2, 3, heads + odd, HEAD, width)
-    done_qkv = reduced(lambda e: sum(tn(v["dqkv" + e], v["h1" + e]) for v in slot), 3, qkv_shape)
+    done_qkv = reduced_heads(lambda e: sum(tn(v["dqkv" + e], v["h1" + e]) for v in slot), 3 * (heads + odd))
+    done_qkv = done_qkv.reshape(2, 3, heads + odd, -1, width)
     grad_i, grad_t, terms = [], [], []
     for j in range(slots):
         v = slot[j]
@@ -357,15 +624,14 @@
         terms.append(
             jnp.stack([dshift1, dscale1, v["dgate1"], v["dshift2"], v["dscale2"], v["dgate2"]], 1)
         )
-    dmod = jnp.stack(terms).reshape(slots, 2, size, -1)
-    dmod = lax.psum_scatter(dmod, "tensor", scatter_dimension=2, tiled=False).astype(jnp.bfloat16)
-    dmod_all = lax.all_gather(dmod, "dp", axis=0, tiled=True)
-    done_mod = jnp.stack([tn(act_own, dmod_all[:, s]) for s in range(2)])
-    cond_part = nt(dmod_all[:, 0], w_mod[0]) + nt(dmod_all[:, 1], w_mod[1])
-    cond_sum = lax.psum(cond_part, "tensor")
-    cond_rows = lax.all_gather(cond_sum, "dp", axis=1, tiled=True)
-    cond_total = lax.dynamic_slice_in_dim(cond_rows, here * slots, slots, 0)
-    unused_value, silu_pull = jax.vjp(jax.nn.silu, cond_f)
+    lost = sum(v["loss"] for v in slot)
+    laid = jnp.stack(terms, 1).reshape(2 * slots, size, -1).transpose(1, 0, 2)
+    laid = jnp.concatenate([laid, jnp.full((size, 1, laid.shape[2]), lost), jnp.zeros((size, 2 * slots - 1, laid.shape[2]), jnp.float32)], 1)
+    done_mod, cond_rows, loss_rows = mod_backward(n_dp, size, laid, act_all, w_mod)
+    loss = loss_rows[0, 0] / (count * width)
+    cond_rows = cond_rows[:, :, : w_mod.shape[1]]
+    cond_total = (cond_rows[:, :slots] + cond_rows[:, slots : 2 * slots]).transpose(1, 0, 2).reshape(slots, width)
+    unused_value, silu_pull = jax.vjp(jax.nn.silu, cond.astype(jnp.float32))
     grad_cond = silu_pull(cond_total)[0]
     if odd:
         done_qkv, done_out = done_qkv[:, :, :heads], done_out[:, :heads]
@@ -384,7 +650,7 @@
 
 def solution(mesh):
     return jax.shard_map(
-        partial(on_device, mesh.shape["dp"], Group(mesh.shape["tensor"])),
+        partial(on_device, Data(mesh.shape["dp"]), Group(mesh.shape["tensor"])),
         mesh=mesh,
         in_specs=(
             P("dp", "tensor", None),

time: 1510 us -> 2040 us (1.35)
  Pallas kernels: 116 us -> 797 us
  blocking collectives: 197 us -> 0 us
  starting transfers between devices: 25 us -> 113 us
  other arithmetic: 95.2 us -> 68.8 us
  waiting for transfers between devices: 722 us -> 701 us
    pallas_call x0 -> x4, Pallas kernels: none -> 681 us  [the longest x2 574 us: place(): pl.pallas_call(partial(place_kernel, size), in_specs=[pl.BlockSpec(memory...]
    ppermute x0 -> x44, waiting for transfers between devices: none -> 494 us  [send(): return lax.ppermute(value, 'dp', [(p, p ^ flip) for p in range(self.size)])]
    all_gather x4 -> x0, waiting for transfers between devices: 243 us -> none  [the longest x1 116 us: on_device(): lax.all_gather(w_down, 'dp', axis=1, tiled=True)]
    reduce_scatter x2 -> x0, waiting for transfers between devices: 193 us -> none  [reduced(): lax.psum_scatter(g, 'dp', scatter_dimension=axis, tiled=True)]
    all_gather x4 -> x0, blocking collectives: 101 us -> none  [the longest x1 32.7 us: on_device(): lax.all_gather(cond, 'dp', axis=0, tiled=True).astype(jnp.float32)]
    ppermute x0 -> x44, starting transfers between devices: none -> 95 us  [send(): return lax.ppermute(value, 'dp', [(p, p ^ flip) for p in range(self.size)])]
    psum x2 -> x0, blocking collectives: 83 us -> none  [the longest x1 72 us: on_device(): lax.psum(sum((v['loss'] for v in slot)), ('dp', 'tensor')) / (count * width)]
    unnamed x12 -> x0, waiting for transfers between devices: 67.8 us -> none
  transfers between devices with their start and end apart: 57 -> 92, of which waited for: 22 -> 36; matrix products, arithmetic and copies ran while one was open for 24% -> 13% of each run, Pallas kernels for 4% -> 37%
where the time goes in v2:
time: 2040 us
  Pallas kernels  797 us (39%)
  waiting for transfers between devices  701 us (34%)
  matrix products  227 us (11%)
  local copies, waits for them, and re-layouts  120 us (6%)
  starting transfers between devices  113 us (6%)
  other arithmetic  68.8 us (3%)
    pallas_call x2, Pallas kernels, place(): pl.pallas_call(partial(place_kernel, size), in_specs=[pl.BlockSpec(memory...  574 us
    ppermute x44, waiting for transfers between devices, send(): return lax.ppermute(value, 'dp', [(p, p ^ flip) for p in range(self.size)])  494 us
    ppermute x48, waiting for transfers between devices, send(): lax.ppermute(value, 'tensor', [(t, t ^ flip) for t in range(self.size)])  206 us
    ppermute x44, starting transfers between devices, send(): return lax.ppermute(value, 'dp', [(p, p ^ flip) for p in range(self.size)])  95 us
    dot_general x24, matrix products, nn(): return jnp.dot(a, b, preferred_element_type=jnp.float32)  79.5 us
    dot_general x24, matrix products, nt(): lax.dot_general(a, b, (((1,), (1,)), ((), ())), preferred_element_type=jn...  75.5 us
    dot_general x16, matrix products, tn(): lax.dot_general(a, b, (((0,), (0,)), ((), ())), preferred_element_type=jn...  72 us
    pallas_call x2, Pallas kernels, attend_back(): pl.pallas_call(partial(back_kernel, block, valid), grid=(pairs,), in_spec...  62.6 us
  transfers between devices with their start and end apart: 92, of which 36 were waited for; matrix products, arithmetic and copies ran while one was open for 13% of the time, Pallas kernels for 37%

profile of v2, /device:TPU:0, one launch (start us, length us, event | category | flops | bytes accessed | tf_op | source)
XLA Modules:
  0.0 2037.4 jit_solution(18276223240356291505)
XLA Ops:
  12.0 57.6 %shard_map.196 = (f32[4,8,2304]{2,1,0:T(8,128)S(1)}, bf16[64,192]{1,0:T(8,128)(2,1)S(1)}) custom-call(f32[8,8,256]{2,1,0:T(8,128)S(1)} %pad.24.cond, bf16[2,192,2304]{2,1,0:T(8,128)(2,1)S(1)} %copy-done.8), custom_call_target="tpu_custom_call" | custom-call | flops 8589934592 | bytes 2097152 | tf_op jit(solution)/shard_map/pallas_call | solution.py:332
  184.8 26.8 %shard_map.201 = (bf16[1024,384]{1,0:T(8,128)(2,1)S(1)}, bf16[160,384]{1,0:T(8,128)(2,1)S(1)}, f32[3,2,1184]{2,1,0:T(2,128)S(1)}) custom-call(bf16[1024,1152]{1,0:T(8,128)(2,1)S(1)} %convolution_convert_fusion.qi.ki.vi, bf16[1024,1152]{1,0:T(8,128)(2,1)S(1)} %convolution_convert_fusion.qi.ki.vi, bf16[1024,1152]{1,0:T(8,128)(2,1)S(1)} %convolution_convert_fusion.qi.ki.vi, ...), custom_call_target="tpu_custom_call" | custom-call | flops 8613003264 | bytes 3637248 | tf_op jit(solution)/shard_map/pallas_call | solution.py:123
  245.2 27.4 %collective-permute-done.31.refs_2_ = bf16[2,192,1536]{2,1,0:T(8,128)(2,1)} collective-permute-done((bf16[2,192,1536]{2,1,0:T(8,128)(2,1)S(1)}, bf16[2,192,1536]{2,1,0:T(8,128)(2,1)}, u32[]{:S(2)}, u32[]{:S(2)}) %collective-permute-start.31) | collective-permute-done | bytes 1179680 | tf_op jit(solution)/shard_map/ppermute | solution.py:208
  273.0 29.2 %collective-permute-done.33.refs_4_ = bf16[2,192,1536]{2,1,0:T(8,128)(2,1)} collective-permute-done((bf16[2,192,1536]{2,1,0:T(8,128)(2,1)S(1)}, bf16[2,192,1536]{2,1,0:T(8,128)(2,1)}, u32[]{:S(2)}, u32[]{:S(2)}) %collective-permute-start.33) | collective-permute-done | bytes 1179680 | tf_op jit(solution)/shard_map/ppermute | solution.py:208
  305.8 18.3 collective-permute-done.24.refs_2_
  326.3 77.0 %collective-permute-done.26.refs_4_ = bf16[2,192,1536]{2,1,0:T(8,128)(2,1)} collective-permute-done((bf16[2,192,1536]{2,1,0:T(8,128)(2,1)}, bf16[2,192,1536]{2,1,0:T(8,128)(2,1)}, u32[]{:S(2)}, u32[]{:S(2)}) %collective-permute-start.26) | collective-permute-done | bytes 1179680 | tf_op jit(solution)/shard_map/ppermute | solution.py:208
  424.4 287.0 %shard_map.199 = bf16[2,1536,1536]{2,1,0:T(8,128)(2,1)} custom-call(bf16[2,192,1536]{2,1,0:T(8,128)(2,1)} %refs_0_.3, bf16[2,192,1536]{2,1,0:T(8,128)(2,1)} %copy-done.98, bf16[2,192,1536]{2,1,0:T(8,128)(2,1)} %collective-permute-done.31.refs_2_, bf16[2,192,1536]{2,1,0:T(8,128)(2,1)} %collective-permute-done.32.refs_3_, ...), custom_call_target="tpu_custom_call" | custom-call | bytes 18874368 | tf_op jit(solution)/shard_map/pallas_call | solution.py:238
  711.5 287.1 %shard_map.198 = bf16[2,1536,1536]{2,1,0:T(8,128)(2,1)} custom-call(bf16[2,192,1536]{2,1,0:T(8,128)(2,1)} %refs_0_.2, bf16[2,192,1536]{2,1,0:T(8,128)(2,1)} %collective-permute-done.23.refs_1_, bf16[2,192,1536]{2,1,0:T(8,128)(2,1)} %collective-permute-done.24.refs_2_, bf16[2,192,1536]{2,1,0:T(8,128)(2,1)} %collective-permute-done.25.refs_3_, ...), custom_call_target="tpu_custom_call" | custom-call | bytes 18874368 | tf_op jit(solution)/shard_map/pallas_call | solution.py:238
  1037.7 19.9 collective-permute-done.63
  1061.5 20.8 %collective-permute-done = bf16[296,1536]{1,0:T(8,128)(2,1)S(1)} collective-permute-done((bf16[296,1536]{1,0:T(8,128)(2,1)S(1)}, bf16[296,1536]{1,0:T(8,128)(2,1)S(1)}, u32[]{:S(2)}, u32[]{:S(2)}) %collective-permute-start) | collective-permute-done | bytes 909344 | tf_op jit(solution)/shard_map/ppermute | solution.py:182
  1094.8 26.3 %shard_map.197 = (bf16[1024,384]{1,0:T(8,128)(2,1)S(1)}, bf16[160,384]{1,0:T(8,128)(2,1)S(1)}, f32[3,2,1184]{2,1,0:T(2,128)S(1)}) custom-call(bf16[1024,1152]{1,0:T(8,128)(2,1)S(1)} %convolution_convert_fusion.1.qi.ki.vi, bf16[1024,1152]{1,0:T(8,128)(2,1)S(1)} %convolution_convert_fusion.1.qi.ki.vi, ...), custom_call_target="tpu_custom_call" | custom-call | flops 8613003264 | bytes 3637248 | tf_op jit(solution)/shard_map/pallas_call | solution.py:123
  1129.0 20.2 collective-permute-done.19
  1156.6 21.2 %collective-permute-done.20 = bf16[296,1536]{1,0:T(8,128)(2,1)} collective-permute-done((bf16[296,1536]{1,0:T(8,128)(2,1)}, bf16[296,1536]{1,0:T(8,128)(2,1)}, u32[]{:S(2)}, u32[]{:S(2)}) %collective-permute-start.20) | collective-permute-done | bytes 909344 | tf_op jit(solution)/shard_map/ppermute | solution.py:182
  1287.5 20.3 collective-permute-done.39
  1463.5 17.9 collective-permute-done.46
  1507.5 31.4 %shard_map.200 = (bf16[1024,384]{1,0:T(8,128)(2,1)S(1)}, bf16[1024,384]{1,0:T(8,128)(2,1)S(1)}, bf16[1024,384]{1,0:T(8,128)(2,1)S(1)}, bf16[160,384]{1,0:T(8,128...) custom-call(bf16[1024,1152]{1,0:T(8,128)(2,1)S(1)} %copy-done.17, ...), custom_call_target="tpu_custom_call" | custom-call | flops 21532508160 | bytes 7274496 | tf_op jit(solution)/shard_map/pallas_call | solution.py:144
  1547.1 31.2 %shard_map.202 = (bf16[1024,384]{1,0:T(8,128)(2,1)S(1)}, bf16[1024,384]{1,0:T(8,128)(2,1)S(1)}, bf16[1024,384]{1,0:T(8,128)(2,1)S(1)}, bf16[160,384]{1,0:T(8,128...) custom-call(bf16[1024,1152]{1,0:T(8,128)(2,1)S(1)} %copy-done.15, ...), custom_call_target="tpu_custom_call" | custom-call | flops 21532508160 | bytes 7274496 | tf_op jit(solution)/shard_map/pallas_call | solution.py:144
  1660.7 34.8 %collective-permute-start.81 = (bf16[2,6,8,1536]{3,2,1,0:T(8,128)(2,1)S(1)}, bf16[2,6,8,1536]{3,2,1,0:T(8,128)(2,1)S(1)}, u32[]{:S(2)}, u32[]{:S(2)}) collective-permute-start(bf16[2,6,8,1536]{3,2,1,0:T(8,128)(2,1)S(1)} %get-tuple-element.206), channel_id=1, source_target_pairs={{0,8},{4,12},{8,0},{12,4},{16,24},{20,28},{24,16},{28,20},{1,9},{5... | collective-permute-start | bytes 884744 | tf_op jit(solution)/shard_map/ppermute | solution.py:208
  1698.5 27.9 %collective-permute-done.82 = bf16[2,6,8,1536]{3,2,1,0:T(8,128)(2,1)S(1)} collective-permute-done((bf16[2,6,8,1536]{3,2,1,0:T(8,128)(2,1)S(1)}, bf16[2,6,8,1536]{3,2,1,0:T(8,128)(2,1)S(1)}, u32[]{:S(2)}, u32[]{:S(2)}) %collective-permute-start.82) | collective-permute-done | bytes 294944 | tf_op jit(solution)/shard_map/ppermute | solution.py:208
  1735.1 45.1 %collective-permute-done.86 = bf16[2,192,1536]{2,1,0:T(8,128)(2,1)S(1)} collective-permute-done((bf16[2,192,1536]{2,1,0:T(8,128)(2,1)S(1)}, bf16[2,192,1536]{2,1,0:T(8,128)(2,1)S(1)}, u32[]{:S(2)}, u32[]{:S(2)}) %collective-permute-start.86) | collective-permute-done | bytes 1179680 | tf_op jit(solution)/shard_map/ppermute | solution.py:208
  1780.7 25.2 %collective-permute-done.85 = bf16[2,192,1536]{2,1,0:T(8,128)(2,1)S(1)} collective-permute-done((bf16[2,192,1536]{2,1,0:T(8,128)(2,1)S(1)}, bf16[2,192,1536]{2,1,0:T(8,128)(2,1)S(1)}, u32[]{:S(2)}, u32[]{:S(2)}) %collective-permute-start.85) | collective-permute-done | bytes 1179680 | tf_op jit(solution)/shard_map/ppermute | solution.py:208
  1810.3 70.4 %collective-permute-done.90 = bf16[2,192,1536]{2,1,0:T(8,128)(2,1)S(1)} collective-permute-done((bf16[2,192,1536]{2,1,0:T(8,128)(2,1)S(1)}, bf16[2,192,1536]{2,1,0:T(8,128)(2,1)S(1)}, u32[]{:S(2)}, u32[]{:S(2)}) %collective-permute-start.90) | collective-permute-done | bytes 1179680 | tf_op jit(solution)/shard_map/ppermute | solution.py:208
  1897.8 49.7 %shard_map.203 = (f32[2,192,2304]{2,1,0:T(8,128)S(1)}, f32[8,8,256]{2,1,0:T(8,128)S(1)}, f32[8,128]{1,0:T(8,128)S(1)}) custom-call(f32[4,8,2304]{2,1,0:T(8,128)S(1)} %maximum_maximum_fusion.terms, bf16[64,192]{1,0:T(8,128)(2,1)S(1)} %copy-done.19, bf16[2,192,2304]{2,1,0:T(8,128)(2,1)S(1)} %copy-done.9), custom_call_target="tpu_custom_call" | custom-call | flops 8589934592 | bytes 2097152 | tf_op jit(solution)/shard_map/pallas_call | solution.py:403
  1975.8 54.7 %collective-permute-done.78 = bf16[2,18,8,1536]{3,2,1,0:T(8,128)(2,1)} collective-permute-done((bf16[2,18,8,1536]{3,2,1,0:T(8,128)(2,1)}, bf16[2,18,8,1536]{3,2,1,0:T(8,128)(2,1)}, u32[]{:S(2)}, u32[]{:S(2)}) %collective-permute-start.78) | collective-permute-done | bytes 884768 | tf_op jit(solution)/shard_map/ppermute | solution.py:208
  (1159 shorter events, 699.5 us)
Async XLA Ops:
  0.7 110.6 %collective-permute-start.3 = (bf16[2,3,6,8,1536]{4,3,2,1,0:T(8,128)(2,1)}, bf16[2,3,6,8,1536]{4,3,2,1,0:T(8,128)(2,1)}, u32[]{:S(2)}, u32[]{:S(2)}) collective-permute-start(bf16[2,3,6,8,1536]{4,3,2,1,0:T(8,128)(2,1)} %param.22), channel_id=1, source_target_pairs={{0,4},{4,0},{8,12},{12,8},{16,20},{20,16},{24,28},{28,24},{1,5},{5... | collective-permute-start | bytes 2654216 | tf_op jit(solution)/shard_map/ppermute | solution.py:208
  3.7 107.7 %collective-permute-start.4 = (bf16[2,3,6,8,1536]{4,3,2,1,0:T(8,128)(2,1)}, bf16[2,3,6,8,1536]{4,3,2,1,0:T(8,128)(2,1)}, u32[]{:S(2)}, u32[]{:S(2)}) collective-permute-start(bf16[2,3,6,8,1536]{4,3,2,1,0:T(8,128)(2,1)} %param.22), channel_id=1, source_target_pairs={{0,8},{4,12},{8,0},{12,4},{16,24},{20,28},{24,16},{28,20},{1,9},{5... | collective-permute-start | bytes 2654216 | tf_op jit(solution)/shard_map/ppermute | solution.py:208
  5.2 106.7 %collective-permute-start.6 = (bf16[2,3,6,8,1536]{4,3,2,1,0:T(8,128)(2,1)}, bf16[2,3,6,8,1536]{4,3,2,1,0:T(8,128)(2,1)}, u32[]{:S(2)}, u32[]{:S(2)}) collective-permute-start(bf16[2,3,6,8,1536]{4,3,2,1,0:T(8,128)(2,1)} %param.22), channel_id=1, source_target_pairs={{0,16},{4,20},{8,24},{12,28},{16,0},{20,4},{24,8},{28,12},{1,17},{... | collective-permute-start | bytes 2654216 | tf_op jit(solution)/shard_map/ppermute | solution.py:208
  221.8 82.0 %collective-permute-start.35 = (bf16[2,192,1536]{2,1,0:T(8,128)(2,1)S(1)}, bf16[2,192,1536]{2,1,0:T(8,128)(2,1)}, u32[]{:S(2)}, u32[]{:S(2)}) collective-permute-start(bf16[2,192,1536]{2,1,0:T(8,128)(2,1)S(1)} %copy-done.97), channel_id=1, source_target_pairs={{0,24},{4,28},{8,16},{12,20},{16,8},{20,12},{24,0},{28,4},{1,25},{... | collective-permute-start | bytes 3538952 | tf_op jit(solution)/shard_map/ppermute | solution.py:208
  241.7 82.4 %collective-permute-start.24 = (bf16[2,192,1536]{2,1,0:T(8,128)(2,1)}, bf16[2,192,1536]{2,1,0:T(8,128)(2,1)}, u32[]{:S(2)}, u32[]{:S(2)}) collective-permute-start(bf16[2,192,1536]{2,1,0:T(8,128)(2,1)} %refs_0_.2), channel_id=1, source_target_pairs={{0,8},{4,12},{8,0},{12,4},{16,24},{20,28},{24,16},{28,20},{1,9},{5... | collective-permute-start | bytes 3538952 | tf_op jit(solution)/shard_map/ppermute | solution.py:208
  272.6 130.7 %collective-permute-start.26 = (bf16[2,192,1536]{2,1,0:T(8,128)(2,1)}, bf16[2,192,1536]{2,1,0:T(8,128)(2,1)}, u32[]{:S(2)}, u32[]{:S(2)}) collective-permute-start(bf16[2,192,1536]{2,1,0:T(8,128)(2,1)} %refs_0_.2), channel_id=1, source_target_pairs={{0,16},{4,20},{8,24},{12,28},{16,0},{20,4},{24,8},{28,12},{1,17},{... | collective-permute-start | bytes 3538952 | tf_op jit(solution)/shard_map/ppermute | solution.py:208
  302.1 103.0 %collective-permute-start.28 = (bf16[2,192,1536]{2,1,0:T(8,128)(2,1)}, bf16[2,192,1536]{2,1,0:T(8,128)(2,1)}, u32[]{:S(2)}, u32[]{:S(2)}) collective-permute-start(bf16[2,192,1536]{2,1,0:T(8,128)(2,1)} %refs_0_.2), channel_id=1, source_target_pairs={{0,24},{4,28},{8,16},{12,20},{16,8},{20,12},{24,0},{28,4},{1,25},{... | collective-permute-start | bytes 3538952 | tf_op jit(solution)/shard_map/ppermute | solution.py:208
  303.7 102.2 %collective-permute-start.32 = (bf16[2,192,1536]{2,1,0:T(8,128)(2,1)}, bf16[2,192,1536]{2,1,0:T(8,128)(2,1)}, u32[]{:S(2)}, u32[]{:S(2)}) collective-permute-start(bf16[2,192,1536]{2,1,0:T(8,128)(2,1)} %collective-permute-done.31.refs_2_), channel_id=1, source_target_pairs={{0,4},{4,0},{8,12},{12,8},{16,20},{20,16},{24,28},{28,24},{1,5},{5... | collective-permute-start | bytes 3538952 | tf_op jit(solution)/shard_map/ppermute | solution.py:208
  304.4 102.9 %collective-permute-start.34 = (bf16[2,192,1536]{2,1,0:T(8,128)(2,1)}, bf16[2,192,1536]{2,1,0:T(8,128)(2,1)}, u32[]{:S(2)}, u32[]{:S(2)}) collective-permute-start(bf16[2,192,1536]{2,1,0:T(8,128)(2,1)} %collective-permute-done.33.refs_4_), channel_id=1, source_target_pairs={{0,4},{4,0},{8,12},{12,8},{16,20},{20,16},{24,28},{28,24},{1,5},{5... | collective-permute-start | bytes 3538952 | tf_op jit(solution)/shard_map/ppermute | solution.py:208
  324.0 84.2 %collective-permute-start.36 = (bf16[2,192,1536]{2,1,0:T(8,128)(2,1)}, bf16[2,192,1536]{2,1,0:T(8,128)(2,1)}, u32[]{:S(2)}, u32[]{:S(2)}) collective-permute-start(bf16[2,192,1536]{2,1,0:T(8,128)(2,1)} %collective-permute-done.35.refs_6_), channel_id=1, source_target_pairs={{0,4},{4,0},{8,12},{12,8},{16,20},{20,16},{24,28},{28,24},{1,5},{5... | collective-permute-start | bytes 3538952 | tf_op jit(solution)/shard_map/ppermute | solution.py:208
  405.2 306.3 %collective-permute-start.25 = (bf16[2,192,1536]{2,1,0:T(8,128)(2,1)}, bf16[2,192,1536]{2,1,0:T(8,128)(2,1)}, u32[]{:S(2)}, u32[]{:S(2)}) collective-permute-start(bf16[2,192,1536]{2,1,0:T(8,128)(2,1)} %collective-permute-done.24.refs_2_), channel_id=1, source_target_pairs={{0,4},{4,0},{8,12},{12,8},{16,20},{20,16},{24,28},{28,24},{1,5},{5... | collective-permute-start | bytes 3538952 | tf_op jit(solution)/shard_map/ppermute | solution.py:208
  405.9 305.6 %collective-permute-start.27 = (bf16[2,192,1536]{2,1,0:T(8,128)(2,1)}, bf16[2,192,1536]{2,1,0:T(8,128)(2,1)}, u32[]{:S(2)}, u32[]{:S(2)}) collective-permute-start(bf16[2,192,1536]{2,1,0:T(8,128)(2,1)} %collective-permute-done.26.refs_4_), channel_id=1, source_target_pairs={{0,4},{4,0},{8,12},{12,8},{16,20},{20,16},{24,28},{28,24},{1,5},{5... | collective-permute-start | bytes 3538952 | tf_op jit(solution)/shard_map/ppermute | solution.py:208
  407.3 304.2 %collective-permute-start.29 = (bf16[2,192,1536]{2,1,0:T(8,128)(2,1)}, bf16[2,192,1536]{2,1,0:T(8,128)(2,1)}, u32[]{:S(2)}, u32[]{:S(2)}) collective-permute-start(bf16[2,192,1536]{2,1,0:T(8,128)(2,1)} %collective-permute-done.28.refs_6_), channel_id=1, source_target_pairs={{0,4},{4,0},{8,12},{12,8},{16,20},{20,16},{24,28},{28,24},{1,5},{5... | collective-permute-start | bytes 3538952 | tf_op jit(solution)/shard_map/ppermute | solution.py:208
  408.2 593.6 %collective-permute-start.59 = (bf16[296,1536]{1,0:T(8,128)(2,1)}, bf16[296,1536]{1,0:T(8,128)(2,1)}, u32[]{:S(2)}, u32[]{:S(2)}) collective-permute-start(bf16[296,1536]{1,0:T(8,128)(2,1)} %add_convert_fusion.2), channel_id=1, source_target_pairs={{0,1},{1,0},{2,3},{3,2},{4,5},{5,4},{6,7},{7,6},{8,9},{9,8},{10,11... | collective-permute-start | bytes 2727944 | tf_op jit(solution)/shard_map/ppermute | solution.py:182
  423.0 582.5 %collective-permute-start.60 = (bf16[296,1536]{1,0:T(8,128)(2,1)}, bf16[296,1536]{1,0:T(8,128)(2,1)}, u32[]{:S(2)}, u32[]{:S(2)}) collective-permute-start(bf16[296,1536]{1,0:T(8,128)(2,1)} %collective-permute-done.58), channel_id=1, source_target_pairs={{0,1},{1,0},{2,3},{3,2},{4,5},{5,4},{6,7},{7,6},{8,9},{9,8},{10,11... | collective-permute-start | bytes 2727944 | tf_op jit(solution)/shard_map/ppermute | solution.py:182
  1400.7 247.4 %collective-permute-start.84 = (bf16[2,4,192,1536]{3,2,0,1:T(8,128)(2,1)}, bf16[2,4,192,1536]{3,2,0,1:T(8,128)(2,1)}, u32[]{:S(2)}, u32[]{:S(2)}) collective-permute-start(bf16[2,4,192,1536]{3,2,0,1:T(8,128)(2,1)} %pad_maximum_fusion), channel_id=1, source_target_pairs={{0,4},{4,0},{8,12},{12,8},{16,20},{20,16},{24,28},{28,24},{1,5},{5... | collective-permute-start | bytes 14155784 | tf_op jit(solution)/shard_map/ppermute | solution.py:208
  1482.6 171.0 %collective-permute-start.88 = (bf16[2,4,192,1536]{3,2,0,1:T(8,128)(2,1)}, bf16[2,4,192,1536]{3,2,0,1:T(8,128)(2,1)}, u32[]{:S(2)}, u32[]{:S(2)}) collective-permute-start(bf16[2,4,192,1536]{3,2,0,1:T(8,128)(2,1)} %pad_maximum_fusion.1), channel_id=1, source_target_pairs={{0,4},{4,0},{8,12},{12,8},{16,20},{20,16},{24,28},{28,24},{1,5},{5... | collective-permute-start | bytes 14155784 | tf_op jit(solution)/shard_map/ppermute | solution.py:208
  1612.7 116.9 %collective-permute-start.49 = (bf16[512,1536]{1,0:T(8,128)(2,1)}, bf16[512,1536]{1,0:T(8,128)(2,1)S(1)}, u32[]{:S(2)}, u32[]{:S(2)}) collective-permute-start(bf16[512,1536]{1,0:T(8,128)(2,1)} %convolution_convert_fusion.3), channel_id=1, source_target_pairs={{0,1},{1,0},{2,3},{3,2},{4,5},{5,4},{6,7},{7,6},{8,9},{9,8},{10,11... | collective-permute-start | bytes 4718600 | tf_op jit(solution)/shard_map/ppermute | solution.py:182
  1629.4 102.9 %collective-permute-start.73 = (bf16[512,1536]{1,0:T(8,128)(2,1)S(1)}, bf16[512,1536]{1,0:T(8,128)(2,1)S(1)}, u32[]{:S(2)}, u32[]{:S(2)}) collective-permute-start(bf16[512,1536]{1,0:T(8,128)(2,1)S(1)} %convolution_convert_fusion.2), channel_id=1, source_target_pairs={{0,1},{1,0},{2,3},{3,2},{4,5},{5,4},{6,7},{7,6},{8,9},{9,8},{10,11... | collective-permute-start | bytes 4718600 | tf_op jit(solution)/shard_map/ppermute | solution.py:182
  1651.3 81.1 %collective-permute-start.87 = (bf16[2,192,1536]{2,1,0:T(8,128)(2,1)S(1)}, bf16[2,192,1536]{2,1,0:T(8,128)(2,1)S(1)}, u32[]{:S(2)}, u32[]{:S(2)}) collective-permute-start(bf16[2,192,1536]{2,1,0:T(8,128)(2,1)S(1)} %get-tuple-element.153), channel_id=1, source_target_pairs={{0,24},{4,28},{8,16},{12,20},{16,8},{20,12},{24,0},{28,4},{1,25},{... | collective-permute-start | bytes 3538952 | tf_op jit(solution)/shard_map/ppermute | solution.py:208
  1732.3 148.3 %collective-permute-start.90 = (bf16[2,192,1536]{2,1,0:T(8,128)(2,1)S(1)}, bf16[2,192,1536]{2,1,0:T(8,128)(2,1)S(1)}, u32[]{:S(2)}, u32[]{:S(2)}) collective-permute-start(bf16[2,192,1536]{2,1,0:T(8,128)(2,1)S(1)} %get-tuple-element.143), channel_id=1, source_target_pairs={{0,16},{4,20},{8,24},{12,28},{16,0},{20,4},{24,8},{28,12},{1,17},{... | collective-permute-start | bytes 3538952 | tf_op jit(solution)/shard_map/ppermute | solution.py:208
  1732.4 148.2 %collective-permute-start.89 = (bf16[2,192,1536]{2,1,0:T(8,128)(2,1)S(1)}, bf16[2,192,1536]{2,1,0:T(8,128)(2,1)S(1)}, u32[]{:S(2)}, u32[]{:S(2)}) collective-permute-start(bf16[2,192,1536]{2,1,0:T(8,128)(2,1)S(1)} %get-tuple-element.141), channel_id=1, source_target_pairs={{0,8},{4,12},{8,0},{12,4},{16,24},{20,28},{24,16},{28,20},{1,9},{5... | collective-permute-start | bytes 3538952 | tf_op jit(solution)/shard_map/ppermute | solution.py:208
  1780.2 104.2 %collective-permute-start.51 = (bf16[296,1536]{1,0:T(8,128)(2,1)S(1)}, bf16[296,1536]{1,0:T(8,128)(2,1)S(1)}, u32[]{:S(2)}, u32[]{:S(2)}) collective-permute-start(bf16[296,1536]{1,0:T(8,128)(2,1)S(1)} %pad_maximum_fusion.16), channel_id=1, source_target_pairs={{0,2},{1,3},{2,0},{3,1},{4,6},{5,7},{6,4},{7,5},{8,10},{9,11},{10,... | collective-permute-start | bytes 2727944 | tf_op jit(solution)/shard_map/ppermute | solution.py:182
  1810.0 137.5 %collective-permute-start.76 = (bf16[2,18,4,8,1536]{4,3,1,0,2:T(8,128)(2,1)}, bf16[2,18,4,8,1536]{4,3,1,0,2:T(8,128)(2,1)}, u32[]{:S(2)}, u32[]{:S(2)}) collective-permute-start(bf16[2,18,4,8,1536]{4,3,1,0,2:T(8,128)(2,1)} %pad_maximum_fusion.2), channel_id=1, source_target_pairs={{0,4},{4,0},{8,12},{12,8},{16,20},{20,16},{24,28},{28,24},{1,5},{5... | collective-permute-start | bytes 10616840 | tf_op jit(solution)/shard_map/ppermute | solution.py:208
  (377 other events, 10677.7 us)

commit v3 on v2

v3 whole, which is shorter than its diff:
```python
import math
from functools import partial

import jax
import jax.numpy as jnp
from jax import lax
from jax.experimental import pallas as pl
from jax.experimental.pallas import tpu as pltpu
from jax.sharding import PartitionSpec as P

norm_eps = 1e-06

LOG2E = math.log2(math.e)
HEAD = 64


def nt(a, b):
    return lax.dot_general(a, b, (((1,), (1,)), ((), ())), preferred_element_type=jnp.float32)


def nn(a, b):
    return jnp.dot(a, b, preferred_element_type=jnp.float32)


def query_blocks(rows_img, rows_txt):
    step = 256 if rows_img % 256 == 0 else rows_img
    return [(0, s, step) for s in range(0, rows_img, step)] + [(1, 0, rows_txt)]


def pad_bias(rows, block, valid):
    place = lax.broadcasted_iota(jnp.int32, (rows, 1), 0)
    return jnp.where(lax.rem(place, block) < valid, 0.0, -1e30).astype(jnp.float32)


def attend_kernel(block, valid, qi, ki, vi, qt, kt, vt, oi, ot, lse):
    factor = HEAD**-0.5
    low = lax.broadcasted_iota(jnp.int32, (1, 2 * HEAD), 1) < HEAD
    zero = jnp.zeros((), jnp.bfloat16)
    bias = pad_bias(qt.shape[0], block, valid)
    vit, vtt = vi[...].T, vt[...].T
    keys = []
    for h in range(2):
        mask = low if h == 0 else ~low
        keys.append((jnp.where(mask, ki[...], zero), jnp.where(mask, kt[...], zero)))
    at = 0
    for which, start, size in query_blocks(qi.shape[0], qt.shape[0]):
        src, dst = (qi, oi) if which == 0 else (qt, ot)
        q = src[start : start + size, :]
        parts = []
        for h in range(2):
            s_i = nt(keys[h][0], q)
            s_t = nt(keys[h][1], q) + bias
            top = jnp.maximum(
                jnp.max(s_i, 0, keepdims=True), jnp.max(s_t, 0, keepdims=True)
            )
            e_i = jnp.exp2((s_i - top) * (factor * LOG2E))
            e_t = jnp.exp2((s_t - top) * (factor * LOG2E))
            total = jnp.sum(e_i, 0, keepdims=True) + jnp.sum(e_t, 0, keepdims=True)
            inv = 1.0 / total
            p_i = (e_i * inv).astype(jnp.bfloat16)
            p_t = (e_t * inv).astype(jnp.bfloat16)
            rows = slice(h * HEAD, (h + 1) * HEAD)
            parts.append(nn(vit[rows], p_i) + nn(vtt[rows], p_t))
            lse[0, h : h + 1, at : at + size] = top * (factor * LOG2E) + jnp.log2(total)
        dst[start : start + size, :] = jnp.concatenate(parts, 0).T.astype(jnp.bfloat16)
        at += size


def back_kernel(block, valid, qi, ki, vi, qt, kt, vt, gi, gt, lse, d_i, d_t, aki, avi, akt, avt):
    dqi, dki, dvi = (d_i.at[k] for k in range(3))
    dqt, dkt, dvt = (d_t.at[k] for k in range(3))
    factor = HEAD**-0.5
    low = lax.broadcasted_iota(jnp.int32, (1, 2 * HEAD), 1) < HEAD
    zero = jnp.zeros((), jnp.bfloat16)
    bias = pad_bias(qt.shape[0], block, valid)
    kit, ktt = ki[...].T, kt[...].T
    masks = [low, ~low]
    at = 0
    first = True
    for which, start, size in query_blocks(qi.shape[0], qt.shape[0]):
        q_ref, g_ref, d_ref = (qi, gi, dqi) if which == 0 else (qt, gt, dqt)
        q, g = q_ref[start : start + size, :], g_ref[start : start + size, :]
        parts = []
        for h in range(2):
            q_h, g_h = jnp.where(masks[h], q, zero), jnp.where(masks[h], g, zero)
            stat = lse[0, h : h + 1, at : at + size]
            p_i = jnp.exp2(nt(ki[...], q_h) * (factor * LOG2E) - stat)
            p_t = jnp.exp2((nt(kt[...], q_h) + bias) * (factor * LOG2E) - stat)
            e_i, e_t = nt(vi[...], g_h), nt(vt[...], g_h)
            delta = jnp.sum(e_i * p_i, 0, keepdims=True) + jnp.sum(e_t * p_t, 0, keepdims=True)
            s_i = (p_i * (e_i - delta)).astype(jnp.bfloat16)
            s_t = (p_t * (e_t - delta)).astype(jnp.bfloat16)
            v_i = nn(p_i.astype(jnp.bfloat16), g_h)
            v_t = nn(p_t.astype(jnp.bfloat16), g_h)
            k_i = nn(s_i, q_h)
            k_t = nn(s_t, q_h)
            if first:
                avi[...], avt[...], aki[...], akt[...] = v_i, v_t, k_i, k_t
                first = False
            else:
                avi[...] += v_i
                avt[...] += v_t
                aki[...] += k_i
                akt[...] += k_t
            rows = slice(h * HEAD, (h + 1) * HEAD)
            parts.append(nn(kit[rows], s_i) + nn(ktt[rows], s_t))
        d_ref[start : start + size, :] = (jnp.concatenate(parts, 0).T * factor).astype(jnp.bfloat16)
        at += size
    dki[...] = (aki[...] * factor).astype(jnp.bfloat16)
    dkt[...] = (akt[...] * factor).astype(jnp.bfloat16)
    dvi[...] = avi[...].astype(jnp.bfloat16)
    dvt[...] = avt[...].astype(jnp.bfloat16)


def kind_specs(rows):
    return [pl.BlockSpec((None, rows, 2 * HEAD), partial(lambda k, p: (k, 0, p), k)) for k in range(3)]


def attend(qkv_img, qkv_txt, block, valid):
    n_i, n_t, inner = qkv_img.shape[1], qkv_txt.shape[1], qkv_img.shape[2]
    pairs = inner // (2 * HEAD)
    col = lambda rows: pl.BlockSpec((rows, 2 * HEAD), lambda p: (0, p))
    return pl.pallas_call(
        partial(attend_kernel, block, valid),
        grid=(pairs,),
        in_specs=kind_specs(n_i) + kind_specs(n_t),
        out_specs=[col(n_i), col(n_t), pl.BlockSpec((1, 2, n_i + n_t), lambda p: (p, 0, 0))],
        out_shape=[
            jax.ShapeDtypeStruct((n_i, inner), jnp.bfloat16),
            jax.ShapeDtypeStruct((n_t, inner), jnp.bfloat16),
            jax.ShapeDtypeStruct((pairs, 2, n_i + n_t), jnp.float32),
        ],
        compiler_params=pltpu.CompilerParams(vmem_limit_bytes=40 << 20),
        cost_estimate=pl.CostEstimate(flops=1 << 34, bytes_accessed=1 << 23, transcendentals=0),
    )(*([qkv_img] * 3 + [qkv_txt] * 3))


def attend_back(qkv_img, qkv_txt, g_img, g_txt, lse, block, valid):
    n_i, n_t, inner = qkv_img.shape[1], qkv_txt.shape[1], qkv_img.shape[2]
    pairs = inner // (2 * HEAD)
    col = lambda rows: pl.BlockSpec((rows, 2 * HEAD), lambda p: (0, p))
    return pl.pallas_call(
        partial(back_kernel, block, valid),
        grid=(pairs,),
        in_specs=kind_specs(n_i)
        + kind_specs(n_t)
        + [col(n_i), col(n_t), pl.BlockSpec((1, 2, n_i + n_t), lambda p: (p, 0, 0))],
        out_specs=[pl.BlockSpec((3, rows, 2 * HEAD), lambda p: (0, 0, p)) for rows in (n_i, n_t)],
        out_shape=[jax.ShapeDtypeStruct((3, rows, inner), jnp.bfloat16) for rows in (n_i, n_t)],
        scratch_shapes=[pltpu.VMEM((n, 2 * HEAD), jnp.float32) for n in (n_i, n_i, n_t, n_t)],
        compiler_params=pltpu.CompilerParams(vmem_limit_bytes=40 << 20),
        cost_estimate=pl.CostEstimate(flops=1 << 35, bytes_accessed=1 << 24, transcendentals=0),
    )(*([qkv_img] * 3 + [qkv_txt] * 3 + [g_img, g_txt, lse]))


def tn(a, b):
    return lax.dot_general(a, b, (((0,), (0,)), ((), ())), preferred_element_type=jnp.float32)


def norm_forward(values):
    center = jnp.mean(values, -1, keepdims=True)
    spread = jnp.mean(jnp.square(values - center), -1, keepdims=True)
    rstd = lax.rsqrt(spread + norm_eps)
    return ((values - center) * rstd, rstd)


def norm_backward(grads, hats, rstd):
    first = jnp.mean(grads, -1, keepdims=True)
    second = jnp.mean(grads * hats, -1, keepdims=True)
    return rstd * (grads - first - hats * second)


def tile(n):
    return 512 if n % 512 == 0 else 256 if n % 256 == 0 else n


def dot_kind(a, w, flip):
    return nt(a, w) if flip else nn(a, w)


def gelu_parts(x):
    c, a = math.sqrt(2.0 / math.pi), 0.044715
    square = x * x
    t = jnp.tanh(c * (x + a * (x * square)))
    slope = 0.5 * (1.0 + t) + 0.5 * x * (1.0 - t * t) * (c * (1.0 + 3.0 * a * square))
    return 0.5 * x * (1.0 + t), slope


def up_kernel(flip, at, ai, w, ht, hi, st, si):
    for s, (a, h, slope) in enumerate(((at, ht, st), (ai, hi, si))):
        value, d = gelu_parts(dot_kind(a[...], w[s], flip))
        h[...] = value.astype(jnp.bfloat16)
        slope[...] = d


def scaled_kernel(flip, at, ai, w, st, si, ot, oi):
    for s, (a, o, slope) in enumerate(((at, ot, st), (ai, oi, si))):
        o[...] = (dot_kind(a[...], w[s], flip) * slope[...]).astype(jnp.bfloat16)


def plain_kernel(flip, at, ai, w, ot, oi):
    for s, (a, o) in enumerate(((at, ot), (ai, oi))):
        o[...] = dot_kind(a[...], w[s], flip).astype(jnp.bfloat16)


def qkv_kernel(at, ai, w, ot, oi):
    for s, (a, o) in enumerate(((at, ot), (ai, oi))):
        o[0] = nt(a[...], w[s, 0]).astype(jnp.bfloat16)


def halves_kernel(flip, at, ai, w, top, own):
    for s, a in ((1, ai), (0, at)):
        half = a.shape[-2] // 2
        start = 0 if s == 1 else ai.shape[-2] // 2
        if len(a.shape) == 3:
            total = nn(a[0], w[s, 0])
            for k in range(1, a.shape[0]):
                total = total + nn(a[k], w[s, k])
        else:
            total = dot_kind(a[...], w[s], flip)
        own[start : start + half, :] = total[:half]
        top[start : start + half, :] = total[half:].astype(jnp.bfloat16)


def over_columns(kernel, operands, w, flip, extra, outs, columns):
    step = tile(columns)
    whole = lambda v: pl.BlockSpec(v.shape, lambda n: (0,) * v.ndim)
    if w.ndim == 4:
        w_spec = pl.BlockSpec(w.shape[:3] + (step,), lambda n: (0, 0, 0, n))
    elif flip:
        w_spec = pl.BlockSpec((2, step, w.shape[2]), lambda n: (0, n, 0))
    else:
        w_spec = pl.BlockSpec((2, w.shape[1], step), lambda n: (0, 0, n))
    by_tile = lambda v: pl.BlockSpec((v.shape[0], step), lambda n: (0, n))
    return pl.pallas_call(
        kernel,
        grid=(columns // step,),
        in_specs=[whole(v) for v in operands] + [w_spec] + [by_tile(v) for v in extra],
        out_specs=[by_tile(v) for v in outs],
        out_shape=outs,
        compiler_params=pltpu.CompilerParams(vmem_limit_bytes=40 << 20),
        cost_estimate=pl.CostEstimate(flops=1 << 33, bytes_accessed=1 << 23, transcendentals=0),
    )(*operands, w, *extra)


def shaped(rows, columns, kind):
    return jax.ShapeDtypeStruct((rows, columns), kind)


def up_and_slope(at, ai, w):
    n = w.shape[2]
    kinds = [jnp.bfloat16, jnp.bfloat16, jnp.float32, jnp.float32]
    rows = [at.shape[0], ai.shape[0]] * 2
    outs = [shaped(r, n, k) for r, k in zip(rows, kinds)]
    return over_columns(partial(up_kernel, False), [at, ai], w, False, [], outs, n)


def scaled(at, ai, w, st, si):
    outs = [shaped(v.shape[0], w.shape[2], jnp.bfloat16) for v in (at, ai)]
    return over_columns(partial(scaled_kernel, False), [at, ai], w, False, [st, si], outs, w.shape[2])


def plain(at, ai, w):
    outs = [shaped(v.shape[0], w.shape[1], jnp.bfloat16) for v in (at, ai)]
    return over_columns(partial(plain_kernel, True), [at, ai], w, True, [], outs, w.shape[1])


def halves(at, ai, w, flip):
    columns = w.shape[1] if flip else w.shape[-1]
    rows = (at.shape[-2] + ai.shape[-2]) // 2
    outs = [shaped(rows, columns, jnp.bfloat16), shaped(rows, columns, jnp.float32)]
    return over_columns(partial(halves_kernel, flip), [at, ai], w, flip, [], outs, columns)


def project_qkv(at, ai, w):
    inner = w.shape[2]
    whole = lambda v: pl.BlockSpec(v.shape, lambda n: (0, 0))
    outs = [jax.ShapeDtypeStruct((3, v.shape[0], inner), jnp.bfloat16) for v in (at, ai)]
    return pl.pallas_call(
        qkv_kernel,
        grid=(3,),
        in_specs=[whole(at), whole(ai), pl.BlockSpec((2, 1) + w.shape[2:], lambda n: (0, n, 0, 0))],
        out_specs=[pl.BlockSpec((1,) + v.shape[1:], lambda n: (n, 0, 0)) for v in outs],
        out_shape=outs,
        compiler_params=pltpu.CompilerParams(vmem_limit_bytes=40 << 20),
        cost_estimate=pl.CostEstimate(flops=1 << 33, bytes_accessed=1 << 23, transcendentals=0),
    )(at, ai, w)


def outer_kernel(n, *refs):
    left, right, out = refs[: 2 * n], refs[2 * n : 4 * n], refs[4 * n]
    for s in range(2):
        total = None
        for j in range(n):
            a = left[s * n + j]
            a = a[0] if len(a.shape) == 3 else a[...]
            term = tn(a, right[s * n + j][...])
            total = term if total is None else total + term
        if len(out.shape) == 3:
            out[s] = total.astype(jnp.bfloat16)
            continue
        ranks = out.shape[1]
        part = HEAD // ranks
        for p in range(ranks):
            rows = [total[h + p * part : h + (p + 1) * part] for h in range(0, total.shape[0], HEAD)]
            out[s, p] = jnp.concatenate(rows, 0).astype(jnp.bfloat16)


def outer(left_t, left_i, right_t, right_i, ranks=None):
    n = len(left_t)
    left, right = left_t + left_i, right_t + right_i
    columns = right[0].shape[1]
    if left[0].ndim == 3:
        step, steps = left[0].shape[2], left[0].shape[0]
        l_spec = lambda v: pl.BlockSpec((1,) + v.shape[1:], lambda m: (m, 0, 0))
    else:
        width = left[0].shape[1]
        step = 512 if width % 512 == 0 else width if width < 512 else 256
        steps = width // step
        l_spec = lambda v: pl.BlockSpec((v.shape[0], step), lambda m: (0, m))
    return pl.pallas_call(
        partial(outer_kernel, n),
        grid=(steps,),
        in_specs=[l_spec(v) for v in left] + [pl.BlockSpec(v.shape, lambda m: (0, 0)) for v in right],
        out_specs=pl.BlockSpec((2, step, columns), lambda m: (0, m, 0))
        if ranks is None
        else pl.BlockSpec((2, ranks, step // ranks, columns), lambda m: (0, 0, m, 0)),
        out_shape=jax.ShapeDtypeStruct(
            (2, steps * step, columns) if ranks is None else (2, ranks, steps * step // ranks, columns),
            jnp.bfloat16,
        ),
        compiler_params=pltpu.CompilerParams(vmem_limit_bytes=52 << 20),
        cost_estimate=pl.CostEstimate(flops=1 << 34, bytes_accessed=1 << 24, transcendentals=0),
    )(*left, *right)


class Group:
    def __init__(self, size):
        self.size = size
        self.evens = [2 * k for k in range(size // 2)]
        self.odds = [2 * k + 1 for k in range(size // 2)]
        self.order = self.evens + self.odds

    def send(self, value, flip):
        return lax.ppermute(value, "tensor", [(t, t ^ flip) for t in range(self.size)])

    def gather(self, own):
        evens = [own] + [self.send(own, flip) for flip in self.evens[1:]]
        return evens + [self.send(value, 1) for value in evens]


MESH = pl.DeviceIdType.MESH


def flip_bits(index, flip, size):
    total, bit = 0, 1
    while bit < size:
        digit = lax.rem(lax.div(index, bit), 2)
        total = total + bit * ((1 - digit) if flip & bit else digit)
        bit *= 2
    return total


class Data:
    def __init__(self, size):
        self.size = size
        self.nx = math.isqrt(size // 2)
        self.nz = size // self.nx


def pass_kernel(*refs):
    pass


def gate(values, others):
    others = jax.tree.leaves(list(others))
    n = len(values)
    anywhere = pl.BlockSpec(memory_space=pl.ANY)
    return pl.pallas_call(
        pass_kernel,
        in_specs=[anywhere] * (n + len(others)),
        out_specs=[anywhere] * n,
        out_shape=[jax.ShapeDtypeStruct(v.shape, v.dtype) for v in values],
        input_output_aliases={i: i for i in range(n)},
        compiler_params=pltpu.CompilerParams(vmem_limit_bytes=1 << 20),
        cost_estimate=pl.CostEstimate(flops=1 << 10, bytes_accessed=1 << 10, transcendentals=0),
    )(*values, *others)


def after(value, *others):
    return gate([value], others)[0]


def greet(n_dp, size):
    me_d, me_t = lax.axis_index("dp"), lax.axis_index("tensor")
    barrier = pltpu.get_barrier_semaphore()
    for k in range(1, n_dp):
        pl.semaphore_signal(barrier, inc=1, device_id=(flip_bits(me_d, k, n_dp), me_t), device_id_type=MESH)
    for k in range(1, size):
        pl.semaphore_signal(barrier, inc=1, device_id=(me_d, flip_bits(me_t, k, size)), device_id_type=MESH)
    pl.semaphore_wait(barrier, n_dp + size - 2)


def to_data(n_dp, source, target, send, recv):
    me_d, me_t = lax.axis_index("dp"), lax.axis_index("tensor")
    copies = []
    for k in range(1, n_dp):
        peer = flip_bits(me_d, k, n_dp)
        copy = pltpu.make_async_remote_copy(
            src_ref=source(peer),
            dst_ref=target.at[me_d],
            send_sem=send.at[k - 1],
            recv_sem=recv.at[k - 1],
            device_id=(peer, me_t),
            device_id_type=MESH,
        )
        copy.start()
        copies.append(copy)
    return copies


def to_tensor(size, source, target, send, recv):
    me_d, me_t = lax.axis_index("dp"), lax.axis_index("tensor")
    copies = []
    for k in range(1, size):
        peer = flip_bits(me_t, k, size)
        copy = pltpu.make_async_remote_copy(
            src_ref=source(peer),
            dst_ref=target.at[me_t],
            send_sem=send.at[k - 1],
            recv_sem=recv.at[k - 1],
            device_id=(me_d, peer),
            device_id_type=MESH,
        )
        copy.start()
        copies.append(copy)
    return copies


def finish(copies):
    for copy in copies:
        copy.wait()


def mod_kernel(n_dp, size, cond, w, mod_out, act_out, conds, parts, got, own, sd1, rd1, sd2, rd2, st, rt):
    me_d, me_t = lax.axis_index("dp"), lax.axis_index("tensor")
    rows, part, columns = conds.shape[1], w.shape[1], w.shape[2] // 2
    greet(n_dp, size)
    copies = to_data(n_dp, lambda peer: cond.at[peer], conds, sd1, rd1)
    conds[me_d] = cond[me_d]
    finish(copies)
    value = conds[...].reshape(n_dp * rows, conds.shape[2])[:, :part]
    act = (value * jax.nn.sigmoid(value)).astype(jnp.bfloat16)
    act_out[...] = act
    place = lax.rem(lax.broadcasted_iota(jnp.int32, (n_dp * rows, 1), 0), rows)
    first = lax.rem(place, rows // 2) < rows // 4
    mixed = [
        jnp.where(first, nn(act, w[0, :, cut]), nn(act, w[1, :, cut]))
        for cut in (slice(0, columns), slice(columns, 2 * columns))
    ]
    mixed = jnp.where(place < rows // 2, mixed[0], mixed[1])
    parts[...] = mixed.reshape(n_dp, rows, columns)
    copies = to_data(n_dp, lambda peer: parts.at[peer], got, sd2, rd2)
    got[me_d] = parts[me_d]
    finish(copies)
    total = got[0]
    for p in range(1, n_dp):
        total = total + got[p]
    own[...] = total
    copies = to_tensor(size, lambda peer: own, mod_out, st, rt)
    mod_out[me_t] = total
    finish(copies)


def mod_forward(n_dp, size, cond, w_mod):
    slots, width = cond.shape
    part, columns = w_mod.shape[1:]
    rows, lanes = 4 * slots, -(-part // 128) * 128
    laid = cond.astype(jnp.float32).reshape(slots, n_dp, part).transpose(1, 0, 2)
    laid = jnp.concatenate([laid, laid, laid, laid], 1)
    laid = jnp.pad(laid, ((0, 0), (0, 0), (0, lanes - part)))
    dma = pltpu.SemaphoreType.DMA
    return pl.pallas_call(
        partial(mod_kernel, n_dp, size),
        in_specs=[pl.BlockSpec(memory_space=pltpu.VMEM)] * 2,
        out_specs=[pl.BlockSpec(memory_space=pltpu.VMEM)] * 2,
        out_shape=[
            jax.ShapeDtypeStruct((size, rows, columns // 2), jnp.float32),
            jax.ShapeDtypeStruct((n_dp * rows, part), jnp.bfloat16),
        ],
        scratch_shapes=[
            pltpu.VMEM((n_dp, rows, lanes), jnp.float32),
            pltpu.VMEM((n_dp, rows, columns // 2), jnp.float32),
            pltpu.VMEM((n_dp, rows, columns // 2), jnp.float32),
            pltpu.VMEM((rows, columns // 2), jnp.float32),
            dma((n_dp - 1,)), dma((n_dp - 1,)), dma((n_dp - 1,)), dma((n_dp - 1,)),
            dma((size - 1,)), dma((size - 1,)),
        ],
        compiler_params=pltpu.CompilerParams(
            collective_id=0, has_side_effects=True, vmem_limit_bytes=40 << 20
        ),
        cost_estimate=pl.CostEstimate(flops=1 << 33, bytes_accessed=1 << 21, transcendentals=0),
    )(laid, w_mod)


def mod_back_kernel(n_dp, size, terms, lost, act, w, grad, cond_out, loss_out, halves, sums, every, cparts, cgot, cfull,
                    lhalves, lsums, levery, st1, rt1, sd1, rd1, sd2, rd2, st2, rt2, st3, rt3, sd3, rd3):
    me_d, me_t = lax.axis_index("dp"), lax.axis_index("tensor")
    rows, columns = terms.shape[1:]
    part = w.shape[1]
    greet(n_dp, size)
    copies = to_tensor(size, lambda peer: terms.at[peer], halves, st1, rt1)
    copies += to_tensor(size, lambda peer: lost, lhalves, st3, rt3)
    halves[me_t] = terms[me_t]
    lhalves[me_t] = lost[...]
    finish(copies)
    total, loss = halves[0], lhalves[0]
    for t in range(1, size):
        total, loss = total + halves[t], loss + lhalves[t]
    sums[...] = total
    lsums[...] = loss
    copies = to_data(n_dp, lambda peer: sums, every, sd1, rd1)
    copies += to_data(n_dp, lambda peer: lsums, levery, sd3, rd3)
    every[me_d] = total
    levery[me_d] = loss
    finish(copies)
    loss = levery[0]
    for p in range(1, n_dp):
        loss = loss + levery[p]
    loss_out[...] = loss
    dmod = every[...].reshape(n_dp * rows, columns).astype(jnp.bfloat16)
    place = lax.rem(lax.broadcasted_iota(jnp.int32, (n_dp * rows, 1), 0), rows)
    quarter = rows // 4
    cuts = (slice(0, columns), slice(columns, 2 * columns))
    back = [nt(dmod, w[s, :, cut]) for cut in cuts for s in range(2)]
    mixed = back[0]
    for n in range(1, 4):
        mixed = jnp.where(place < n * quarter, mixed, back[n])
    cparts[:, :, :part] = mixed.reshape(n_dp, rows, part)
    copies = to_data(n_dp, lambda peer: cparts.at[peer], cgot, sd2, rd2)
    cgot[me_d] = cparts[me_d]
    for n in range(4):
        mask = (place >= n * quarter) & (place < (n + 1) * quarter)
        picked = jnp.where(mask, act[...], jnp.zeros((), jnp.bfloat16))
        grad[n % 2, :, cuts[n // 2]] = tn(picked, dmod)
    finish(copies)
    copies = to_tensor(size, lambda peer: cgot, cfull, st2, rt2)
    cfull[me_t] = cgot[...]
    finish(copies)
    full = cfull[0]
    for t in range(1, size):
        full = full + cfull[t]
    cond_out[...] = full


def mod_backward(n_dp, size, terms, lost, act, w_mod):
    rows, columns = terms.shape[1:]
    part = w_mod.shape[1]
    lanes = -(-part // 128) * 128
    dma = pltpu.SemaphoreType.DMA
    f32 = jnp.float32
    return pl.pallas_call(
        partial(mod_back_kernel, n_dp, size),
        in_specs=[pl.BlockSpec(memory_space=pltpu.VMEM)] * 4,
        out_specs=[pl.BlockSpec(memory_space=pltpu.VMEM)] * 3,
        out_shape=[
            jax.ShapeDtypeStruct(w_mod.shape, f32),
            jax.ShapeDtypeStruct((n_dp, rows, lanes), f32),
            jax.ShapeDtypeStruct((8, 128), f32),
        ],
        scratch_shapes=[
            pltpu.VMEM((size, rows, columns), f32),
            pltpu.VMEM((rows, columns), f32),
            pltpu.VMEM((n_dp, rows, columns), f32),
            pltpu.VMEM((n_dp, rows, lanes), f32),
            pltpu.VMEM((n_dp, rows, lanes), f32),
            pltpu.VMEM((size, n_dp, rows, lanes), f32),
            pltpu.VMEM((size, 8, 128), f32),
            pltpu.VMEM((8, 128), f32),
            pltpu.VMEM((n_dp, 8, 128), f32),
            dma((size - 1,)), dma((size - 1,)),
            dma((n_dp - 1,)), dma((n_dp - 1,)), dma((n_dp - 1,)), dma((n_dp - 1,)),
            dma((size - 1,)), dma((size - 1,)),
            dma((size - 1,)), dma((size - 1,)), dma((n_dp - 1,)), dma((n_dp - 1,)),
        ],
        compiler_params=pltpu.CompilerParams(
            collective_id=1, has_side_effects=True, vmem_limit_bytes=40 << 20
        ),
        cost_estimate=pl.CostEstimate(flops=1 << 33, bytes_accessed=1 << 21, transcendentals=0),
    )(terms, lost, act, w_mod)


def on_device(
    data,
    group,
    image,
    text,
    cond,
    teacher_image,
    teacher_text,
    grad_image,
    grad_text,
    live,
    w_mod,
    w_qkv,
    w_out,
    w_up,
    w_down,
):
    slots, width = cond.shape
    rows_i, rows_t = image.shape[1], text.shape[1]
    pad_t = -(-rows_t // 8) * 8
    size = group.size
    n_dp = data.size
    heads = w_qkv.shape[2]
    odd = heads % 2

    wide = jnp.concatenate([w_qkv, w_out[:, None]], 1)
    f_wide = lax.all_gather(wide, "dp", axis=3, tiled=True)
    f_up = lax.all_gather(w_up, "dp", axis=1, tiled=True)
    f_down = lax.all_gather(w_down, "dp", axis=1, tiled=True)
    if odd:
        f_wide = jnp.pad(f_wide, ((0, 0), (0, 0), (0, odd), (0, 0), (0, 0)))
    f_wide = f_wide.reshape(2, 4, -1, width)
    f_qkv, f_out = f_wide[:, :3], f_wide[:, 3]

    mod_all, act_all = mod_forward(n_dp, size, cond, w_mod)
    mods = jnp.stack(
        [
            jnp.stack(
                [
                    jnp.stack([mod_all[:, (h * 2 + s) * slots + j] for h in range(2)], 1).reshape(6, width)
                    for s in range(2)
                ]
            )
            for j in range(slots)
        ]
    )

    is_image = (lax.broadcasted_iota(jnp.int32, (rows_i + pad_t, 1), 0) < rows_i)
    is_real = (lax.broadcasted_iota(jnp.int32, (rows_i + pad_t, 1), 0) < rows_i + rows_t)

    def merged(img, txt, j):
        return jnp.concatenate([img[j], jnp.pad(txt[j], ((0, pad_t - rows_t), (0, 0)))], 0)

    def pick(j, span):
        return jnp.where(is_image, mods[j, 1, span][None], mods[j, 0, span][None])

    def token_sums(values):
        return jnp.stack([jnp.sum(values[rows_i:], 0), jnp.sum(values[:rows_i], 0)])

    def spread(blocks):
        return (
            jnp.concatenate([b[:rows_i] for b in blocks], 0),
            jnp.concatenate([b[rows_i:] for b in blocks], 0),
        )

    half_i = size // 2 * rows_i

    def scatter_begin(rows_txt, rows_img, w, flip):
        top, own = halves(rows_txt, rows_img, w, flip)
        got = group.send(top, 1)
        blocks = []
        for k in range(size // 2):
            cuts = (slice(k * rows_i, (k + 1) * rows_i), slice(half_i + k * pad_t, half_i + (k + 1) * pad_t))
            blocks.append(jnp.concatenate([own[cut] + got[cut].astype(jnp.float32) for cut in cuts], 0))
        blocks = [blocks[0]] + [block.astype(jnp.bfloat16) for block in blocks[1:]]
        return blocks, [group.send(blocks[k], 2 * k) for k in range(1, size // 2)]

    def scatter_end(started, *others):
        blocks, got = started
        total = blocks[0]
        for value in got:
            total = total + after(value, *others).astype(jnp.float32)
        return total

    def gather_begin(own):
        return [own], [group.send(own, flip) for flip in group.evens[1:]]

    def gather_end(started, *others):
        own, got = started
        evens = own + [after(value, *others) for value in got]
        odds = group.send(jnp.concatenate(evens, 0), 1)
        return spread(evens + [odds[k : k + rows_i + pad_t] for k in range(0, odds.shape[0], rows_i + pad_t)])

    count = 3.0 * (n_dp // 2) * size * (rows_i + rows_t)

    slot = [dict() for j in range(slots)]
    for j, v in enumerate(slot):
        v["x"] = merged(image, text, j).astype(jnp.float32)
        v["hat1"], v["rstd1"] = norm_forward(v["x"])
        h1 = (v["hat1"] * (1.0 + pick(j, 1)) + pick(j, 0)).astype(jnp.bfloat16)
        v["go"] = gather_begin(h1)
    for j, v in enumerate(slot):
        v["h1_i"], v["h1_t"] = gather_end(v["go"], slot[-1]["go"][0])
    for j, v in enumerate(slot):
        if j:
            v["h1_i"] = after(v["h1_i"], slot[j - 1]["att_i"])
        v["qkv_t"], v["qkv_i"] = project_qkv(v["h1_t"], v["h1_i"], f_qkv)
        v["att_i"], v["att_t"], v["lse"] = attend(v["qkv_i"], v["qkv_t"], pad_t, rows_t)
    for j, v in enumerate(slot):
        v["go"] = scatter_begin(v["att_t"], v["att_i"], f_out, False)
    for j, v in enumerate(slot):
        v["y"] = scatter_end(v["go"], slot[-1]["go"][0])
        v["mid"] = v["x"] + pick(j, 2) * v["y"]
        v["hat2"], v["rstd2"] = norm_forward(v["mid"])
        h2 = (v["hat2"] * (1.0 + pick(j, 4)) + pick(j, 3)).astype(jnp.bfloat16)
        v["go"] = gather_begin(h2)
    for j, v in enumerate(slot):
        v["h2_i"], v["h2_t"] = gather_end(v["go"], slot[-1]["go"][0])
    for j, v in enumerate(slot):
        if j:
            v["h2_i"] = after(v["h2_i"], slot[j - 1]["hid_i"])
        v["hid_t"], v["hid_i"], v["slope_t"], v["slope_i"] = up_and_slope(v["h2_t"], v["h2_i"], f_up)
    f_down = after(f_down, slot[-1]["hid_i"])
    for j, v in enumerate(slot):
        v["go"] = scatter_begin(v["hid_t"], v["hid_i"], f_down, True)
    for j, v in enumerate(slot):
        v["m"] = scatter_end(v["go"], slot[-1]["go"][0])
        out = v["mid"] + pick(j, 5) * v["m"]
        mask = jnp.where(is_real, live[j].astype(jnp.float32), 0.0)
        err = mask * (out - merged(teacher_image, teacher_text, j).astype(jnp.float32))
        v["loss"] = jnp.sum(err * err)
        v["cot"] = mask * merged(grad_image, grad_text, j).astype(jnp.float32) + 2.0 * err
        v["dgate2"] = token_sums(v["cot"] * v["m"])
        dm = (v["cot"] * pick(j, 5)).astype(jnp.bfloat16)
        v["go"] = gather_begin(dm)
    for j, v in enumerate(slot):
        v["dm_i"], v["dm_t"] = gather_end(v["go"], slot[-1]["go"][0])

    here = lax.axis_index("dp")

    both = lambda a, b, *ranks: outer(*([v[name + e] for v in slot] for name in (a, b) for e in ("_t", "_i")), *ranks)

    def reduced(grads):
        return lax.psum_scatter(grads.reshape(2, -1, grads.shape[-1]), "dp", scatter_dimension=1, tiled=True)

    g_down = both("dm", "hid")
    done_down = reduced(g_down)
    for j, v in enumerate(slot):
        v["dm_i"] = after(v["dm_i"], g_down if j == 0 else slot[j - 1]["dpre_i"])
        v["dpre_t"], v["dpre_i"] = scaled(v["dm_t"], v["dm_i"], f_down, v["slope_t"], v["slope_i"])
        v["go"] = scatter_begin(v["dpre_t"], v["dpre_i"], f_up, True)
    g_up = both("h2", "dpre")
    done_up = reduced(g_up)
    for j, v in enumerate(slot):
        v["dh2"] = scatter_end(v["go"], g_up)
        v["dshift2"] = token_sums(v["dh2"])
        v["dscale2"] = token_sums(v["dh2"] * v["hat2"])
        v["dmid"] = v["cot"] + norm_backward(v["dh2"] * (1.0 + pick(j, 4)), v["hat2"], v["rstd2"])
        v["dgate1"] = token_sums(v["dmid"] * v["y"])
        dy = (v["dmid"] * pick(j, 2)).astype(jnp.bfloat16)
        v["go"] = gather_begin(dy)
    for j, v in enumerate(slot):
        v["dy_i"], v["dy_t"] = gather_end(v["go"], slot[-1]["go"][0])
    g_out = both("att", "dy", n_dp)
    done_out = reduced(g_out)
    for j, v in enumerate(slot):
        v["dy_i"] = after(v["dy_i"], g_out, done_down) if j == 0 else after(v["dy_i"], slot[j - 1]["dqkv_i"])
        g_t, g_i = plain(v["dy_t"], v["dy_i"], f_out)
        v["dqkv_i"], v["dqkv_t"] = attend_back(v["qkv_i"], v["qkv_t"], g_i, g_t, v["lse"], pad_t, rows_t)
    g_qkv = both("dqkv", "h1", n_dp)
    done_qkv = reduced(g_qkv)
    for j, v in enumerate(slot):
        v["dqkv_i"] = after(v["dqkv_i"], g_qkv)
        v["go"] = scatter_begin(v["dqkv_t"], v["dqkv_i"], f_qkv, False)
    for j, v in enumerate(slot):
        v["dh1"] = scatter_end(v["go"], slot[-1]["go"][0])
    grad_i, grad_t, terms = [], [], []
    for j in range(slots):
        v = slot[j]
        dshift1 = token_sums(v["dh1"])
        dscale1 = token_sums(v["dh1"] * v["hat1"])
        back = v["dmid"] + norm_backward(v["dh1"] * (1.0 + pick(j, 1)), v["hat1"], v["rstd1"])
        grad_i.append(back[:rows_i])
        grad_t.append(back[rows_i : rows_i + rows_t])
        terms.append(
            jnp.stack([dshift1, dscale1, v["dgate1"], v["dshift2"], v["dscale2"], v["dgate2"]], 1)
        )
    lost = jnp.full((8, 128), sum(v["loss"] for v in slot))
    laid = jnp.stack(terms, 1).reshape(2 * slots, size, 2, -1).transpose(1, 2, 0, 3)
    laid = laid.reshape(size, 4 * slots, -1)
    laid = after(laid, done_up)
    done_mod, cond_rows, loss_rows = mod_backward(n_dp, size, laid, lost, act_all, w_mod)
    loss = loss_rows[0, 0] / (count * width)
    cond_rows = cond_rows[:, :, : w_mod.shape[1]]
    cond_total = jnp.sum(cond_rows.reshape(n_dp, 4, slots, -1), 1).transpose(1, 0, 2).reshape(slots, width)
    unused_value, silu_pull = jax.vjp(jax.nn.silu, cond.astype(jnp.float32))
    grad_cond = silu_pull(cond_total)[0]
    done_down = done_down.astype(jnp.float32)
    done_up = done_up.astype(jnp.float32)
    done_out = done_out.astype(jnp.float32).reshape(2, heads + odd, -1, width)
    done_qkv = done_qkv.astype(jnp.float32).reshape(2, 3, heads + odd, -1, width)
    if odd:
        done_qkv, done_out = done_qkv[:, :, :heads], done_out[:, :heads]
    return (
        loss,
        done_mod,
        done_qkv,
        done_out,
        done_up,
        done_down,
        jnp.stack(grad_i),
        jnp.stack(grad_t),
        grad_cond,
    )


def solution(mesh):
    return jax.shard_map(
        partial(on_device, Data(mesh.shape["dp"]), Group(mesh.shape["tensor"])),
        mesh=mesh,
        in_specs=(
            P("dp", "tensor", None),
            P("dp", "tensor", None),
            P("dp", None),
            P("dp", "tensor", None),
            P("dp", "tensor", None),
            P("dp", "tensor", None),
            P("dp", "tensor", None),
            P("dp"),
            P(None, "dp", "tensor"),
            P(None, None, "tensor", "dp", None),
            P(None, "tensor", "dp", None),
            P(None, "dp", "tensor"),
            P(None, "dp", "tensor"),
        ),
        out_specs=(
            P(),
            P(None, "dp", "tensor"),
            P(None, None, "tensor", "dp", None),
            P(None, "tensor", "dp", None),
            P(None, "dp", "tensor"),
            P(None, "dp", "tensor"),
            P("dp", "tensor", None),
            P("dp", "tensor", None),
            P("dp", None),
        ),
        check_vma=False,
    )
```

time: 2040 us -> 1190 us (0.58)
  Pallas kernels: 797 us -> 353 us
  matrix products: 227 us -> 0 us
  waiting for transfers between devices: 701 us -> 572 us
  starting transfers between devices: 113 us -> 21.9 us
  other arithmetic: 68.8 us -> 98.7 us
    ppermute x44 -> x0, waiting for transfers between devices: 494 us -> none  [send(): return lax.ppermute(value, 'dp', [(p, p ^ flip) for p in range(self.size)])]
    pallas_call x2 -> x46, Pallas kernels: 574 us -> 181 us  [the longest x14 108 us: over_columns(): pl.pallas_call(kernel, grid=(columns // step,), in_specs=[whole(v) for v...]
    dot_general x64 -> x0, matrix products: 227 us -> none  [the longest x24 79.5 us: nn(): return jnp.dot(a, b, preferred_element_type=jnp.float32)]
    reduce_scatter x0 -> x4, waiting for transfers between devices: none -> 169 us  [reduced(): lax.psum_scatter(grads.reshape(2, -1, grads.shape[-1]), 'dp', scatter_dim...]
    all_gather x0 -> x3, waiting for transfers between devices: none -> 109 us  [the longest x1 56.9 us: on_device(): f_down = lax.all_gather(w_down, 'dp', axis=1, tiled=True)]
    ppermute x44 -> x0, starting transfers between devices: 95 us -> none  [send(): return lax.ppermute(value, 'dp', [(p, p ^ flip) for p in range(self.size)])]
    ppermute x48 -> x32, waiting for transfers between devices: 206 us -> 293 us  [send(): lax.ppermute(value, 'tensor', [(t, t ^ flip) for t in range(self.size)])]
    pallas_call x1, Pallas kernels: 57.6 us -> 22.6 us  [mod_forward(): pl.pallas_call(partial(mod_kernel, n_dp, size), in_specs=[pl.BlockSpec(me...]
  transfers between devices with their start and end apart: 92 -> 39, of which waited for: 36 -> 25; matrix products, arithmetic and copies ran while one was open for 13% -> 10% of each run, Pallas kernels for 37% -> 25%
where the time goes in v3:
time: 1190 us; the launch traced here: 1180 us
  waiting for transfers between devices  572 us (48%)
  Pallas kernels  353 us (30%)
  local copies, waits for them, and re-layouts  112 us (9%)
  other arithmetic  98.7 us (8%)
  between operations  22.1 us (2%)
  starting transfers between devices  21.9 us (2%)
    ppermute x32, waiting for transfers between devices, send(): lax.ppermute(value, 'tensor', [(t, t ^ flip) for t in range(self.size)])  293 us
    reduce_scatter x4, waiting for transfers between devices, reduced(): lax.psum_scatter(grads.reshape(2, -1, grads.shape[-1]), 'dp', scatter_dim...  169 us
    pallas_call x14, Pallas kernels, over_columns(): pl.pallas_call(kernel, grid=(columns // step,), in_specs=[whole(v) for v...  108 us
    unnamed x430, local copies, waits for them, and re-layouts  80.2 us
    pallas_call x2, Pallas kernels, attend_back(): pl.pallas_call(partial(back_kernel, block, valid), grid=(pairs,), in_spec...  62 us
    pallas_call x4, Pallas kernels, outer(): pl.pallas_call(partial(outer_kernel, n), grid=(steps,), in_specs=[l_spec(...  58.9 us
    all_gather x1, waiting for transfers between devices, on_device(): f_down = lax.all_gather(w_down, 'dp', axis=1, tiled=True)  56.9 us
    pallas_call x2, Pallas kernels, attend(): pl.pallas_call(partial(attend_kernel, block, valid), grid=(pairs,), in_sp...  52.7 us
  transfers between devices with their start and end apart: 39, of which 25 were waited for; matrix products, arithmetic and copies ran while one was open for 10% of the time, Pallas kernels for 25%

profile of v3, /device:TPU:0, one launch (start us, length us, event | category | flops | bytes accessed | tf_op | source)
XLA Modules:
  0.0 1179.7 jit_solution(12263325725065199111)
XLA Ops:
  11.1 22.6 %shard_map.196 = (f32[4,8,1152]{2,1,0:T(8,128)S(1)}, bf16[64,192]{1,0:T(8,128)(2,1)S(1)}) custom-call(f32[8,8,256]{2,1,0:T(8,128)S(1)} %select_maximum_fusion.cond, bf16[2,192,2304]{2,1,0:T(8,128)(2,1)S(1)} %copy-done.62), custom_call_target="tpu_custom_call" | custom-call | flops 8589934592 | bytes 2097152 | tf_op jit(solution)/shard_map/pallas_call | solution.py:483
  42.2 22.3 %collective-permute-done.4.refs_0_ = bf16[296,1536]{1,0:T(8,128)(2,1)S(1)} collective-permute-done((bf16[296,1536]{1,0:T(8,128)(2,1)S(1)}, bf16[296,1536]{1,0:T(8,128)(2,1)S(1)}, u32[]{:S(2)}, u32[]{:S(2)}) %collective-permute-start.4) | collective-permute-done | bytes 909344 | tf_op jit(solution)/shard_map/ppermute | solution.py:345
  66.2 22.2 %collective-permute-done.refs_0_ = bf16[296,1536]{1,0:T(8,128)(2,1)S(1)} collective-permute-done((bf16[296,1536]{1,0:T(8,128)(2,1)S(1)}, bf16[296,1536]{1,0:T(8,128)(2,1)S(1)}, u32[]{:S(2)}, u32[]{:S(2)}) %collective-permute-start) | collective-permute-done | bytes 909344 | tf_op jit(solution)/shard_map/ppermute | solution.py:345
  101.3 52.3 %all-gather.4.cloned.1.call-done = bf16[2,4,6,64,1536]{4,3,2,1,0:T(8,128)(2,1)} async-done(((bf16[2,4,6,8,1536]{4,3,2,1,0:T(8,128)(2,1)}), bf16[2,4,6,64,1536]{4,3,2,1,0:T(8,128)(2,1)}) %all-gather.4.cloned.1.call-update) | async-done | bytes 9437200 | tf_op jit(solution)/shard_map/all_gather | solution.py:619
  164.5 26.2 %shard_map.199 = (bf16[1024,384]{1,0:T(8,128)(2,1)S(1)}, bf16[160,384]{1,0:T(8,128)(2,1)S(1)}, f32[3,2,1184]{2,1,0:T(2,128)S(1)}) custom-call(bf16[3,1024,384]{2,1,0:T(8,128)(2,1)S(1)} %get-tuple-element.61.qi.ki.vi, bf16[3,1024,384]{2,1,0:T(8,128)(2,1)S(1)} %get-tuple-element.61.qi.ki.vi, bf16[3,1024,384]{2,1,0:T(8,128)(2,1)S(1)} %get-tuple-element.61.qi.ki.vi, ...), custom_call_target="tpu_custom_call" | custom-call | flops 17179869184 | bytes 8388608 | tf_op jit(solution)/shard_map/pallas_call | solution.py:123
  199.1 26.4 %shard_map.204 = (bf16[1024,384]{1,0:T(8,128)(2,1)S(1)}, bf16[160,384]{1,0:T(8,128)(2,1)S(1)}, f32[3,2,1184]{2,1,0:T(2,128)S(1)}) custom-call(bf16[3,1024,384]{2,1,0:T(8,128)(2,1)S(1)} %get-tuple-element.67.qi.ki.vi, bf16[3,1024,384]{2,1,0:T(8,128)(2,1)S(1)} %get-tuple-element.67.qi.ki.vi, bf16[3,1024,384]{2,1,0:T(8,128)(2,1)S(1)} %get-tuple-element.67.qi.ki.vi, ...), custom_call_target="tpu_custom_call" | custom-call | flops 17179869184 | bytes 8388608 | tf_op jit(solution)/shard_map/pallas_call | solution.py:123
  239.9 18.3 %collective-permute-done.8.refs_0_ = bf16[296,1536]{1,0:T(8,128)(2,1)S(1)} collective-permute-done((bf16[296,1536]{1,0:T(8,128)(2,1)S(1)}, bf16[296,1536]{1,0:T(8,128)(2,1)S(1)}, u32[]{:S(2)}, u32[]{:S(2)}) %collective-permute-start.8) | collective-permute-done | bytes 909344 | tf_op jit(solution)/shard_map/ppermute | solution.py:345
  258.2 18.7 %collective-permute-done.3.refs_0_ = bf16[296,1536]{1,0:T(8,128)(2,1)S(1)} collective-permute-done((bf16[296,1536]{1,0:T(8,128)(2,1)S(1)}, bf16[296,1536]{1,0:T(8,128)(2,1)S(1)}, u32[]{:S(2)}, u32[]{:S(2)}) %collective-permute-start.3) | collective-permute-done | bytes 909344 | tf_op jit(solution)/shard_map/ppermute | solution.py:345
  285.0 21.1 %collective-permute-done.7.refs_0_ = bf16[296,1536]{1,0:T(8,128)(2,1)S(1)} collective-permute-done((bf16[296,1536]{1,0:T(8,128)(2,1)S(1)}, bf16[296,1536]{1,0:T(8,128)(2,1)S(1)}, u32[]{:S(2)}, u32[]{:S(2)}) %collective-permute-start.7) | collective-permute-done | bytes 909344 | tf_op jit(solution)/shard_map/ppermute | solution.py:345
  373.6 56.9 %all-gather.8.cloned.1.call-done.refs_0_ = bf16[2,1536,1536]{2,1,0:T(8,128)(2,1)} async-done(((bf16[2,192,1536]{2,1,0:T(8,128)(2,1)}), bf16[2,1536,1536]{2,1,0:T(8,128)(2,1)}) %all-gather.8.cloned.1.call-update) | async-done | bytes 9437200 | tf_op jit(solution)/shard_map/all_gather | solution.py:621
  467.0 18.6 %collective-permute-done.16.refs_0_ = bf16[296,1536]{1,0:T(8,128)(2,1)S(1)} collective-permute-done((bf16[296,1536]{1,0:T(8,128)(2,1)S(1)}, bf16[296,1536]{1,0:T(8,128)(2,1)S(1)}, u32[]{:S(2)}, u32[]{:S(2)}) %collective-permute-start.16) | collective-permute-done | bytes 909344 | tf_op jit(solution)/shard_map/ppermute | solution.py:345
  485.6 18.5 %collective-permute-done.13.refs_0_ = bf16[296,1536]{1,0:T(8,128)(2,1)S(1)} collective-permute-done((bf16[296,1536]{1,0:T(8,128)(2,1)S(1)}, bf16[296,1536]{1,0:T(8,128)(2,1)S(1)}, u32[]{:S(2)}, u32[]{:S(2)}) %collective-permute-start.13) | collective-permute-done | bytes 909344 | tf_op jit(solution)/shard_map/ppermute | solution.py:345
  512.9 19.7 %collective-permute-done.18.refs_0_ = bf16[296,1536]{1,0:T(8,128)(2,1)S(1)} collective-permute-done((bf16[296,1536]{1,0:T(8,128)(2,1)S(1)}, bf16[296,1536]{1,0:T(8,128)(2,1)S(1)}, u32[]{:S(2)}, u32[]{:S(2)}) %collective-permute-start.18) | collective-permute-done | bytes 909344 | tf_op jit(solution)/shard_map/ppermute | solution.py:345
  537.1 21.1 %collective-permute-done.15.refs_0_ = bf16[296,1536]{1,0:T(8,128)(2,1)S(1)} collective-permute-done((bf16[296,1536]{1,0:T(8,128)(2,1)S(1)}, bf16[296,1536]{1,0:T(8,128)(2,1)S(1)}, u32[]{:S(2)}, u32[]{:S(2)}) %collective-permute-start.15) | collective-permute-done | bytes 909344 | tf_op jit(solution)/shard_map/ppermute | solution.py:345
  564.2 18.3 %shard_map.220.refs_1_ = bf16[2,1536,1536]{2,1,0:T(8,128)(2,1)} custom-call(bf16[160,1536]{1,0:T(8,128)(2,1)S(1)} %pad_maximum_fusion.33.refs_0_.at, bf16[160,1536]{1,0:T(8,128)(2,1)S(1)} %pad_maximum_fusion.34.refs_1_.at, bf16[1024,1536]{1,0:T(8,128)(2,1)} %pad_maximum_fusion.4.refs_2_.refs_0_, bf16[1024,1536]{1,0:T(8,128)(2,1)} %pad_maximum_fusion.5.refs_3_.refs_0_, ...), custom_call_target="tpu_custom_call" | custom-call | flops 17179869184 | bytes 16777216 | tf_op jit(solution)/shard_map/pallas_call | solution.py:321
  646.8 18.2 %shard_map.226.refs_1_ = bf16[2,1536,1536]{2,1,0:T(8,128)(2,1)} custom-call(bf16[160,1536]{1,0:T(8,128)(2,1)S(1)} %copy-done.50, bf16[160,1536]{1,0:T(8,128)(2,1)S(1)} %copy-done.52, bf16[1024,1536]{1,0:T(8,128)(2,1)} %pad_maximum_fusion.2.ai.refs_2_, bf16[1024,1536]{1,0:T(8,128)(2,1)} %copy-done.9, bf16[160,1536]{1,0:T(8,128)(2,1)S(1)} %copy-done.78, ...), custom_call_target="tpu_custom_call" | custom-call | flops 17179869184 | bytes 16777216 | tf_op jit(solution)/shard_map/pallas_call | solution.py:321
  702.9 21.1 %collective-permute-done.26.refs_0_ = bf16[296,1536]{1,0:T(8,128)(2,1)S(1)} collective-permute-done((bf16[296,1536]{1,0:T(8,128)(2,1)S(1)}, bf16[296,1536]{1,0:T(8,128)(2,1)S(1)}, u32[]{:S(2)}, u32[]{:S(2)}) %collective-permute-start.26) | collective-permute-done | bytes 909344 | tf_op jit(solution)/shard_map/ppermute | solution.py:345
  768.6 18.1 %reduce-scatter.5.cloned.1.call-done.refs_2_ = bf16[2,192,1536]{2,1,0:T(8,128)(2,1)} async-done(((bf16[2,1536,1536]{2,1,0:T(8,128)(2,1)}), bf16[2,192,1536]{2,1,0:T(8,128)(2,1)}) %reduce-scatter.5.cloned.1.call-update) | async-done | bytes 1179664 | tf_op jit(solution)/shard_map/reduce_scatter | solution.py:736
  793.5 30.9 %shard_map.235 = (bf16[3,1024,384]{2,1,0:T(8,128)(2,1)S(1)}, bf16[3,160,384]{2,1,0:T(8,128)(2,1)S(1)}) custom-call(bf16[3,1024,384]{2,1,0:T(8,128)(2,1)S(1)} %copy-done.75, bf16[3,1024,384]{2,1,0:T(8,128)(2,1)S(1)} %copy-done.75, bf16[3,1024,384]{2,1,0:T(8,128)(2,1)S(1)} %copy-done.75, bf16[3,160,384]{2,1,0:T(8,128)(2,1)S(1)} %copy-done.89, ...), custom_call_target="tpu_custom_call" | custom-call | flops 34359738368 | bytes 16777216 | tf_op jit(solution)/shard_map/pallas_call | solution.py:142
  828.1 31.1 %shard_map.238 = (bf16[3,1024,384]{2,1,0:T(8,128)(2,1)S(1)}, bf16[3,160,384]{2,1,0:T(8,128)(2,1)S(1)}) custom-call(bf16[3,1024,384]{2,1,0:T(8,128)(2,1)S(1)} %copy-done.73, bf16[3,1024,384]{2,1,0:T(8,128)(2,1)S(1)} %copy-done.73, bf16[3,1024,384]{2,1,0:T(8,128)(2,1)S(1)} %copy-done.73, bf16[3,160,384]{2,1,0:T(8,128)(2,1)S(1)} %copy-done.87, ...), custom_call_target="tpu_custom_call" | custom-call | flops 34359738368 | bytes 16777216 | tf_op jit(solution)/shard_map/pallas_call | solution.py:142
  917.2 34.3 %collective-permute-done.31.refs_0_ = bf16[296,1536]{1,0:T(8,128)(2,1)} collective-permute-done((bf16[296,1536]{1,0:T(8,128)(2,1)S(1)}, bf16[296,1536]{1,0:T(8,128)(2,1)}, u32[]{:S(2)}, u32[]{:S(2)}) %collective-permute-start.31) | collective-permute-done | bytes 909344 | tf_op jit(solution)/shard_map/ppermute | solution.py:345
  965.9 59.0 %reduce-scatter.7.cloned.1.call-done.refs_1_ = bf16[2,192,1536]{2,1,0:T(8,128)(2,1)} async-done(((bf16[2,1536,1536]{2,1,0:T(8,128)(2,1)}), bf16[2,192,1536]{2,1,0:T(8,128)(2,1)}) %reduce-scatter.7.cloned.1.call-update) | async-done | bytes 1179664 | tf_op jit(solution)/shard_map/reduce_scatter | solution.py:736
  1031.2 34.5 %shard_map.247 = (f32[2,192,2304]{2,1,0:T(8,128)S(1)}, f32[8,8,256]{2,1,0:T(8,128)S(1)}, f32[8,128]{1,0:T(8,128)S(1)}) custom-call(f32[4,8,1152]{2,1,0:T(8,128)S(1)} %copy-done.44, f32[8,128]{1,0:T(8,128)S(1)} %broadcast_in_dim.396.lost, bf16[64,192]{1,0:T(8,128)(2,1)S(1)} %copy-done.95, bf16[2,192,2304]{2,1,0:T(8,128)(2,1)S(1)} %copy-done.63), custom_call_target="tpu_custom_call" | custom-call | flops 8589934592 | bytes 2097152 | tf_op jit(solution)/shard_map/pallas_call | solution.py:562
  1075.6 91.6 %reduce-scatter.9.cloned.1.call-done = bf16[2,144,1536]{2,1,0:T(8,128)(2,1)} async-done(((bf16[2,1152,1536]{2,1,0:T(8,128)(2,1)}), bf16[2,144,1536]{2,1,0:T(8,128)(2,1)}) %reduce-scatter.9.cloned.1.call-update) | async-done | bytes 884752 | tf_op jit(solution)/shard_map/reduce_scatter | solution.py:736
  (804 shorter events, 435.8 us)
Async XLA Ops:
  7.2 146.4 %all-gather.4.cloned.1.call-start = ((), (), s32[]{:S(2)}) async-start(), calls=%async_computation.4 | async-start | bytes 10616832 | tf_op jit(solution)/shard_map/all_gather | solution.py:619
  9.6 323.1 %all-gather.6.cloned.1.call-start = ((), (), s32[]{:S(2)}) async-start(), calls=%async_computation.5 | async-start | bytes 10616832 | tf_op jit(solution)/shard_map/all_gather | solution.py:620
  10.4 420.1 %all-gather.8.cloned.1.call-start = ((), (), s32[]{:S(2)}) async-start(), calls=%async_computation.6 | async-start | bytes 10616832 | tf_op jit(solution)/shard_map/all_gather | solution.py:621
  41.7 22.7 %collective-permute-start.4 = (bf16[296,1536]{1,0:T(8,128)(2,1)S(1)}, bf16[296,1536]{1,0:T(8,128)(2,1)S(1)}, u32[]{:S(2)}, u32[]{:S(2)}) collective-permute-start(bf16[296,1536]{1,0:T(8,128)(2,1)S(1)} %get-tuple-element.303.refs_1_), channel_id=1, source_target_pairs={{0,2},{1,3},{2,0},{3,1},{4,6},{5,7},{6,4},{7,5},{8,10},{9,11},{10,... | collective-permute-start | bytes 2727944 | tf_op jit(solution)/shard_map/ppermute | solution.py:345
  65.8 26.8 %collective-permute-start.5 = (bf16[592,1536]{1,0:T(8,128)(2,1)}, bf16[592,1536]{1,0:T(8,128)(2,1)}, u32[]{:S(2)}, u32[]{:S(2)}) collective-permute-start(bf16[592,1536]{1,0:T(8,128)(2,1)} %pad_maximum_fusion.10), channel_id=1, source_target_pairs={{0,1},{1,0},{2,3},{3,2},{4,5},{5,4},{6,7},{7,6},{8,9},{9,8},{10,11... | collective-permute-start | bytes 5455880 | tf_op jit(solution)/shard_map/ppermute | solution.py:345
  65.8 22.6 %collective-permute-start = (bf16[296,1536]{1,0:T(8,128)(2,1)S(1)}, bf16[296,1536]{1,0:T(8,128)(2,1)S(1)}, u32[]{:S(2)}, u32[]{:S(2)}) collective-permute-start(bf16[296,1536]{1,0:T(8,128)(2,1)S(1)} %get-tuple-element.304), channel_id=1, source_target_pairs={{0,2},{1,3},{2,0},{3,1},{4,6},{5,7},{6,4},{7,5},{8,10},{9,11},{10,... | collective-permute-start | bytes 2727944 | tf_op jit(solution)/shard_map/ppermute | solution.py:345
  89.8 696.9 %reduce-scatter.5.cloned.1.call-start = ((), (), s32[]{:S(2)}) async-start(), calls=%async_computation.7 | async-start | bytes 10616832 | tf_op jit(solution)/shard_map/reduce_scatter | solution.py:736
  235.1 23.1 %collective-permute-start.8 = (bf16[296,1536]{1,0:T(8,128)(2,1)S(1)}, bf16[296,1536]{1,0:T(8,128)(2,1)S(1)}, u32[]{:S(2)}, u32[]{:S(2)}) collective-permute-start(bf16[296,1536]{1,0:T(8,128)(2,1)S(1)} %pad_maximum_fusion.22.refs_2_), channel_id=1, source_target_pairs={{0,2},{1,3},{2,0},{3,1},{4,6},{5,7},{6,4},{7,5},{8,10},{9,11},{10,... | collective-permute-start | bytes 2727944 | tf_op jit(solution)/shard_map/ppermute | solution.py:345
  238.2 38.7 %collective-permute-start.3 = (bf16[296,1536]{1,0:T(8,128)(2,1)S(1)}, bf16[296,1536]{1,0:T(8,128)(2,1)S(1)}, u32[]{:S(2)}, u32[]{:S(2)}) collective-permute-start(bf16[296,1536]{1,0:T(8,128)(2,1)S(1)} %pad_maximum_fusion.21), channel_id=1, source_target_pairs={{0,2},{1,3},{2,0},{3,1},{4,6},{5,7},{6,4},{7,5},{8,10},{9,11},{10,... | collective-permute-start | bytes 2727944 | tf_op jit(solution)/shard_map/ppermute | solution.py:345
  282.9 23.2 %collective-permute-start.7 = (bf16[296,1536]{1,0:T(8,128)(2,1)S(1)}, bf16[296,1536]{1,0:T(8,128)(2,1)S(1)}, u32[]{:S(2)}, u32[]{:S(2)}) collective-permute-start(bf16[296,1536]{1,0:T(8,128)(2,1)S(1)} %get-tuple-element.300), channel_id=1, source_target_pairs={{0,2},{1,3},{2,0},{3,1},{4,6},{5,7},{6,4},{7,5},{8,10},{9,11},{10,... | collective-permute-start | bytes 2727944 | tf_op jit(solution)/shard_map/ppermute | solution.py:345
  284.5 39.5 %collective-permute-start.10 = (bf16[296,1536]{1,0:T(8,128)(2,1)S(1)}, bf16[296,1536]{1,0:T(8,128)(2,1)S(1)}, u32[]{:S(2)}, u32[]{:S(2)}) collective-permute-start(bf16[296,1536]{1,0:T(8,128)(2,1)S(1)} %get-tuple-element.299.refs_1_), channel_id=1, source_target_pairs={{0,2},{1,3},{2,0},{3,1},{4,6},{5,7},{6,4},{7,5},{8,10},{9,11},{10,... | collective-permute-start | bytes 2727944 | tf_op jit(solution)/shard_map/ppermute | solution.py:345
  462.5 23.1 %collective-permute-start.16 = (bf16[296,1536]{1,0:T(8,128)(2,1)S(1)}, bf16[296,1536]{1,0:T(8,128)(2,1)S(1)}, u32[]{:S(2)}, u32[]{:S(2)}) collective-permute-start(bf16[296,1536]{1,0:T(8,128)(2,1)S(1)} %pad_maximum_fusion.24.refs_2_), channel_id=1, source_target_pairs={{0,2},{1,3},{2,0},{3,1},{4,6},{5,7},{6,4},{7,5},{8,10},{9,11},{10,... | collective-permute-start | bytes 2727944 | tf_op jit(solution)/shard_map/ppermute | solution.py:345
  465.2 38.9 %collective-permute-start.13 = (bf16[296,1536]{1,0:T(8,128)(2,1)S(1)}, bf16[296,1536]{1,0:T(8,128)(2,1)S(1)}, u32[]{:S(2)}, u32[]{:S(2)}) collective-permute-start(bf16[296,1536]{1,0:T(8,128)(2,1)S(1)} %pad_maximum_fusion.23), channel_id=1, source_target_pairs={{0,2},{1,3},{2,0},{3,1},{4,6},{5,7},{6,4},{7,5},{8,10},{9,11},{10,... | collective-permute-start | bytes 2727944 | tf_op jit(solution)/shard_map/ppermute | solution.py:345
  532.8 25.9 %collective-permute-start.19 = (bf16[592,1536]{1,0:T(8,128)(2,1)S(1)}, bf16[592,1536]{1,0:T(8,128)(2,1)S(1)}, u32[]{:S(2)}, u32[]{:S(2)}) collective-permute-start(bf16[592,1536]{1,0:T(8,128)(2,1)S(1)} %pad_maximum_fusion.16), channel_id=1, source_target_pairs={{0,1},{1,0},{2,3},{3,2},{4,5},{5,4},{6,7},{7,6},{8,9},{9,8},{10,11... | collective-permute-start | bytes 5455880 | tf_op jit(solution)/shard_map/ppermute | solution.py:345
  535.6 22.6 %collective-permute-start.15 = (bf16[296,1536]{1,0:T(8,128)(2,1)S(1)}, bf16[296,1536]{1,0:T(8,128)(2,1)S(1)}, u32[]{:S(2)}, u32[]{:S(2)}) collective-permute-start(bf16[296,1536]{1,0:T(8,128)(2,1)S(1)} %get-tuple-element.238), channel_id=1, source_target_pairs={{0,2},{1,3},{2,0},{3,1},{4,6},{5,7},{6,4},{7,5},{8,10},{9,11},{10,... | collective-permute-start | bytes 2727944 | tf_op jit(solution)/shard_map/ppermute | solution.py:345
  624.8 288.6 %reduce-scatter.11.cloned.1.call-start = ((), (), s32[]{:S(2)}) async-start(), calls=%async_computation.10 | async-start | bytes 2654208 | tf_op jit(solution)/shard_map/reduce_scatter | solution.py:736
  642.0 23.2 %collective-permute-start.24 = (bf16[296,1536]{1,0:T(8,128)(2,1)}, bf16[296,1536]{1,0:T(8,128)(2,1)S(1)}, u32[]{:S(2)}, u32[]{:S(2)}) collective-permute-start(bf16[296,1536]{1,0:T(8,128)(2,1)} %pad_maximum_fusion.26), channel_id=1, source_target_pairs={{0,2},{1,3},{2,0},{3,1},{4,6},{5,7},{6,4},{7,5},{8,10},{9,11},{10,... | collective-permute-start | bytes 2727944 | tf_op jit(solution)/shard_map/ppermute | solution.py:345
  646.2 38.0 %collective-permute-start.21 = (bf16[296,1536]{1,0:T(8,128)(2,1)}, bf16[296,1536]{1,0:T(8,128)(2,1)S(1)}, u32[]{:S(2)}, u32[]{:S(2)}) collective-permute-start(bf16[296,1536]{1,0:T(8,128)(2,1)} %pad_maximum_fusion.25), channel_id=1, source_target_pairs={{0,2},{1,3},{2,0},{3,1},{4,6},{5,7},{6,4},{7,5},{8,10},{9,11},{10,... | collective-permute-start | bytes 2727944 | tf_op jit(solution)/shard_map/ppermute | solution.py:345
  700.8 23.2 %collective-permute-start.26 = (bf16[296,1536]{1,0:T(8,128)(2,1)S(1)}, bf16[296,1536]{1,0:T(8,128)(2,1)S(1)}, u32[]{:S(2)}, u32[]{:S(2)}) collective-permute-start(bf16[296,1536]{1,0:T(8,128)(2,1)S(1)} %get-tuple-element.293.refs_1_), channel_id=1, source_target_pairs={{0,2},{1,3},{2,0},{3,1},{4,6},{5,7},{6,4},{7,5},{8,10},{9,11},{10,... | collective-permute-start | bytes 2727944 | tf_op jit(solution)/shard_map/ppermute | solution.py:345
  702.3 39.8 %collective-permute-start.22 = (bf16[296,1536]{1,0:T(8,128)(2,1)S(1)}, bf16[296,1536]{1,0:T(8,128)(2,1)S(1)}, u32[]{:S(2)}, u32[]{:S(2)}) collective-permute-start(bf16[296,1536]{1,0:T(8,128)(2,1)S(1)} %get-tuple-element.294), channel_id=1, source_target_pairs={{0,2},{1,3},{2,0},{3,1},{4,6},{5,7},{6,4},{7,5},{8,10},{9,11},{10,... | collective-permute-start | bytes 2727944 | tf_op jit(solution)/shard_map/ppermute | solution.py:345
  758.2 266.6 %reduce-scatter.7.cloned.1.call-start = ((), (), s32[]{:S(2)}) async-start(), calls=%async_computation.8 | async-start | bytes 10616832 | tf_op jit(solution)/shard_map/reduce_scatter | solution.py:736
  758.8 408.3 %reduce-scatter.9.cloned.1.call-start = ((), (), s32[]{:S(2)}) async-start(), calls=%async_computation.9 | async-start | bytes 7962624 | tf_op jit(solution)/shard_map/reduce_scatter | solution.py:736
  909.6 42.0 %collective-permute-start.29 = (bf16[296,1536]{1,0:T(8,128)(2,1)}, bf16[296,1536]{1,0:T(8,128)(2,1)S(1)}, u32[]{:S(2)}, u32[]{:S(2)}) collective-permute-start(bf16[296,1536]{1,0:T(8,128)(2,1)} %pad_maximum_fusion.27), channel_id=1, source_target_pairs={{0,2},{1,3},{2,0},{3,1},{4,6},{5,7},{6,4},{7,5},{8,10},{9,11},{10,... | collective-permute-start | bytes 2727944 | tf_op jit(solution)/shard_map/ppermute | solution.py:345
  912.8 38.7 %collective-permute-start.31 = (bf16[296,1536]{1,0:T(8,128)(2,1)S(1)}, bf16[296,1536]{1,0:T(8,128)(2,1)}, u32[]{:S(2)}, u32[]{:S(2)}) collective-permute-start(bf16[296,1536]{1,0:T(8,128)(2,1)S(1)} %pad_maximum_fusion.28.refs_2_), channel_id=1, source_target_pairs={{0,2},{1,3},{2,0},{3,1},{4,6},{5,7},{6,4},{7,5},{8,10},{9,11},{10,... | collective-permute-start | bytes 2727944 | tf_op jit(solution)/shard_map/ppermute | solution.py:345
  (228 other events, 4160.0 us)
Sparse Core Ops, SparseCore 0:
  10.8 142.7 all-gather.3
  155.8 136.2 all-gather.5
  294.2 136.2 all-gather.7
  624.9 161.6 reduce-scatter.4
  790.6 68.2 reduce-scatter.10
  862.3 162.5 reduce-scatter.6
  1028.6 138.5 reduce-scatter.8

commit v4 on v3

--- a/solution.py
+++ b/solution.py
@@ -288,7 +288,7 @@
 
 
 def outer_kernel(n, *refs):
-    left, right, out = refs[: 2 * n], refs[2 * n : 4 * n], refs[4 * n]
+    left, right, out = refs[: 2 * n], refs[2 * n : 4 * n], refs[-1]
     for s in range(2):
         total = None
         for j in range(n):
@@ -306,7 +306,7 @@
             out[s, p] = jnp.concatenate(rows, 0).astype(jnp.bfloat16)
 
 
-def outer(left_t, left_i, right_t, right_i, ranks=None):
+def outer(left_t, left_i, right_t, right_i, ranks=None, into=None, kinds=1, first=0):
     n = len(left_t)
     left, right = left_t + left_i, right_t + right_i
     columns = right[0].shape[1]
@@ -318,20 +318,25 @@
         step = 512 if width % 512 == 0 else width if width < 512 else 256
         steps = width // step
         l_spec = lambda v: pl.BlockSpec((v.shape[0], step), lambda m: (0, m))
+    if ranks is None:
+        shape, block, place = (2, steps * step, columns), (2, step, columns), lambda m: (0, m, 0)
+    else:
+        part = step // ranks
+        shape, block = (2, ranks, kinds * part, columns), (2, ranks, part, columns)
+        place = lambda m: (0, 0, first + m, 0)
+    held = [] if into is None else [into]
     return pl.pallas_call(
         partial(outer_kernel, n),
         grid=(steps,),
-        in_specs=[l_spec(v) for v in left] + [pl.BlockSpec(v.shape, lambda m: (0, 0)) for v in right],
-        out_specs=pl.BlockSpec((2, step, columns), lambda m: (0, m, 0))
-        if ranks is None
-        else pl.BlockSpec((2, ranks, step // ranks, columns), lambda m: (0, 0, m, 0)),
-        out_shape=jax.ShapeDtypeStruct(
-            (2, steps * step, columns) if ranks is None else (2, ranks, steps * step // ranks, columns),
-            jnp.bfloat16,
-        ),
+        in_specs=[l_spec(v) for v in left]
+        + [pl.BlockSpec(v.shape, lambda m: (0, 0)) for v in right]
+        + [pl.BlockSpec(memory_space=pl.ANY)] * len(held),
+        out_specs=pl.BlockSpec(block, place),
+        out_shape=jax.ShapeDtypeStruct(shape, jnp.bfloat16),
+        input_output_aliases={4 * n: 0} if held else {},
         compiler_params=pltpu.CompilerParams(vmem_limit_bytes=52 << 20),
         cost_estimate=pl.CostEstimate(flops=1 << 34, bytes_accessed=1 << 24, transcendentals=0),
-    )(*left, *right)
+    )(*left, *right, *held)
 
 
 class Group:
@@ -714,9 +719,11 @@
         v["hid_t"], v["hid_i"], v["slope_t"], v["slope_i"] = up_and_slope(v["h2_t"], v["h2_i"], f_up)
     f_down = after(f_down, slot[-1]["hid_i"])
     for j, v in enumerate(slot):
+        if j:
+            v["hid_t"] = after(v["hid_t"], *slot[j - 1]["go"][0])
         v["go"] = scatter_begin(v["hid_t"], v["hid_i"], f_down, True)
     for j, v in enumerate(slot):
-        v["m"] = scatter_end(v["go"], slot[-1]["go"][0])
+        v["m"] = scatter_end(v["go"], slot[j - 1]["go"][0])
         out = v["mid"] + pick(j, 5) * v["m"]
         mask = jnp.where(is_real, live[j].astype(jnp.float32), 0.0)
         err = mask * (out - merged(teacher_image, teacher_text, j).astype(jnp.float32))
@@ -730,7 +737,7 @@
 
     here = lax.axis_index("dp")
 
-    both = lambda a, b, *ranks: outer(*([v[name + e] for v in slot] for name in (a, b) for e in ("_t", "_i")), *ranks)
+    both = lambda a, b, *dealt: outer(*([v[name + e] for v in slot] for name in (a, b) for e in ("_t", "_i")), *dealt)
 
     def reduced(grads):
         return lax.psum_scatter(grads.reshape(2, -1, grads.shape[-1]), "dp", scatter_dimension=1, tiled=True)
@@ -738,13 +745,13 @@
     g_down = both("dm", "hid")
     done_down = reduced(g_down)
     for j, v in enumerate(slot):
-        v["dm_i"] = after(v["dm_i"], g_down if j == 0 else slot[j - 1]["dpre_i"])
+        v["dm_i"] = after(v["dm_i"], g_down if j == 0 else slot[j - 1]["go"][0])
         v["dpre_t"], v["dpre_i"] = scaled(v["dm_t"], v["dm_i"], f_down, v["slope_t"], v["slope_i"])
         v["go"] = scatter_begin(v["dpre_t"], v["dpre_i"], f_up, True)
     g_up = both("h2", "dpre")
     done_up = reduced(g_up)
     for j, v in enumerate(slot):
-        v["dh2"] = scatter_end(v["go"], g_up)
+        v["dh2"] = scatter_end(v["go"], g_up, slot[j - 1]["go"][0])
         v["dshift2"] = token_sums(v["dh2"])
         v["dscale2"] = token_sums(v["dh2"] * v["hat2"])
         v["dmid"] = v["cot"] + norm_backward(v["dh2"] * (1.0 + pick(j, 4)), v["hat2"], v["rstd2"])
@@ -753,16 +760,16 @@
         v["go"] = gather_begin(dy)
     for j, v in enumerate(slot):
         v["dy_i"], v["dy_t"] = gather_end(v["go"], slot[-1]["go"][0])
-    g_out = both("att", "dy", n_dp)
-    done_out = reduced(g_out)
-    for j, v in enumerate(slot):
-        v["dy_i"] = after(v["dy_i"], g_out, done_down) if j == 0 else after(v["dy_i"], slot[j - 1]["dqkv_i"])
+    slot[-1]["dy_i"] = after(slot[-1]["dy_i"], done_down)
+    g_out = both("att", "dy", n_dp, None, 4, 3)
+    for j, v in enumerate(slot):
+        v["dy_i"] = after(v["dy_i"], g_out) if j == 0 else after(v["dy_i"], slot[j - 1]["dqkv_i"])
         g_t, g_i = plain(v["dy_t"], v["dy_i"], f_out)
         v["dqkv_i"], v["dqkv_t"] = attend_back(v["qkv_i"], v["qkv_t"], g_i, g_t, v["lse"], pad_t, rows_t)
-    g_qkv = both("dqkv", "h1", n_dp)
-    done_qkv = reduced(g_qkv)
-    for j, v in enumerate(slot):
-        v["dqkv_i"] = after(v["dqkv_i"], g_qkv)
+    g_wide = both("dqkv", "h1", n_dp, g_out, 4, 0)
+    done_wide = reduced(g_wide)
+    for j, v in enumerate(slot):
+        v["dqkv_i"] = after(v["dqkv_i"], g_wide)
         v["go"] = scatter_begin(v["dqkv_t"], v["dqkv_i"], f_qkv, False)
     for j, v in enumerate(slot):
         v["dh1"] = scatter_end(v["go"], slot[-1]["go"][0])
@@ -789,8 +796,8 @@
     grad_cond = silu_pull(cond_total)[0]
     done_down = done_down.astype(jnp.float32)
     done_up = done_up.astype(jnp.float32)
-    done_out = done_out.astype(jnp.float32).reshape(2, heads + odd, -1, width)
-    done_qkv = done_qkv.astype(jnp.float32).reshape(2, 3, heads + odd, -1, width)
+    done_wide = done_wide.astype(jnp.float32).reshape(2, 4, heads + odd, -1, width)
+    done_qkv, done_out = done_wide[:, :3], done_wide[:, 3]
     if odd:
         done_qkv, done_out = done_qkv[:, :, :heads], done_out[:, :heads]
     return (

time: 1190 us -> 1100 us (0.924)
  waiting for transfers between devices: 572 us -> 501 us
  other arithmetic: 98.7 us -> 85.3 us
    reduce_scatter x4 -> x3, waiting for transfers between devices: 169 us -> 112 us  [reduced(): lax.psum_scatter(grads.reshape(2, -1, grads.shape[-1]), 'dp', scatter_dim...]
    ppermute x32, waiting for transfers between devices: 293 us -> 278 us  [send(): lax.ppermute(value, 'tensor', [(t, t ^ flip) for t in range(self.size)])]
    unnamed x430 -> x398, local copies, waits for them, and re-layouts: 80.2 us -> 83.7 us
  transfers between devices with their start and end apart: 39 -> 38, of which waited for: 25 -> 26; matrix products, arithmetic and copies ran while one was open for 10% -> 10% of each run, Pallas kernels for 25% -> 29%
where the time goes in v4:
time: 1100 us
  waiting for transfers between devices  501 us (46%)
  Pallas kernels  355 us (32%)
  local copies, waits for them, and re-layouts  113 us (10%)
  other arithmetic  85.3 us (8%)
  between operations  22.6 us (2%)
  starting transfers between devices  21.2 us (2%)
    ppermute x32, waiting for transfers between devices, send(): lax.ppermute(value, 'tensor', [(t, t ^ flip) for t in range(self.size)])  278 us
    reduce_scatter x3, waiting for transfers between devices, reduced(): lax.psum_scatter(grads.reshape(2, -1, grads.shape[-1]), 'dp', scatter_dim...  112 us
    pallas_call x14, Pallas kernels, over_columns(): pl.pallas_call(kernel, grid=(columns // step,), in_specs=[whole(v) for v...  109 us
    unnamed x398, local copies, waits for them, and re-layouts  83.7 us
    pallas_call x2, Pallas kernels, attend_back(): pl.pallas_call(partial(back_kernel, block, valid), grid=(pairs,), in_spec...  62.2 us
    pallas_call x4, Pallas kernels, outer(): pl.pallas_call(partial(outer_kernel, n), grid=(steps,), in_specs=[l_spec(...  59.2 us
    all_gather x1, waiting for transfers between devices, on_device(): f_down = lax.all_gather(w_down, 'dp', axis=1, tiled=True)  58 us
    pallas_call x2, Pallas kernels, attend(): pl.pallas_call(partial(attend_kernel, block, valid), grid=(pairs,), in_sp...  52.7 us
  transfers between devices with their start and end apart: 38, of which 26 were waited for; matrix products, arithmetic and copies ran while one was open for 10% of the time, Pallas kernels for 29%

profile of v4, /device:TPU:0, one launch (start us, length us, event | category | flops | bytes accessed | tf_op | source)
XLA Modules:
  0.0 1098.5 jit_solution(4576728474648793487)
XLA Ops:
  11.1 22.6 %shard_map.196 = (f32[4,8,1152]{2,1,0:T(8,128)S(1)}, bf16[64,192]{1,0:T(8,128)(2,1)S(1)}) custom-call(f32[8,8,256]{2,1,0:T(8,128)S(1)} %select_maximum_fusion.cond, bf16[2,192,2304]{2,1,0:T(8,128)(2,1)S(1)} %copy-done.56), custom_call_target="tpu_custom_call" | custom-call | flops 8589934592 | bytes 2097152 | tf_op jit(solution)/shard_map/pallas_call | solution.py:488
  42.2 22.3 %collective-permute-done.4.refs_0_ = bf16[296,1536]{1,0:T(8,128)(2,1)S(1)} collective-permute-done((bf16[296,1536]{1,0:T(8,128)(2,1)S(1)}, bf16[296,1536]{1,0:T(8,128)(2,1)S(1)}, u32[]{:S(2)}, u32[]{:S(2)}) %collective-permute-start.4) | collective-permute-done | bytes 909344 | tf_op jit(solution)/shard_map/ppermute | solution.py:350
  66.2 22.2 %collective-permute-done.refs_0_ = bf16[296,1536]{1,0:T(8,128)(2,1)S(1)} collective-permute-done((bf16[296,1536]{1,0:T(8,128)(2,1)S(1)}, bf16[296,1536]{1,0:T(8,128)(2,1)S(1)}, u32[]{:S(2)}, u32[]{:S(2)}) %collective-permute-start) | collective-permute-done | bytes 909344 | tf_op jit(solution)/shard_map/ppermute | solution.py:350
  101.0 52.6 %all-gather.4.cloned.1.call-done = bf16[2,4,6,64,1536]{4,3,2,1,0:T(8,128)(2,1)} async-done(((bf16[2,4,6,8,1536]{4,3,2,1,0:T(8,128)(2,1)}), bf16[2,4,6,64,1536]{4,3,2,1,0:T(8,128)(2,1)}) %all-gather.4.cloned.1.call-update) | async-done | bytes 9437200 | tf_op jit(solution)/shard_map/all_gather | solution.py:624
  164.5 26.2 %shard_map.199 = (bf16[1024,384]{1,0:T(8,128)(2,1)S(1)}, bf16[160,384]{1,0:T(8,128)(2,1)S(1)}, f32[3,2,1184]{2,1,0:T(2,128)S(1)}) custom-call(bf16[3,1024,384]{2,1,0:T(8,128)(2,1)S(1)} %get-tuple-element.61.qi.ki.vi, bf16[3,1024,384]{2,1,0:T(8,128)(2,1)S(1)} %get-tuple-element.61.qi.ki.vi, bf16[3,1024,384]{2,1,0:T(8,128)(2,1)S(1)} %get-tuple-element.61.qi.ki.vi, ...), custom_call_target="tpu_custom_call" | custom-call | flops 17179869184 | bytes 8388608 | tf_op jit(solution)/shard_map/pallas_call | solution.py:123
  199.1 26.5 %shard_map.204 = (bf16[1024,384]{1,0:T(8,128)(2,1)S(1)}, bf16[160,384]{1,0:T(8,128)(2,1)S(1)}, f32[3,2,1184]{2,1,0:T(2,128)S(1)}) custom-call(bf16[3,1024,384]{2,1,0:T(8,128)(2,1)S(1)} %get-tuple-element.67.qi.ki.vi, bf16[3,1024,384]{2,1,0:T(8,128)(2,1)S(1)} %get-tuple-element.67.qi.ki.vi, bf16[3,1024,384]{2,1,0:T(8,128)(2,1)S(1)} %get-tuple-element.67.qi.ki.vi, ...), custom_call_target="tpu_custom_call" | custom-call | flops 17179869184 | bytes 8388608 | tf_op jit(solution)/shard_map/pallas_call | solution.py:123
  239.9 18.3 %collective-permute-done.8.refs_0_ = bf16[296,1536]{1,0:T(8,128)(2,1)S(1)} collective-permute-done((bf16[296,1536]{1,0:T(8,128)(2,1)S(1)}, bf16[296,1536]{1,0:T(8,128)(2,1)S(1)}, u32[]{:S(2)}, u32[]{:S(2)}) %collective-permute-start.8) | collective-permute-done | bytes 909344 | tf_op jit(solution)/shard_map/ppermute | solution.py:350
  258.2 18.7 %collective-permute-done.3.refs_0_ = bf16[296,1536]{1,0:T(8,128)(2,1)S(1)} collective-permute-done((bf16[296,1536]{1,0:T(8,128)(2,1)S(1)}, bf16[296,1536]{1,0:T(8,128)(2,1)S(1)}, u32[]{:S(2)}, u32[]{:S(2)}) %collective-permute-start.3) | collective-permute-done | bytes 909344 | tf_op jit(solution)/shard_map/ppermute | solution.py:350
  285.2 21.1 %collective-permute-done.7.refs_0_ = bf16[296,1536]{1,0:T(8,128)(2,1)S(1)} collective-permute-done((bf16[296,1536]{1,0:T(8,128)(2,1)S(1)}, bf16[296,1536]{1,0:T(8,128)(2,1)S(1)}, u32[]{:S(2)}, u32[]{:S(2)}) %collective-permute-start.7) | collective-permute-done | bytes 909344 | tf_op jit(solution)/shard_map/ppermute | solution.py:350
  306.5 17.7 %collective-permute-done.10.refs_0_ = bf16[296,1536]{1,0:T(8,128)(2,1)S(1)} collective-permute-done((bf16[296,1536]{1,0:T(8,128)(2,1)S(1)}, bf16[296,1536]{1,0:T(8,128)(2,1)S(1)}, u32[]{:S(2)}, u32[]{:S(2)}) %collective-permute-start.10) | collective-permute-done | bytes 909344 | tf_op jit(solution)/shard_map/ppermute | solution.py:350
  372.5 58.0 %all-gather.8.cloned.1.call-done.refs_0_ = bf16[2,1536,1536]{2,1,0:T(8,128)(2,1)} async-done(((bf16[2,192,1536]{2,1,0:T(8,128)(2,1)}), bf16[2,1536,1536]{2,1,0:T(8,128)(2,1)}) %all-gather.8.cloned.1.call-update) | async-done | bytes 9437200 | tf_op jit(solution)/shard_map/all_gather | solution.py:626
  473.3 20.2 %collective-permute-done.13.refs_0_ = bf16[296,1536]{1,0:T(8,128)(2,1)S(1)} collective-permute-done((bf16[296,1536]{1,0:T(8,128)(2,1)S(1)}, bf16[296,1536]{1,0:T(8,128)(2,1)S(1)}, u32[]{:S(2)}, u32[]{:S(2)}) %collective-permute-start.13) | collective-permute-done | bytes 909344 | tf_op jit(solution)/shard_map/ppermute | solution.py:350
  500.2 12.9 %collective-permute-done.16.refs_0_ = bf16[296,1536]{1,0:T(8,128)(2,1)S(1)} collective-permute-done((bf16[296,1536]{1,0:T(8,128)(2,1)S(1)}, bf16[296,1536]{1,0:T(8,128)(2,1)S(1)}, u32[]{:S(2)}, u32[]{:S(2)}) %collective-permute-start.16) | collective-permute-done | bytes 909344 | tf_op jit(solution)/shard_map/ppermute | solution.py:350
  518.2 13.7 %collective-permute-done.15.refs_0_ = bf16[296,1536]{1,0:T(8,128)(2,1)S(1)} collective-permute-done((bf16[296,1536]{1,0:T(8,128)(2,1)S(1)}, bf16[296,1536]{1,0:T(8,128)(2,1)S(1)}, u32[]{:S(2)}, u32[]{:S(2)}) %collective-permute-start.15) | collective-permute-done | bytes 909344 | tf_op jit(solution)/shard_map/ppermute | solution.py:350
  533.7 21.1 %collective-permute-done.18.refs_0_ = bf16[296,1536]{1,0:T(8,128)(2,1)S(1)} collective-permute-done((bf16[296,1536]{1,0:T(8,128)(2,1)S(1)}, bf16[296,1536]{1,0:T(8,128)(2,1)S(1)}, u32[]{:S(2)}, u32[]{:S(2)}) %collective-permute-start.18) | collective-permute-done | bytes 909344 | tf_op jit(solution)/shard_map/ppermute | solution.py:350
  560.7 18.2 %shard_map.221.refs_1_ = bf16[2,1536,1536]{2,1,0:T(8,128)(2,1)} custom-call(bf16[160,1536]{1,0:T(8,128)(2,1)S(1)} %pad_maximum_fusion.36.refs_0_.at, bf16[160,1536]{1,0:T(8,128)(2,1)S(1)} %pad_maximum_fusion.37.refs_1_.at, bf16[1024,1536]{1,0:T(8,128)(2,1)} %pad_maximum_fusion.4.refs_2_.refs_0_, bf16[1024,1536]{1,0:T(8,128)(2,1)} %pad_maximum_fusion.5.refs_3_.refs_0_, ...), custom_call_target="tpu_custom_call" | custom-call | flops 17179869184 | bytes 16777216 | tf_op jit(solution)/shard_map/pallas_call | solution.py:328
  640.8 18.2 %shard_map.227.refs_1_ = bf16[2,1536,1536]{2,1,0:T(8,128)(2,1)} custom-call(bf16[160,1536]{1,0:T(8,128)(2,1)S(1)} %copy-done.46, bf16[160,1536]{1,0:T(8,128)(2,1)S(1)} %copy-done.48, bf16[1024,1536]{1,0:T(8,128)(2,1)} %pad_maximum_fusion.2.ai.refs_2_, bf16[1024,1536]{1,0:T(8,128)(2,1)} %copy-done.8, bf16[160,1536]{1,0:T(8,128)(2,1)S(1)} %copy-done.72, ...), custom_call_target="tpu_custom_call" | custom-call | flops 17179869184 | bytes 16777216 | tf_op jit(solution)/shard_map/pallas_call | solution.py:328
  706.4 22.2 %collective-permute-done.26.refs_0_ = bf16[296,1536]{1,0:T(8,128)(2,1)S(1)} collective-permute-done((bf16[296,1536]{1,0:T(8,128)(2,1)S(1)}, bf16[296,1536]{1,0:T(8,128)(2,1)S(1)}, u32[]{:S(2)}, u32[]{:S(2)}) %collective-permute-start.26) | collective-permute-done | bytes 909344 | tf_op jit(solution)/shard_map/ppermute | solution.py:350
  760.7 31.1 %shard_map.237 = (bf16[3,1024,384]{2,1,0:T(8,128)(2,1)S(1)}, bf16[3,160,384]{2,1,0:T(8,128)(2,1)S(1)}) custom-call(bf16[3,1024,384]{2,1,0:T(8,128)(2,1)S(1)} %copy-done.70, bf16[3,1024,384]{2,1,0:T(8,128)(2,1)S(1)} %copy-done.70, bf16[3,1024,384]{2,1,0:T(8,128)(2,1)S(1)} %copy-done.70, bf16[3,160,384]{2,1,0:T(8,128)(2,1)S(1)} %copy-done.79, ...), custom_call_target="tpu_custom_call" | custom-call | flops 34359738368 | bytes 16777216 | tf_op jit(solution)/shard_map/pallas_call | solution.py:142
  795.4 31.1 %shard_map.240 = (bf16[3,1024,384]{2,1,0:T(8,128)(2,1)S(1)}, bf16[3,160,384]{2,1,0:T(8,128)(2,1)S(1)}) custom-call(bf16[3,1024,384]{2,1,0:T(8,128)(2,1)S(1)} %copy-done.68, bf16[3,1024,384]{2,1,0:T(8,128)(2,1)S(1)} %copy-done.68, bf16[3,1024,384]{2,1,0:T(8,128)(2,1)S(1)} %copy-done.68, bf16[3,160,384]{2,1,0:T(8,128)(2,1)S(1)} %copy-done.77, ...), custom_call_target="tpu_custom_call" | custom-call | flops 34359738368 | bytes 16777216 | tf_op jit(solution)/shard_map/pallas_call | solution.py:142
  828.0 14.9 %shard_map.241.refs_1_ = bf16[2,8,192,1536]{3,2,1,0:T(8,128)(2,1)} custom-call(bf16[3,160,384]{2,1,0:T(8,128)(2,1)S(1)} %get-tuple-element.96.refs_0_.at, bf16[3,160,384]{2,1,0:T(8,128)(2,1)S(1)} %get-tuple-element.101.refs_1_.at, bf16[3,1024,384]{2,1,0:T(8,128)(2,1)} %copy-done.11, ...), custom_call_target="tpu_custom_call", output_to_operand_aliasing={{}: (8, {})} | custom-call | flops 17179869184 | bytes 16777216 | tf_op jit(solution)/shard_map/pallas_call | solution.py:328
  881.2 34.6 %collective-permute-done.31.refs_0_ = bf16[296,1536]{1,0:T(8,128)(2,1)S(1)} collective-permute-done((bf16[296,1536]{1,0:T(8,128)(2,1)S(1)}, bf16[296,1536]{1,0:T(8,128)(2,1)S(1)}, u32[]{:S(2)}, u32[]{:S(2)}) %collective-permute-start.31) | collective-permute-done | bytes 909344 | tf_op jit(solution)/shard_map/ppermute | solution.py:350
  935.5 35.1 %shard_map.249 = (f32[2,192,2304]{2,1,0:T(8,128)S(1)}, f32[8,8,256]{2,1,0:T(8,128)S(1)}, f32[8,128]{1,0:T(8,128)S(1)}) custom-call(f32[4,8,1152]{2,1,0:T(8,128)S(1)} %copy-done.38, f32[8,128]{1,0:T(8,128)S(1)} %broadcast_in_dim.396.lost, bf16[64,192]{1,0:T(8,128)(2,1)S(1)} %copy-done.85, bf16[2,192,2304]{2,1,0:T(8,128)(2,1)S(1)} %copy-done.57), custom_call_target="tpu_custom_call" | custom-call | flops 8589934592 | bytes 2097152 | tf_op jit(solution)/shard_map/pallas_call | solution.py:567
  980.5 103.9 %reduce-scatter.8.cloned.1.call-done = bf16[2,192,1536]{2,1,0:T(8,128)(2,1)} async-done(((bf16[2,1536,1536]{2,1,0:T(8,128)(2,1)}), bf16[2,192,1536]{2,1,0:T(8,128)(2,1)}) %reduce-scatter.8.cloned.1.call-update) | async-done | bytes 1179664 | tf_op jit(solution)/shard_map/reduce_scatter | solution.py:743
  (778 shorter events, 392.6 us)
Async XLA Ops:
  7.2 146.4 %all-gather.4.cloned.1.call-start = ((), (), s32[]{:S(2)}) async-start(), calls=%async_computation.3 | async-start | bytes 10616832 | tf_op jit(solution)/shard_map/all_gather | solution.py:624
  9.6 321.9 %all-gather.6.cloned.1.call-start = ((), (), s32[]{:S(2)}) async-start(), calls=%async_computation.4 | async-start | bytes 10616832 | tf_op jit(solution)/shard_map/all_gather | solution.py:625
  10.4 420.1 %all-gather.8.cloned.1.call-start = ((), (), s32[]{:S(2)}) async-start(), calls=%async_computation.5 | async-start | bytes 10616832 | tf_op jit(solution)/shard_map/all_gather | solution.py:626
  41.7 22.7 %collective-permute-start.4 = (bf16[296,1536]{1,0:T(8,128)(2,1)S(1)}, bf16[296,1536]{1,0:T(8,128)(2,1)S(1)}, u32[]{:S(2)}, u32[]{:S(2)}) collective-permute-start(bf16[296,1536]{1,0:T(8,128)(2,1)S(1)} %get-tuple-element.297.refs_1_), channel_id=1, source_target_pairs={{0,2},{1,3},{2,0},{3,1},{4,6},{5,7},{6,4},{7,5},{8,10},{9,11},{10,... | collective-permute-start | bytes 2727944 | tf_op jit(solution)/shard_map/ppermute | solution.py:350
  65.8 26.5 %collective-permute-start.5 = (bf16[592,1536]{1,0:T(8,128)(2,1)}, bf16[592,1536]{1,0:T(8,128)(2,1)}, u32[]{:S(2)}, u32[]{:S(2)}) collective-permute-start(bf16[592,1536]{1,0:T(8,128)(2,1)} %pad_maximum_fusion.10), channel_id=1, source_target_pairs={{0,1},{1,0},{2,3},{3,2},{4,5},{5,4},{6,7},{7,6},{8,9},{9,8},{10,11... | collective-permute-start | bytes 5455880 | tf_op jit(solution)/shard_map/ppermute | solution.py:350
  89.8 651.7 %reduce-scatter.4.cloned.1.call-start = ((), (), s32[]{:S(2)}) async-start(), calls=%async_computation.6 | async-start | bytes 10616832 | tf_op jit(solution)/shard_map/reduce_scatter | solution.py:743
  235.2 23.1 %collective-permute-start.8 = (bf16[296,1536]{1,0:T(8,128)(2,1)S(1)}, bf16[296,1536]{1,0:T(8,128)(2,1)S(1)}, u32[]{:S(2)}, u32[]{:S(2)}) collective-permute-start(bf16[296,1536]{1,0:T(8,128)(2,1)S(1)} %pad_maximum_fusion.25.refs_2_), channel_id=1, source_target_pairs={{0,2},{1,3},{2,0},{3,1},{4,6},{5,7},{6,4},{7,5},{8,10},{9,11},{10,... | collective-permute-start | bytes 2727944 | tf_op jit(solution)/shard_map/ppermute | solution.py:350
  238.3 38.7 %collective-permute-start.3 = (bf16[296,1536]{1,0:T(8,128)(2,1)S(1)}, bf16[296,1536]{1,0:T(8,128)(2,1)S(1)}, u32[]{:S(2)}, u32[]{:S(2)}) collective-permute-start(bf16[296,1536]{1,0:T(8,128)(2,1)S(1)} %pad_maximum_fusion.24), channel_id=1, source_target_pairs={{0,2},{1,3},{2,0},{3,1},{4,6},{5,7},{6,4},{7,5},{8,10},{9,11},{10,... | collective-permute-start | bytes 2727944 | tf_op jit(solution)/shard_map/ppermute | solution.py:350
  283.2 23.2 %collective-permute-start.7 = (bf16[296,1536]{1,0:T(8,128)(2,1)S(1)}, bf16[296,1536]{1,0:T(8,128)(2,1)S(1)}, u32[]{:S(2)}, u32[]{:S(2)}) collective-permute-start(bf16[296,1536]{1,0:T(8,128)(2,1)S(1)} %get-tuple-element.294), channel_id=1, source_target_pairs={{0,2},{1,3},{2,0},{3,1},{4,6},{5,7},{6,4},{7,5},{8,10},{9,11},{10,... | collective-permute-start | bytes 2727944 | tf_op jit(solution)/shard_map/ppermute | solution.py:350
  284.7 39.5 %collective-permute-start.10 = (bf16[296,1536]{1,0:T(8,128)(2,1)S(1)}, bf16[296,1536]{1,0:T(8,128)(2,1)S(1)}, u32[]{:S(2)}, u32[]{:S(2)}) collective-permute-start(bf16[296,1536]{1,0:T(8,128)(2,1)S(1)} %get-tuple-element.293.refs_1_), channel_id=1, source_target_pairs={{0,2},{1,3},{2,0},{3,1},{4,6},{5,7},{6,4},{7,5},{8,10},{9,11},{10,... | collective-permute-start | bytes 2727944 | tf_op jit(solution)/shard_map/ppermute | solution.py:350
  470.5 23.1 %collective-permute-start.13 = (bf16[296,1536]{1,0:T(8,128)(2,1)S(1)}, bf16[296,1536]{1,0:T(8,128)(2,1)S(1)}, u32[]{:S(2)}, u32[]{:S(2)}) collective-permute-start(bf16[296,1536]{1,0:T(8,128)(2,1)S(1)} %pad_maximum_fusion.26.refs_2_), channel_id=1, source_target_pairs={{0,2},{1,3},{2,0},{3,1},{4,6},{5,7},{6,4},{7,5},{8,10},{9,11},{10,... | collective-permute-start | bytes 2727944 | tf_op jit(solution)/shard_map/ppermute | solution.py:350
  472.6 40.5 %collective-permute-start.16 = (bf16[296,1536]{1,0:T(8,128)(2,1)S(1)}, bf16[296,1536]{1,0:T(8,128)(2,1)S(1)}, u32[]{:S(2)}, u32[]{:S(2)}) collective-permute-start(bf16[296,1536]{1,0:T(8,128)(2,1)S(1)} %pad_maximum_fusion.27.refs_2_), channel_id=1, source_target_pairs={{0,2},{1,3},{2,0},{3,1},{4,6},{5,7},{6,4},{7,5},{8,10},{9,11},{10,... | collective-permute-start | bytes 2727944 | tf_op jit(solution)/shard_map/ppermute | solution.py:350
  498.6 33.3 %collective-permute-start.15 = (bf16[296,1536]{1,0:T(8,128)(2,1)S(1)}, bf16[296,1536]{1,0:T(8,128)(2,1)S(1)}, u32[]{:S(2)}, u32[]{:S(2)}) collective-permute-start(bf16[296,1536]{1,0:T(8,128)(2,1)S(1)} %get-tuple-element.236.refs_1_), channel_id=1, source_target_pairs={{0,2},{1,3},{2,0},{3,1},{4,6},{5,7},{6,4},{7,5},{8,10},{9,11},{10,... | collective-permute-start | bytes 2727944 | tf_op jit(solution)/shard_map/ppermute | solution.py:350
  532.1 23.2 %collective-permute-start.17 = (bf16[592,1536]{1,0:T(8,128)(2,1)S(1)}, bf16[592,1536]{1,0:T(8,128)(2,1)S(1)}, u32[]{:S(2)}, u32[]{:S(2)}) collective-permute-start(bf16[592,1536]{1,0:T(8,128)(2,1)S(1)} %pad_maximum_fusion.16), channel_id=1, source_target_pairs={{0,1},{1,0},{2,3},{3,2},{4,5},{5,4},{6,7},{7,6},{8,9},{9,8},{10,11... | collective-permute-start | bytes 5455880 | tf_op jit(solution)/shard_map/ppermute | solution.py:350
  532.2 22.6 %collective-permute-start.18 = (bf16[296,1536]{1,0:T(8,128)(2,1)S(1)}, bf16[296,1536]{1,0:T(8,128)(2,1)S(1)}, u32[]{:S(2)}, u32[]{:S(2)}) collective-permute-start(bf16[296,1536]{1,0:T(8,128)(2,1)S(1)} %get-tuple-element.238.refs_1_), channel_id=1, source_target_pairs={{0,2},{1,3},{2,0},{3,1},{4,6},{5,7},{6,4},{7,5},{8,10},{9,11},{10,... | collective-permute-start | bytes 2727944 | tf_op jit(solution)/shard_map/ppermute | solution.py:350
  579.7 349.5 %reduce-scatter.6.cloned.1.call-start = ((), (), s32[]{:S(2)}) async-start(), calls=%async_computation.7 | async-start | bytes 10616832 | tf_op jit(solution)/shard_map/reduce_scatter | solution.py:743
  639.2 25.4 %collective-permute-start.21 = (bf16[296,1536]{1,0:T(8,128)(2,1)S(1)}, bf16[296,1536]{1,0:T(8,128)(2,1)S(1)}, u32[]{:S(2)}, u32[]{:S(2)}) collective-permute-start(bf16[296,1536]{1,0:T(8,128)(2,1)S(1)} %pad_maximum_fusion.28.refs_2_), channel_id=1, source_target_pairs={{0,2},{1,3},{2,0},{3,1},{4,6},{5,7},{6,4},{7,5},{8,10},{9,11},{10,... | collective-permute-start | bytes 2727944 | tf_op jit(solution)/shard_map/ppermute | solution.py:350
  659.0 425.4 %reduce-scatter.8.cloned.1.call-start = ((), (), s32[]{:S(2)}) async-start(), calls=%async_computation.8 | async-start | bytes 10616832 | tf_op jit(solution)/shard_map/reduce_scatter | solution.py:743
  664.0 23.1 %collective-permute-start.24 = (bf16[296,1536]{1,0:T(8,128)(2,1)S(1)}, bf16[296,1536]{1,0:T(8,128)(2,1)S(1)}, u32[]{:S(2)}, u32[]{:S(2)}) collective-permute-start(bf16[296,1536]{1,0:T(8,128)(2,1)S(1)} %pad_maximum_fusion.29.refs_3_), channel_id=1, source_target_pairs={{0,2},{1,3},{2,0},{3,1},{4,6},{5,7},{6,4},{7,5},{8,10},{9,11},{10,... | collective-permute-start | bytes 2727944 | tf_op jit(solution)/shard_map/ppermute | solution.py:350
  675.9 30.0 %collective-permute-start.23 = (bf16[296,1536]{1,0:T(8,128)(2,1)S(1)}, bf16[296,1536]{1,0:T(8,128)(2,1)S(1)}, u32[]{:S(2)}, u32[]{:S(2)}) collective-permute-start(bf16[296,1536]{1,0:T(8,128)(2,1)S(1)} %fusion.26.refs_2_), channel_id=1, source_target_pairs={{0,2},{1,3},{2,0},{3,1},{4,6},{5,7},{6,4},{7,5},{8,10},{9,11},{10,... | collective-permute-start | bytes 2727944 | tf_op jit(solution)/shard_map/ppermute | solution.py:350
  706.0 23.2 %collective-permute-start.25 = (bf16[592,1536]{1,0:T(8,128)(2,1)S(1)}, bf16[592,1536]{1,0:T(8,128)(2,1)S(1)}, u32[]{:S(2)}, u32[]{:S(2)}) collective-permute-start(bf16[592,1536]{1,0:T(8,128)(2,1)S(1)} %pad_maximum_fusion.20), channel_id=1, source_target_pairs={{0,1},{1,0},{2,3},{3,2},{4,5},{5,4},{6,7},{7,6},{8,9},{9,8},{10,11... | collective-permute-start | bytes 5455880 | tf_op jit(solution)/shard_map/ppermute | solution.py:350
  706.1 22.6 %collective-permute-start.26 = (bf16[296,1536]{1,0:T(8,128)(2,1)S(1)}, bf16[296,1536]{1,0:T(8,128)(2,1)S(1)}, u32[]{:S(2)}, u32[]{:S(2)}) collective-permute-start(bf16[296,1536]{1,0:T(8,128)(2,1)S(1)} %fusion.31.refs_1_), channel_id=1, source_target_pairs={{0,2},{1,3},{2,0},{3,1},{4,6},{5,7},{6,4},{7,5},{8,10},{9,11},{10,... | collective-permute-start | bytes 2727944 | tf_op jit(solution)/shard_map/ppermute | solution.py:350
  874.1 41.8 %collective-permute-start.29 = (bf16[296,1536]{1,0:T(8,128)(2,1)S(1)}, bf16[296,1536]{1,0:T(8,128)(2,1)S(1)}, u32[]{:S(2)}, u32[]{:S(2)}) collective-permute-start(bf16[296,1536]{1,0:T(8,128)(2,1)S(1)} %pad_maximum_fusion.30), channel_id=1, source_target_pairs={{0,2},{1,3},{2,0},{3,1},{4,6},{5,7},{6,4},{7,5},{8,10},{9,11},{10,... | collective-permute-start | bytes 2727944 | tf_op jit(solution)/shard_map/ppermute | solution.py:350
  877.4 38.4 %collective-permute-start.31 = (bf16[296,1536]{1,0:T(8,128)(2,1)S(1)}, bf16[296,1536]{1,0:T(8,128)(2,1)S(1)}, u32[]{:S(2)}, u32[]{:S(2)}) collective-permute-start(bf16[296,1536]{1,0:T(8,128)(2,1)S(1)} %pad_maximum_fusion.31.refs_2_), channel_id=1, source_target_pairs={{0,2},{1,3},{2,0},{3,1},{4,6},{5,7},{6,4},{7,5},{8,10},{9,11},{10,... | collective-permute-start | bytes 2727944 | tf_op jit(solution)/shard_map/ppermute | solution.py:350
  (210 other events, 3875.5 us)
Sparse Core Ops, SparseCore 0:
  10.8 142.7 all-gather.3
  155.8 136.2 all-gather.5
  294.3 136.2 all-gather.7
  579.8 161.6 reduce-scatter.3
  744.9 162.5 reduce-scatter.5
  910.9 173.4 reduce-scatter.7

commit v5 on v4

--- a/solution.py
+++ b/solution.py
@@ -371,6 +371,25 @@
         self.size = size
         self.nx = math.isqrt(size // 2)
         self.nz = size // self.nx
+
+    def send(self, value, flip):
+        return lax.ppermute(value, "dp", [(p, p ^ flip) for p in range(self.size)])
+
+    def across(self, partial_of):
+        here = lax.axis_index("dp")
+        rank = lambda zk, xk: flip_bits(here, zk * self.nx + xk, self.size)
+        sent = lambda xk: jnp.stack([partial_of(rank(zk, xk)) for zk in range(self.nz)])
+        own = [partial_of(rank(zk, 0)) for zk in range(self.nz)]
+        return own, [self.send(sent(xk), xk) for xk in range(1, self.nx)]
+
+    def along(self, own, got):
+        totals = []
+        for zk in range(self.nz):
+            total = own[zk].astype(jnp.float32)
+            for value in got:
+                total = total + value[zk].astype(jnp.float32)
+            totals.append(total)
+        return totals[0], [self.send(totals[zk].astype(jnp.bfloat16), zk * self.nx) for zk in range(1, self.nz)]
 
 
 def pass_kernel(*refs):
@@ -761,13 +780,17 @@
     for j, v in enumerate(slot):
         v["dy_i"], v["dy_t"] = gather_end(v["go"], slot[-1]["go"][0])
     slot[-1]["dy_i"] = after(slot[-1]["dy_i"], done_down)
-    g_out = both("att", "dy", n_dp, None, 4, 3)
+    g_out = both("att", "dy", n_dp)
+    out_own, out_got = data.across(lambda rank: lax.dynamic_index_in_dim(g_out, rank, 1, keepdims=False))
     for j, v in enumerate(slot):
         v["dy_i"] = after(v["dy_i"], g_out) if j == 0 else after(v["dy_i"], slot[j - 1]["dqkv_i"])
         g_t, g_i = plain(v["dy_t"], v["dy_i"], f_out)
         v["dqkv_i"], v["dqkv_t"] = attend_back(v["qkv_i"], v["qkv_t"], g_i, g_t, v["lse"], pad_t, rows_t)
-    g_wide = both("dqkv", "h1", n_dp, g_out, 4, 0)
-    done_wide = reduced(g_wide)
+        if j == 0:
+            out_got = [after(value, v["dqkv_i"]) for value in out_got]
+    g_wide = both("dqkv", "h1", n_dp, None, 3, 0)
+    done_qkv = reduced(g_wide)
+    out_total, out_got = data.along(out_own, out_got)
     for j, v in enumerate(slot):
         v["dqkv_i"] = after(v["dqkv_i"], g_wide)
         v["go"] = scatter_begin(v["dqkv_t"], v["dqkv_i"], f_qkv, False)
@@ -796,8 +819,9 @@
     grad_cond = silu_pull(cond_total)[0]
     done_down = done_down.astype(jnp.float32)
     done_up = done_up.astype(jnp.float32)
-    done_wide = done_wide.astype(jnp.float32).reshape(2, 4, heads + odd, -1, width)
-    done_qkv, done_out = done_wide[:, :3], done_wide[:, 3]
+    done_qkv = done_qkv.astype(jnp.float32).reshape(2, 3, heads + odd, -1, width)
+    done_out = out_total + sum(after(value, slot[-1]["go"][0]).astype(jnp.float32) for value in out_got)
+    done_out = done_out.reshape(2, heads + odd, -1, width)
     if odd:
         done_qkv, done_out = done_qkv[:, :, :heads], done_out[:, :heads]
     return (

time: 1100 us -> 1080 us (0.982)
  waiting for transfers between devices: 501 us -> 460 us
  other arithmetic: 85.3 us -> 104 us
    reduce_scatter x3, waiting for transfers between devices: 112 us -> 41.6 us  [reduced(): lax.psum_scatter(grads.reshape(2, -1, grads.shape[-1]), 'dp', scatter_dim...]
    ppermute x0 -> x4, waiting for transfers between devices: none -> 68 us  [send(): return lax.ppermute(value, 'dp', [(p, p ^ flip) for p in range(self.size)])]
    ppermute x32, waiting for transfers between devices: 278 us -> 239 us  [send(): lax.ppermute(value, 'tensor', [(t, t ^ flip) for t in range(self.size)])]
    unnamed x398 -> x418, local copies, waits for them, and re-layouts: 83.7 us -> 84.4 us
  transfers between devices with their start and end apart: 38 -> 42, of which waited for: 26 -> 24; matrix products, arithmetic and copies ran while one was open for 10% -> 13% of each run, Pallas kernels for 29% -> 29%
where the time goes in v5:
time: 1080 us
  waiting for transfers between devices  460 us (43%)
  Pallas kernels  346 us (32%)
  local copies, waits for them, and re-layouts  123 us (11%)
  other arithmetic  104 us (10%)
  starting transfers between devices  23.4 us (2%)
  between operations  22.3 us (2%)
    ppermute x32, waiting for transfers between devices, send(): lax.ppermute(value, 'tensor', [(t, t ^ flip) for t in range(self.size)])  239 us
    pallas_call x14, Pallas kernels, over_columns(): pl.pallas_call(kernel, grid=(columns // step,), in_specs=[whole(v) for v...  109 us
    unnamed x418, local copies, waits for them, and re-layouts  84.4 us
    ppermute x4, waiting for transfers between devices, send(): return lax.ppermute(value, 'dp', [(p, p ^ flip) for p in range(self.size)])  68 us
    pallas_call x2, Pallas kernels, attend_back(): pl.pallas_call(partial(back_kernel, block, valid), grid=(pairs,), in_spec...  62.2 us
    pallas_call x4, Pallas kernels, outer(): pl.pallas_call(partial(outer_kernel, n), grid=(steps,), in_specs=[l_spec(...  59 us
    all_gather x1, waiting for transfers between devices, on_device(): f_down = lax.all_gather(w_down, 'dp', axis=1, tiled=True)  57.9 us
    pallas_call x2, Pallas kernels, attend(): pl.pallas_call(partial(attend_kernel, block, valid), grid=(pairs,), in_sp...  52.7 us
  transfers between devices with their start and end apart: 42, of which 24 were waited for; matrix products, arithmetic and copies ran while one was open for 13% of the time, Pallas kernels for 29%

profile of v5, /device:TPU:0, one launch (start us, length us, event | category | flops | bytes accessed | tf_op | source)
XLA Modules:
  0.0 1078.4 jit_solution(6487460868552105686)
XLA Ops:
  11.1 22.6 %shard_map.196 = (f32[4,8,1152]{2,1,0:T(8,128)S(1)}, bf16[64,192]{1,0:T(8,128)(2,1)S(1)}) custom-call(f32[8,8,256]{2,1,0:T(8,128)S(1)} %select_maximum_fusion.cond, bf16[2,192,2304]{2,1,0:T(8,128)(2,1)S(1)} %copy-done.64), custom_call_target="tpu_custom_call" | custom-call | flops 8589934592 | bytes 2097152 | tf_op jit(solution)/shard_map/pallas_call | solution.py:507
  42.2 22.3 %collective-permute-done.4.refs_0_ = bf16[296,1536]{1,0:T(8,128)(2,1)S(1)} collective-permute-done((bf16[296,1536]{1,0:T(8,128)(2,1)S(1)}, bf16[296,1536]{1,0:T(8,128)(2,1)S(1)}, u32[]{:S(2)}, u32[]{:S(2)}) %collective-permute-start.4) | collective-permute-done | bytes 909344 | tf_op jit(solution)/shard_map/ppermute | solution.py:350
  66.3 22.2 %collective-permute-done.refs_0_ = bf16[296,1536]{1,0:T(8,128)(2,1)S(1)} collective-permute-done((bf16[296,1536]{1,0:T(8,128)(2,1)S(1)}, bf16[296,1536]{1,0:T(8,128)(2,1)S(1)}, u32[]{:S(2)}, u32[]{:S(2)}) %collective-permute-start) | collective-permute-done | bytes 909344 | tf_op jit(solution)/shard_map/ppermute | solution.py:350
  101.0 52.5 %all-gather.4.cloned.1.call-done = bf16[2,4,6,64,1536]{4,3,2,1,0:T(8,128)(2,1)} async-done(((bf16[2,4,6,8,1536]{4,3,2,1,0:T(8,128)(2,1)}), bf16[2,4,6,64,1536]{4,3,2,1,0:T(8,128)(2,1)}) %all-gather.4.cloned.1.call-update) | async-done | bytes 9437200 | tf_op jit(solution)/shard_map/all_gather | solution.py:643
  164.5 26.2 %shard_map.199 = (bf16[1024,384]{1,0:T(8,128)(2,1)S(1)}, bf16[160,384]{1,0:T(8,128)(2,1)S(1)}, f32[3,2,1184]{2,1,0:T(2,128)S(1)}) custom-call(bf16[3,1024,384]{2,1,0:T(8,128)(2,1)S(1)} %get-tuple-element.61.qi.ki.vi, bf16[3,1024,384]{2,1,0:T(8,128)(2,1)S(1)} %get-tuple-element.61.qi.ki.vi, bf16[3,1024,384]{2,1,0:T(8,128)(2,1)S(1)} %get-tuple-element.61.qi.ki.vi, ...), custom_call_target="tpu_custom_call" | custom-call | flops 17179869184 | bytes 8388608 | tf_op jit(solution)/shard_map/pallas_call | solution.py:123
  199.1 26.5 %shard_map.204 = (bf16[1024,384]{1,0:T(8,128)(2,1)S(1)}, bf16[160,384]{1,0:T(8,128)(2,1)S(1)}, f32[3,2,1184]{2,1,0:T(2,128)S(1)}) custom-call(bf16[3,1024,384]{2,1,0:T(8,128)(2,1)S(1)} %get-tuple-element.67.qi.ki.vi, bf16[3,1024,384]{2,1,0:T(8,128)(2,1)S(1)} %get-tuple-element.67.qi.ki.vi, bf16[3,1024,384]{2,1,0:T(8,128)(2,1)S(1)} %get-tuple-element.67.qi.ki.vi, ...), custom_call_target="tpu_custom_call" | custom-call | flops 17179869184 | bytes 8388608 | tf_op jit(solution)/shard_map/pallas_call | solution.py:123
  239.9 18.3 %collective-permute-done.8.refs_0_ = bf16[296,1536]{1,0:T(8,128)(2,1)S(1)} collective-permute-done((bf16[296,1536]{1,0:T(8,128)(2,1)S(1)}, bf16[296,1536]{1,0:T(8,128)(2,1)S(1)}, u32[]{:S(2)}, u32[]{:S(2)}) %collective-permute-start.8) | collective-permute-done | bytes 909344 | tf_op jit(solution)/shard_map/ppermute | solution.py:350
  258.3 18.7 %collective-permute-done.3.refs_0_ = bf16[296,1536]{1,0:T(8,128)(2,1)S(1)} collective-permute-done((bf16[296,1536]{1,0:T(8,128)(2,1)S(1)}, bf16[296,1536]{1,0:T(8,128)(2,1)S(1)}, u32[]{:S(2)}, u32[]{:S(2)}) %collective-permute-start.3) | collective-permute-done | bytes 909344 | tf_op jit(solution)/shard_map/ppermute | solution.py:350
  285.3 21.1 %collective-permute-done.7.refs_0_ = bf16[296,1536]{1,0:T(8,128)(2,1)S(1)} collective-permute-done((bf16[296,1536]{1,0:T(8,128)(2,1)S(1)}, bf16[296,1536]{1,0:T(8,128)(2,1)S(1)}, u32[]{:S(2)}, u32[]{:S(2)}) %collective-permute-start.7) | collective-permute-done | bytes 909344 | tf_op jit(solution)/shard_map/ppermute | solution.py:350
  306.6 17.7 %collective-permute-done.10.refs_0_ = bf16[296,1536]{1,0:T(8,128)(2,1)S(1)} collective-permute-done((bf16[296,1536]{1,0:T(8,128)(2,1)S(1)}, bf16[296,1536]{1,0:T(8,128)(2,1)S(1)}, u32[]{:S(2)}, u32[]{:S(2)}) %collective-permute-start.10) | collective-permute-done | bytes 909344 | tf_op jit(solution)/shard_map/ppermute | solution.py:350
  372.7 57.9 %all-gather.8.cloned.1.call-done.refs_0_ = bf16[2,1536,1536]{2,1,0:T(8,128)(2,1)} async-done(((bf16[2,192,1536]{2,1,0:T(8,128)(2,1)}), bf16[2,1536,1536]{2,1,0:T(8,128)(2,1)}) %all-gather.8.cloned.1.call-update) | async-done | bytes 9437200 | tf_op jit(solution)/shard_map/all_gather | solution.py:645
  473.4 20.2 %collective-permute-done.13.refs_0_ = bf16[296,1536]{1,0:T(8,128)(2,1)S(1)} collective-permute-done((bf16[296,1536]{1,0:T(8,128)(2,1)S(1)}, bf16[296,1536]{1,0:T(8,128)(2,1)S(1)}, u32[]{:S(2)}, u32[]{:S(2)}) %collective-permute-start.13) | collective-permute-done | bytes 909344 | tf_op jit(solution)/shard_map/ppermute | solution.py:350
  518.2 13.8 %collective-permute-done.15.refs_0_ = bf16[296,1536]{1,0:T(8,128)(2,1)S(1)} collective-permute-done((bf16[296,1536]{1,0:T(8,128)(2,1)S(1)}, bf16[296,1536]{1,0:T(8,128)(2,1)S(1)}, u32[]{:S(2)}, u32[]{:S(2)}) %collective-permute-start.15) | collective-permute-done | bytes 909344 | tf_op jit(solution)/shard_map/ppermute | solution.py:350
  533.7 21.1 %collective-permute-done.18.refs_0_ = bf16[296,1536]{1,0:T(8,128)(2,1)S(1)} collective-permute-done((bf16[296,1536]{1,0:T(8,128)(2,1)S(1)}, bf16[296,1536]{1,0:T(8,128)(2,1)S(1)}, u32[]{:S(2)}, u32[]{:S(2)}) %collective-permute-start.18) | collective-permute-done | bytes 909344 | tf_op jit(solution)/shard_map/ppermute | solution.py:350
  560.8 18.1 %shard_map.221.refs_1_ = bf16[2,1536,1536]{2,1,0:T(8,128)(2,1)} custom-call(bf16[160,1536]{1,0:T(8,128)(2,1)S(1)} %pad_maximum_fusion.37.refs_0_.at, bf16[160,1536]{1,0:T(8,128)(2,1)S(1)} %pad_maximum_fusion.38.refs_1_.at, bf16[1024,1536]{1,0:T(8,128)(2,1)} %pad_maximum_fusion.4.refs_2_.refs_0_, bf16[1024,1536]{1,0:T(8,128)(2,1)} %pad_maximum_fusion.5.refs_3_.refs_0_, ...), custom_call_target="tpu_custom_call" | custom-call | flops 17179869184 | bytes 16777216 | tf_op jit(solution)/shard_map/pallas_call | solution.py:328
  650.6 18.2 %shard_map.227.refs_1_ = bf16[2,1536,1536]{2,1,0:T(8,128)(2,1)} custom-call(bf16[160,1536]{1,0:T(8,128)(2,1)S(1)} %copy-done.54, bf16[160,1536]{1,0:T(8,128)(2,1)S(1)} %copy-done.56, bf16[1024,1536]{1,0:T(8,128)(2,1)} %pad_maximum_fusion.2.ai.refs_2_, bf16[1024,1536]{1,0:T(8,128)(2,1)} %copy-done.11, bf16[160,1536]{1,0:T(8,128)(2,1)S(1)} %copy-done.80, ...), custom_call_target="tpu_custom_call" | custom-call | flops 17179869184 | bytes 16777216 | tf_op jit(solution)/shard_map/pallas_call | solution.py:328
  717.8 20.6 %collective-permute-done.26.refs_0_ = bf16[296,1536]{1,0:T(8,128)(2,1)S(1)} collective-permute-done((bf16[296,1536]{1,0:T(8,128)(2,1)S(1)}, bf16[296,1536]{1,0:T(8,128)(2,1)S(1)}, u32[]{:S(2)}, u32[]{:S(2)}) %collective-permute-start.26) | collective-permute-done | bytes 909344 | tf_op jit(solution)/shard_map/ppermute | solution.py:350
  761.0 31.1 %shard_map.237 = (bf16[3,1024,384]{2,1,0:T(8,128)(2,1)S(1)}, bf16[3,160,384]{2,1,0:T(8,128)(2,1)S(1)}) custom-call(bf16[3,1024,384]{2,1,0:T(8,128)(2,1)S(1)} %copy-done.78, bf16[3,1024,384]{2,1,0:T(8,128)(2,1)S(1)} %copy-done.78, bf16[3,1024,384]{2,1,0:T(8,128)(2,1)S(1)} %copy-done.78, bf16[3,160,384]{2,1,0:T(8,128)(2,1)S(1)} %copy-done.89, ...), custom_call_target="tpu_custom_call" | custom-call | flops 34359738368 | bytes 16777216 | tf_op jit(solution)/shard_map/pallas_call | solution.py:142
  795.7 31.1 %shard_map.240 = (bf16[3,1024,384]{2,1,0:T(8,128)(2,1)S(1)}, bf16[3,160,384]{2,1,0:T(8,128)(2,1)S(1)}) custom-call(bf16[3,1024,384]{2,1,0:T(8,128)(2,1)S(1)} %copy-done.76, bf16[3,1024,384]{2,1,0:T(8,128)(2,1)S(1)} %copy-done.76, bf16[3,1024,384]{2,1,0:T(8,128)(2,1)S(1)} %copy-done.76, bf16[3,160,384]{2,1,0:T(8,128)(2,1)S(1)} %copy-done.87, ...), custom_call_target="tpu_custom_call" | custom-call | flops 34359738368 | bytes 16777216 | tf_op jit(solution)/shard_map/pallas_call | solution.py:142
  828.3 14.8 %shard_map.241.refs_1_ = bf16[2,8,144,1536]{3,2,1,0:T(8,128)(2,1)} custom-call(bf16[3,160,384]{2,1,0:T(8,128)(2,1)S(1)} %get-tuple-element.96.refs_0_.at, bf16[3,160,384]{2,1,0:T(8,128)(2,1)S(1)} %get-tuple-element.101.refs_1_.at, bf16[3,1024,384]{2,1,0:T(8,128)(2,1)} %copy-done.6, bf16[3,1024,384]{2,1,0:T(8,128)(2,1)} %copy-done.42, ...), custom_call_target="tpu_custom_call" | custom-call | flops 17179869184 | bytes 16777216 | tf_op jit(solution)/shard_map/pallas_call | solution.py:328
  858.1 28.6 %collective-permute-done.32.refs_0_ = bf16[4,2,48,1536]{3,2,1,0:T(8,128)(2,1)S(1)} collective-permute-done((bf16[4,2,48,1536]{3,2,1,0:T(8,128)(2,1)S(1)}, bf16[4,2,48,1536]{3,2,1,0:T(8,128)(2,1)S(1)}, u32[]{:S(2)}, u32[]{:S(2)}) %collective-permute-start.32) | collective-permute-done | bytes 1179680 | tf_op jit(solution)/shard_map/ppermute | solution.py:376
  919.7 39.3 %collective-permute-done.34.refs_0_ = bf16[2,48,1536]{2,1,0:T(8,128)(2,1)} collective-permute-done((bf16[2,48,1536]{2,1,0:T(8,128)(2,1)}, bf16[2,48,1536]{2,1,0:T(8,128)(2,1)}, u32[]{:S(2)}, u32[]{:S(2)}) %collective-permute-start.34) | collective-permute-done | bytes 294944 | tf_op jit(solution)/shard_map/ppermute | solution.py:376
  988.2 25.8 %shard_map.249 = (f32[2,192,2304]{2,1,0:T(8,128)S(1)}, f32[8,8,256]{2,1,0:T(8,128)S(1)}, f32[8,128]{1,0:T(8,128)S(1)}) custom-call(f32[4,8,1152]{2,1,0:T(8,128)S(1)} %shard_map.248.terms, f32[8,128]{1,0:T(8,128)S(1)} %broadcast_in_dim.396.lost, bf16[64,192]{1,0:T(8,128)(2,1)S(1)} %copy-done.95, bf16[2,192,2304]{2,1,0:T(8,128)(2,1)S(1)} %copy-done.65), custom_call_target="tpu_custom_call" | custom-call | flops 8589934592 | bytes 2097152 | tf_op jit(solution)/shard_map/pallas_call | solution.py:586
  1023.9 41.6 %reduce-scatter.8.cloned.1.call-done = bf16[2,144,1536]{2,1,0:T(8,128)(2,1)} async-done(((bf16[2,1152,1536]{2,1,0:T(8,128)(2,1)}), bf16[2,144,1536]{2,1,0:T(8,128)(2,1)}) %reduce-scatter.8.cloned.1.call-update) | async-done | bytes 884752 | tf_op jit(solution)/shard_map/reduce_scatter | solution.py:762
  (811 shorter events, 425.7 us)
Async XLA Ops:
  7.2 146.4 %all-gather.4.cloned.1.call-start = ((), (), s32[]{:S(2)}) async-start(), calls=%async_computation.3 | async-start | bytes 10616832 | tf_op jit(solution)/shard_map/all_gather | solution.py:643
  9.6 321.9 %all-gather.6.cloned.1.call-start = ((), (), s32[]{:S(2)}) async-start(), calls=%async_computation.4 | async-start | bytes 10616832 | tf_op jit(solution)/shard_map/all_gather | solution.py:644
  10.4 420.1 %all-gather.8.cloned.1.call-start = ((), (), s32[]{:S(2)}) async-start(), calls=%async_computation.5 | async-start | bytes 10616832 | tf_op jit(solution)/shard_map/all_gather | solution.py:645
  65.8 26.5 %collective-permute-start.5 = (bf16[592,1536]{1,0:T(8,128)(2,1)}, bf16[592,1536]{1,0:T(8,128)(2,1)}, u32[]{:S(2)}, u32[]{:S(2)}) collective-permute-start(bf16[592,1536]{1,0:T(8,128)(2,1)} %pad_maximum_fusion.10), channel_id=1, source_target_pairs={{0,1},{1,0},{2,3},{3,2},{4,5},{5,4},{6,7},{7,6},{8,9},{9,8},{10,11... | collective-permute-start | bytes 5455880 | tf_op jit(solution)/shard_map/ppermute | solution.py:350
  89.8 653.8 %reduce-scatter.4.cloned.1.call-start = ((), (), s32[]{:S(2)}) async-start(), calls=%async_computation.6 | async-start | bytes 10616832 | tf_op jit(solution)/shard_map/reduce_scatter | solution.py:762
  235.2 23.1 %collective-permute-start.8 = (bf16[296,1536]{1,0:T(8,128)(2,1)S(1)}, bf16[296,1536]{1,0:T(8,128)(2,1)S(1)}, u32[]{:S(2)}, u32[]{:S(2)}) collective-permute-start(bf16[296,1536]{1,0:T(8,128)(2,1)S(1)} %pad_maximum_fusion.26.refs_2_), channel_id=1, source_target_pairs={{0,2},{1,3},{2,0},{3,1},{4,6},{5,7},{6,4},{7,5},{8,10},{9,11},{10,... | collective-permute-start | bytes 2727944 | tf_op jit(solution)/shard_map/ppermute | solution.py:350
  238.3 38.6 %collective-permute-start.3 = (bf16[296,1536]{1,0:T(8,128)(2,1)S(1)}, bf16[296,1536]{1,0:T(8,128)(2,1)S(1)}, u32[]{:S(2)}, u32[]{:S(2)}) collective-permute-start(bf16[296,1536]{1,0:T(8,128)(2,1)S(1)} %pad_maximum_fusion.25), channel_id=1, source_target_pairs={{0,2},{1,3},{2,0},{3,1},{4,6},{5,7},{6,4},{7,5},{8,10},{9,11},{10,... | collective-permute-start | bytes 2727944 | tf_op jit(solution)/shard_map/ppermute | solution.py:350
  283.2 23.2 %collective-permute-start.7 = (bf16[296,1536]{1,0:T(8,128)(2,1)S(1)}, bf16[296,1536]{1,0:T(8,128)(2,1)S(1)}, u32[]{:S(2)}, u32[]{:S(2)}) collective-permute-start(bf16[296,1536]{1,0:T(8,128)(2,1)S(1)} %get-tuple-element.301), channel_id=1, source_target_pairs={{0,2},{1,3},{2,0},{3,1},{4,6},{5,7},{6,4},{7,5},{8,10},{9,11},{10,... | collective-permute-start | bytes 2727944 | tf_op jit(solution)/shard_map/ppermute | solution.py:350
  284.7 39.5 %collective-permute-start.10 = (bf16[296,1536]{1,0:T(8,128)(2,1)S(1)}, bf16[296,1536]{1,0:T(8,128)(2,1)S(1)}, u32[]{:S(2)}, u32[]{:S(2)}) collective-permute-start(bf16[296,1536]{1,0:T(8,128)(2,1)S(1)} %get-tuple-element.300.refs_1_), channel_id=1, source_target_pairs={{0,2},{1,3},{2,0},{3,1},{4,6},{5,7},{6,4},{7,5},{8,10},{9,11},{10,... | collective-permute-start | bytes 2727944 | tf_op jit(solution)/shard_map/ppermute | solution.py:350
  472.6 40.5 %collective-permute-start.16 = (bf16[296,1536]{1,0:T(8,128)(2,1)S(1)}, bf16[296,1536]{1,0:T(8,128)(2,1)S(1)}, u32[]{:S(2)}, u32[]{:S(2)}) collective-permute-start(bf16[296,1536]{1,0:T(8,128)(2,1)S(1)} %pad_maximum_fusion.28.refs_2_), channel_id=1, source_target_pairs={{0,2},{1,3},{2,0},{3,1},{4,6},{5,7},{6,4},{7,5},{8,10},{9,11},{10,... | collective-permute-start | bytes 2727944 | tf_op jit(solution)/shard_map/ppermute | solution.py:350
  498.8 33.2 %collective-permute-start.15 = (bf16[296,1536]{1,0:T(8,128)(2,1)S(1)}, bf16[296,1536]{1,0:T(8,128)(2,1)S(1)}, u32[]{:S(2)}, u32[]{:S(2)}) collective-permute-start(bf16[296,1536]{1,0:T(8,128)(2,1)S(1)} %get-tuple-element.239.refs_1_), channel_id=1, source_target_pairs={{0,2},{1,3},{2,0},{3,1},{4,6},{5,7},{6,4},{7,5},{8,10},{9,11},{10,... | collective-permute-start | bytes 2727944 | tf_op jit(solution)/shard_map/ppermute | solution.py:350
  532.1 23.2 %collective-permute-start.17 = (bf16[592,1536]{1,0:T(8,128)(2,1)S(1)}, bf16[592,1536]{1,0:T(8,128)(2,1)S(1)}, u32[]{:S(2)}, u32[]{:S(2)}) collective-permute-start(bf16[592,1536]{1,0:T(8,128)(2,1)S(1)} %pad_maximum_fusion.16), channel_id=1, source_target_pairs={{0,1},{1,0},{2,3},{3,2},{4,5},{5,4},{6,7},{7,6},{8,9},{9,8},{10,11... | collective-permute-start | bytes 5455880 | tf_op jit(solution)/shard_map/ppermute | solution.py:350
  579.8 336.8 %reduce-scatter.6.cloned.1.call-start = ((), (), s32[]{:S(2)}) async-start(), calls=%async_computation.7 | async-start | bytes 10616832 | tf_op jit(solution)/shard_map/reduce_scatter | solution.py:762
  647.8 26.4 %collective-permute-start.21 = (bf16[296,1536]{1,0:T(8,128)(2,1)S(1)}, bf16[296,1536]{1,0:T(8,128)(2,1)S(1)}, u32[]{:S(2)}, u32[]{:S(2)}) collective-permute-start(bf16[296,1536]{1,0:T(8,128)(2,1)S(1)} %pad_maximum_fusion.29.refs_2_), channel_id=1, source_target_pairs={{0,2},{1,3},{2,0},{3,1},{4,6},{5,7},{6,4},{7,5},{8,10},{9,11},{10,... | collective-permute-start | bytes 2727944 | tf_op jit(solution)/shard_map/ppermute | solution.py:350
  668.8 396.8 %reduce-scatter.8.cloned.1.call-start = ((), (), s32[]{:S(2)}) async-start(), calls=%async_computation.8 | async-start | bytes 7962624 | tf_op jit(solution)/shard_map/reduce_scatter | solution.py:762
  683.2 32.2 %collective-permute-start.23 = (bf16[296,1536]{1,0:T(8,128)(2,1)S(1)}, bf16[296,1536]{1,0:T(8,128)(2,1)S(1)}, u32[]{:S(2)}, u32[]{:S(2)}) collective-permute-start(bf16[296,1536]{1,0:T(8,128)(2,1)S(1)} %fusion.26.refs_2_), channel_id=1, source_target_pairs={{0,2},{1,3},{2,0},{3,1},{4,6},{5,7},{6,4},{7,5},{8,10},{9,11},{10,... | collective-permute-start | bytes 2727944 | tf_op jit(solution)/shard_map/ppermute | solution.py:350
  715.6 23.9 %collective-permute-start.25 = (bf16[592,1536]{1,0:T(8,128)(2,1)S(1)}, bf16[592,1536]{1,0:T(8,128)(2,1)S(1)}, u32[]{:S(2)}, u32[]{:S(2)}) collective-permute-start(bf16[592,1536]{1,0:T(8,128)(2,1)S(1)} %pad_maximum_fusion.20), channel_id=1, source_target_pairs={{0,1},{1,0},{2,3},{3,2},{4,5},{5,4},{6,7},{7,6},{8,9},{9,8},{10,11... | collective-permute-start | bytes 5455880 | tf_op jit(solution)/shard_map/ppermute | solution.py:350
  848.2 38.6 %collective-permute-start.32 = (bf16[4,2,48,1536]{3,2,1,0:T(8,128)(2,1)S(1)}, bf16[4,2,48,1536]{3,2,1,0:T(8,128)(2,1)S(1)}, u32[]{:S(2)}, u32[]{:S(2)}) collective-permute-start(bf16[4,2,48,1536]{3,2,1,0:T(8,128)(2,1)S(1)} %pad_maximum_fusion.24), channel_id=1, source_target_pairs={{0,4},{4,0},{8,12},{12,8},{16,20},{20,16},{24,28},{28,24},{1,5},{5... | collective-permute-start | bytes 3538952 | tf_op jit(solution)/shard_map/ppermute | solution.py:376
  857.8 42.4 %collective-permute-start.30 = (bf16[592,1536]{1,0:T(8,128)(2,1)}, bf16[592,1536]{1,0:T(8,128)(2,1)}, u32[]{:S(2)}, u32[]{:S(2)}) collective-permute-start(bf16[592,1536]{1,0:T(8,128)(2,1)} %get-tuple-element.106), channel_id=1, source_target_pairs={{0,1},{1,0},{2,3},{3,2},{4,5},{5,4},{6,7},{7,6},{8,9},{9,8},{10,11... | collective-permute-start | bytes 5455880 | tf_op jit(solution)/shard_map/ppermute | solution.py:350
  904.3 54.8 %collective-permute-start.31 = (bf16[296,1536]{1,0:T(8,128)(2,1)S(1)}, bf16[296,1536]{1,0:T(8,128)(2,1)}, u32[]{:S(2)}, u32[]{:S(2)}) collective-permute-start(bf16[296,1536]{1,0:T(8,128)(2,1)S(1)} %pad_maximum_fusion.32.refs_2_), channel_id=1, source_target_pairs={{0,2},{1,3},{2,0},{3,1},{4,6},{5,7},{6,4},{7,5},{8,10},{9,11},{10,... | collective-permute-start | bytes 2727944 | tf_op jit(solution)/shard_map/ppermute | solution.py:350
  908.7 50.5 %collective-permute-start.29 = (bf16[296,1536]{1,0:T(8,128)(2,1)}, bf16[296,1536]{1,0:T(8,128)(2,1)}, u32[]{:S(2)}, u32[]{:S(2)}) collective-permute-start(bf16[296,1536]{1,0:T(8,128)(2,1)} %pad_maximum_fusion.31), channel_id=1, source_target_pairs={{0,2},{1,3},{2,0},{3,1},{4,6},{5,7},{6,4},{7,5},{8,10},{9,11},{10,... | collective-permute-start | bytes 2727944 | tf_op jit(solution)/shard_map/ppermute | solution.py:350
  910.7 48.4 %collective-permute-start.33 = (bf16[2,48,1536]{2,1,0:T(8,128)(2,1)}, bf16[2,48,1536]{2,1,0:T(8,128)(2,1)}, u32[]{:S(2)}, u32[]{:S(2)}) collective-permute-start(bf16[2,48,1536]{2,1,0:T(8,128)(2,1)} %get-tuple-element.231), channel_id=1, source_target_pairs={{0,8},{4,12},{8,0},{12,4},{16,24},{20,28},{24,16},{28,20},{1,9},{5... | collective-permute-start | bytes 884744 | tf_op jit(solution)/shard_map/ppermute | solution.py:376
  910.7 48.4 %collective-permute-start.35 = (bf16[2,48,1536]{2,1,0:T(8,128)(2,1)}, bf16[2,48,1536]{2,1,0:T(8,128)(2,1)}, u32[]{:S(2)}, u32[]{:S(2)}) collective-permute-start(bf16[2,48,1536]{2,1,0:T(8,128)(2,1)} %get-tuple-element.232), channel_id=1, source_target_pairs={{0,24},{4,28},{8,16},{12,20},{16,8},{20,12},{24,0},{28,4},{1,25},{... | collective-permute-start | bytes 884744 | tf_op jit(solution)/shard_map/ppermute | solution.py:376
  912.9 46.1 %collective-permute-start.34 = (bf16[2,48,1536]{2,1,0:T(8,128)(2,1)}, bf16[2,48,1536]{2,1,0:T(8,128)(2,1)}, u32[]{:S(2)}, u32[]{:S(2)}) collective-permute-start(bf16[2,48,1536]{2,1,0:T(8,128)(2,1)} %get-tuple-element.233), channel_id=1, source_target_pairs={{0,16},{4,20},{8,24},{12,28},{16,0},{20,4},{24,8},{28,12},{1,17},{... | collective-permute-start | bytes 884744 | tf_op jit(solution)/shard_map/ppermute | solution.py:376
  (224 other events, 4110.1 us)
Sparse Core Ops, SparseCore 0:
  10.8 142.7 all-gather.3
  155.8 136.2 all-gather.5
  294.3 136.2 all-gather.7
  579.9 161.4 reduce-scatter.3
  744.8 168.2 reduce-scatter.5
  916.6 148.8 reduce-scatter.7

commit v6 on v5

--- a/solution.py
+++ b/solution.py
@@ -738,8 +738,6 @@
         v["hid_t"], v["hid_i"], v["slope_t"], v["slope_i"] = up_and_slope(v["h2_t"], v["h2_i"], f_up)
     f_down = after(f_down, slot[-1]["hid_i"])
     for j, v in enumerate(slot):
-        if j:
-            v["hid_t"] = after(v["hid_t"], *slot[j - 1]["go"][0])
         v["go"] = scatter_begin(v["hid_t"], v["hid_i"], f_down, True)
     for j, v in enumerate(slot):
         v["m"] = scatter_end(v["go"], slot[j - 1]["go"][0])

time: 1080 us -> 1080 us (level)
  waiting for transfers between devices: 460 us -> 449 us
    unnamed x418 -> x426, local copies, waits for them, and re-layouts: 84.4 us -> 84.3 us
  transfers between devices with their start and end apart: 42 -> 42, of which waited for: 24 -> 23; matrix products, arithmetic and copies ran while one was open for 13% -> 13% of each run, Pallas kernels for 29% -> 30%
where the time goes in v6:
time: 1080 us; the launch traced here: 1070 us
  waiting for transfers between devices  449 us (42%)
  Pallas kernels  346 us (32%)
  local copies, waits for them, and re-layouts  125 us (12%)
  other arithmetic  104 us (10%)
  starting transfers between devices  24.3 us (2%)
  between operations  22.4 us (2%)
    ppermute x32, waiting for transfers between devices, send(): lax.ppermute(value, 'tensor', [(t, t ^ flip) for t in range(self.size)])  230 us
    pallas_call x14, Pallas kernels, over_columns(): pl.pallas_call(kernel, grid=(columns // step,), in_specs=[whole(v) for v...  109 us
    unnamed x426, local copies, waits for them, and re-layouts  84.3 us
    ppermute x4, waiting for transfers between devices, send(): return lax.ppermute(value, 'dp', [(p, p ^ flip) for p in range(self.size)])  68.5 us
    pallas_call x2, Pallas kernels, attend_back(): pl.pallas_call(partial(back_kernel, block, valid), grid=(pairs,), in_spec...  62.2 us
    pallas_call x4, Pallas kernels, outer(): pl.pallas_call(partial(outer_kernel, n), grid=(steps,), in_specs=[l_spec(...  59.1 us
    all_gather x1, waiting for transfers between devices, on_device(): f_down = lax.all_gather(w_down, 'dp', axis=1, tiled=True)  56.6 us
    pallas_call x2, Pallas kernels, attend(): pl.pallas_call(partial(attend_kernel, block, valid), grid=(pairs,), in_sp...  52.7 us
  transfers between devices with their start and end apart: 42, of which 23 were waited for; matrix products, arithmetic and copies ran while one was open for 13% of the time, Pallas kernels for 30%

profile of v6, /device:TPU:0, one launch (start us, length us, event | category | flops | bytes accessed | tf_op | source)
XLA Modules:
  0.0 1070.3 jit_solution(9972140839996678839)
XLA Ops:
  11.1 22.6 %shard_map.196 = (f32[4,8,1152]{2,1,0:T(8,128)S(1)}, bf16[64,192]{1,0:T(8,128)(2,1)S(1)}) custom-call(f32[8,8,256]{2,1,0:T(8,128)S(1)} %select_maximum_fusion.cond, bf16[2,192,2304]{2,1,0:T(8,128)(2,1)S(1)} %copy-done.62), custom_call_target="tpu_custom_call" | custom-call | flops 8589934592 | bytes 2097152 | tf_op jit(solution)/shard_map/pallas_call | solution.py:507
  42.2 22.3 %collective-permute-done.4.refs_0_ = bf16[296,1536]{1,0:T(8,128)(2,1)S(1)} collective-permute-done((bf16[296,1536]{1,0:T(8,128)(2,1)S(1)}, bf16[296,1536]{1,0:T(8,128)(2,1)S(1)}, u32[]{:S(2)}, u32[]{:S(2)}) %collective-permute-start.4) | collective-permute-done | bytes 909344 | tf_op jit(solution)/shard_map/ppermute | solution.py:350
  66.2 22.2 %collective-permute-done.refs_0_ = bf16[296,1536]{1,0:T(8,128)(2,1)S(1)} collective-permute-done((bf16[296,1536]{1,0:T(8,128)(2,1)S(1)}, bf16[296,1536]{1,0:T(8,128)(2,1)S(1)}, u32[]{:S(2)}, u32[]{:S(2)}) %collective-permute-start) | collective-permute-done | bytes 909344 | tf_op jit(solution)/shard_map/ppermute | solution.py:350
  101.0 52.6 %all-gather.4.cloned.1.call-done = bf16[2,4,6,64,1536]{4,3,2,1,0:T(8,128)(2,1)} async-done(((bf16[2,4,6,8,1536]{4,3,2,1,0:T(8,128)(2,1)}), bf16[2,4,6,64,1536]{4,3,2,1,0:T(8,128)(2,1)}) %all-gather.4.cloned.1.call-update) | async-done | bytes 9437200 | tf_op jit(solution)/shard_map/all_gather | solution.py:643
  164.5 26.2 %shard_map.199 = (bf16[1024,384]{1,0:T(8,128)(2,1)S(1)}, bf16[160,384]{1,0:T(8,128)(2,1)S(1)}, f32[3,2,1184]{2,1,0:T(2,128)S(1)}) custom-call(bf16[3,1024,384]{2,1,0:T(8,128)(2,1)S(1)} %get-tuple-element.61.qi.ki.vi, bf16[3,1024,384]{2,1,0:T(8,128)(2,1)S(1)} %get-tuple-element.61.qi.ki.vi, bf16[3,1024,384]{2,1,0:T(8,128)(2,1)S(1)} %get-tuple-element.61.qi.ki.vi, ...), custom_call_target="tpu_custom_call" | custom-call | flops 17179869184 | bytes 8388608 | tf_op jit(solution)/shard_map/pallas_call | solution.py:123
  199.1 26.5 %shard_map.204 = (bf16[1024,384]{1,0:T(8,128)(2,1)S(1)}, bf16[160,384]{1,0:T(8,128)(2,1)S(1)}, f32[3,2,1184]{2,1,0:T(2,128)S(1)}) custom-call(bf16[3,1024,384]{2,1,0:T(8,128)(2,1)S(1)} %get-tuple-element.67.qi.ki.vi, bf16[3,1024,384]{2,1,0:T(8,128)(2,1)S(1)} %get-tuple-element.67.qi.ki.vi, bf16[3,1024,384]{2,1,0:T(8,128)(2,1)S(1)} %get-tuple-element.67.qi.ki.vi, ...), custom_call_target="tpu_custom_call" | custom-call | flops 17179869184 | bytes 8388608 | tf_op jit(solution)/shard_map/pallas_call | solution.py:123
  239.9 18.3 %collective-permute-done.8.refs_0_ = bf16[296,1536]{1,0:T(8,128)(2,1)S(1)} collective-permute-done((bf16[296,1536]{1,0:T(8,128)(2,1)S(1)}, bf16[296,1536]{1,0:T(8,128)(2,1)S(1)}, u32[]{:S(2)}, u32[]{:S(2)}) %collective-permute-start.8) | collective-permute-done | bytes 909344 | tf_op jit(solution)/shard_map/ppermute | solution.py:350
  258.3 18.7 %collective-permute-done.3.refs_0_ = bf16[296,1536]{1,0:T(8,128)(2,1)S(1)} collective-permute-done((bf16[296,1536]{1,0:T(8,128)(2,1)S(1)}, bf16[296,1536]{1,0:T(8,128)(2,1)S(1)}, u32[]{:S(2)}, u32[]{:S(2)}) %collective-permute-start.3) | collective-permute-done | bytes 909344 | tf_op jit(solution)/shard_map/ppermute | solution.py:350
  285.3 21.1 %collective-permute-done.7.refs_0_ = bf16[296,1536]{1,0:T(8,128)(2,1)S(1)} collective-permute-done((bf16[296,1536]{1,0:T(8,128)(2,1)S(1)}, bf16[296,1536]{1,0:T(8,128)(2,1)S(1)}, u32[]{:S(2)}, u32[]{:S(2)}) %collective-permute-start.7) | collective-permute-done | bytes 909344 | tf_op jit(solution)/shard_map/ppermute | solution.py:350
  308.9 15.3 %collective-permute-done.10.refs_0_ = bf16[296,1536]{1,0:T(8,128)(2,1)S(1)} collective-permute-done((bf16[296,1536]{1,0:T(8,128)(2,1)S(1)}, bf16[296,1536]{1,0:T(8,128)(2,1)S(1)}, u32[]{:S(2)}, u32[]{:S(2)}) %collective-permute-start.10) | collective-permute-done | bytes 909344 | tf_op jit(solution)/shard_map/ppermute | solution.py:350
  373.9 56.6 %all-gather.8.cloned.1.call-done.refs_0_ = bf16[2,1536,1536]{2,1,0:T(8,128)(2,1)} async-done(((bf16[2,192,1536]{2,1,0:T(8,128)(2,1)}), bf16[2,1536,1536]{2,1,0:T(8,128)(2,1)}) %all-gather.8.cloned.1.call-update) | async-done | bytes 9437200 | tf_op jit(solution)/shard_map/all_gather | solution.py:645
  467.5 17.6 %collective-permute-done.13.refs_0_ = bf16[296,1536]{1,0:T(8,128)(2,1)S(1)} collective-permute-done((bf16[296,1536]{1,0:T(8,128)(2,1)S(1)}, bf16[296,1536]{1,0:T(8,128)(2,1)S(1)}, u32[]{:S(2)}, u32[]{:S(2)}) %collective-permute-start.13) | collective-permute-done | bytes 909344 | tf_op jit(solution)/shard_map/ppermute | solution.py:350
  509.7 14.0 %collective-permute-done.15.refs_0_ = bf16[296,1536]{1,0:T(8,128)(2,1)S(1)} collective-permute-done((bf16[296,1536]{1,0:T(8,128)(2,1)S(1)}, bf16[296,1536]{1,0:T(8,128)(2,1)S(1)}, u32[]{:S(2)}, u32[]{:S(2)}) %collective-permute-start.15) | collective-permute-done | bytes 909344 | tf_op jit(solution)/shard_map/ppermute | solution.py:350
  525.4 21.0 %collective-permute-done.18.refs_0_ = bf16[296,1536]{1,0:T(8,128)(2,1)S(1)} collective-permute-done((bf16[296,1536]{1,0:T(8,128)(2,1)S(1)}, bf16[296,1536]{1,0:T(8,128)(2,1)S(1)}, u32[]{:S(2)}, u32[]{:S(2)}) %collective-permute-start.18) | collective-permute-done | bytes 909344 | tf_op jit(solution)/shard_map/ppermute | solution.py:350
  552.4 18.2 %shard_map.220.refs_1_ = bf16[2,1536,1536]{2,1,0:T(8,128)(2,1)} custom-call(bf16[160,1536]{1,0:T(8,128)(2,1)S(1)} %pad_maximum_fusion.36.refs_0_.at, bf16[160,1536]{1,0:T(8,128)(2,1)S(1)} %pad_maximum_fusion.37.refs_1_.at, bf16[1024,1536]{1,0:T(8,128)(2,1)} %pad_maximum_fusion.4.refs_2_.refs_0_, bf16[1024,1536]{1,0:T(8,128)(2,1)} %pad_maximum_fusion.5.refs_3_.refs_0_, ...), custom_call_target="tpu_custom_call" | custom-call | flops 17179869184 | bytes 16777216 | tf_op jit(solution)/shard_map/pallas_call | solution.py:328
  642.4 18.2 %shard_map.226.refs_1_ = bf16[2,1536,1536]{2,1,0:T(8,128)(2,1)} custom-call(bf16[160,1536]{1,0:T(8,128)(2,1)S(1)} %copy-done.52, bf16[160,1536]{1,0:T(8,128)(2,1)S(1)} %copy-done.54, bf16[1024,1536]{1,0:T(8,128)(2,1)} %pad_maximum_fusion.2.ai.refs_2_, bf16[1024,1536]{1,0:T(8,128)(2,1)} %copy-done.11, bf16[160,1536]{1,0:T(8,128)(2,1)S(1)} %copy-done.78, ...), custom_call_target="tpu_custom_call" | custom-call | flops 17179869184 | bytes 16777216 | tf_op jit(solution)/shard_map/pallas_call | solution.py:328
  709.7 20.6 %collective-permute-done.26.refs_0_ = bf16[296,1536]{1,0:T(8,128)(2,1)S(1)} collective-permute-done((bf16[296,1536]{1,0:T(8,128)(2,1)S(1)}, bf16[296,1536]{1,0:T(8,128)(2,1)S(1)}, u32[]{:S(2)}, u32[]{:S(2)}) %collective-permute-start.26) | collective-permute-done | bytes 909344 | tf_op jit(solution)/shard_map/ppermute | solution.py:350
  752.9 31.1 %shard_map.236 = (bf16[3,1024,384]{2,1,0:T(8,128)(2,1)S(1)}, bf16[3,160,384]{2,1,0:T(8,128)(2,1)S(1)}) custom-call(bf16[3,1024,384]{2,1,0:T(8,128)(2,1)S(1)} %copy-done.76, bf16[3,1024,384]{2,1,0:T(8,128)(2,1)S(1)} %copy-done.76, bf16[3,1024,384]{2,1,0:T(8,128)(2,1)S(1)} %copy-done.76, bf16[3,160,384]{2,1,0:T(8,128)(2,1)S(1)} %copy-done.89, ...), custom_call_target="tpu_custom_call" | custom-call | flops 34359738368 | bytes 16777216 | tf_op jit(solution)/shard_map/pallas_call | solution.py:142
  787.5 31.1 %shard_map.239 = (bf16[3,1024,384]{2,1,0:T(8,128)(2,1)S(1)}, bf16[3,160,384]{2,1,0:T(8,128)(2,1)S(1)}) custom-call(bf16[3,1024,384]{2,1,0:T(8,128)(2,1)S(1)} %copy-done.74, bf16[3,1024,384]{2,1,0:T(8,128)(2,1)S(1)} %copy-done.74, bf16[3,1024,384]{2,1,0:T(8,128)(2,1)S(1)} %copy-done.74, bf16[3,160,384]{2,1,0:T(8,128)(2,1)S(1)} %copy-done.87, ...), custom_call_target="tpu_custom_call" | custom-call | flops 34359738368 | bytes 16777216 | tf_op jit(solution)/shard_map/pallas_call | solution.py:142
  820.1 14.8 %shard_map.240.refs_1_ = bf16[2,8,144,1536]{3,2,1,0:T(8,128)(2,1)} custom-call(bf16[3,160,384]{2,1,0:T(8,128)(2,1)S(1)} %get-tuple-element.96.refs_0_.at, bf16[3,160,384]{2,1,0:T(8,128)(2,1)S(1)} %get-tuple-element.101.refs_1_.at, bf16[3,1024,384]{2,1,0:T(8,128)(2,1)} %copy-done.6, bf16[3,1024,384]{2,1,0:T(8,128)(2,1)} %copy-done.42, ...), custom_call_target="tpu_custom_call" | custom-call | flops 17179869184 | bytes 16777216 | tf_op jit(solution)/shard_map/pallas_call | solution.py:328
  849.9 28.8 %collective-permute-done.32.refs_0_ = bf16[4,2,48,1536]{3,2,1,0:T(8,128)(2,1)S(1)} collective-permute-done((bf16[4,2,48,1536]{3,2,1,0:T(8,128)(2,1)S(1)}, bf16[4,2,48,1536]{3,2,1,0:T(8,128)(2,1)S(1)}, u32[]{:S(2)}, u32[]{:S(2)}) %collective-permute-start.32) | collective-permute-done | bytes 1179680 | tf_op jit(solution)/shard_map/ppermute | solution.py:376
  911.8 39.7 %collective-permute-done.34.refs_0_ = bf16[2,48,1536]{2,1,0:T(8,128)(2,1)} collective-permute-done((bf16[2,48,1536]{2,1,0:T(8,128)(2,1)}, bf16[2,48,1536]{2,1,0:T(8,128)(2,1)}, u32[]{:S(2)}, u32[]{:S(2)}) %collective-permute-start.34) | collective-permute-done | bytes 294944 | tf_op jit(solution)/shard_map/ppermute | solution.py:376
  980.7 25.8 %shard_map.248 = (f32[2,192,2304]{2,1,0:T(8,128)S(1)}, f32[8,8,256]{2,1,0:T(8,128)S(1)}, f32[8,128]{1,0:T(8,128)S(1)}) custom-call(f32[4,8,1152]{2,1,0:T(8,128)S(1)} %shard_map.247.terms, f32[8,128]{1,0:T(8,128)S(1)} %broadcast_in_dim.396.lost, bf16[64,192]{1,0:T(8,128)(2,1)S(1)} %copy-done.95, bf16[2,192,2304]{2,1,0:T(8,128)(2,1)S(1)} %copy-done.63), custom_call_target="tpu_custom_call" | custom-call | flops 8589934592 | bytes 2097152 | tf_op jit(solution)/shard_map/pallas_call | solution.py:586
  1016.4 41.1 %reduce-scatter.8.cloned.1.call-done = bf16[2,144,1536]{2,1,0:T(8,128)(2,1)} async-done(((bf16[2,1152,1536]{2,1,0:T(8,128)(2,1)}), bf16[2,144,1536]{2,1,0:T(8,128)(2,1)}) %reduce-scatter.8.cloned.1.call-update) | async-done | bytes 884752 | tf_op jit(solution)/shard_map/reduce_scatter | solution.py:760
  (817 shorter events, 423.4 us)
Async XLA Ops:
  7.2 146.4 %all-gather.4.cloned.1.call-start = ((), (), s32[]{:S(2)}) async-start(), calls=%async_computation.3 | async-start | bytes 10616832 | tf_op jit(solution)/shard_map/all_gather | solution.py:643
  9.6 323.5 %all-gather.6.cloned.1.call-start = ((), (), s32[]{:S(2)}) async-start(), calls=%async_computation.4 | async-start | bytes 10616832 | tf_op jit(solution)/shard_map/all_gather | solution.py:644
  10.4 420.1 %all-gather.8.cloned.1.call-start = ((), (), s32[]{:S(2)}) async-start(), calls=%async_computation.5 | async-start | bytes 10616832 | tf_op jit(solution)/shard_map/all_gather | solution.py:645
  65.8 26.5 %collective-permute-start.5 = (bf16[592,1536]{1,0:T(8,128)(2,1)}, bf16[592,1536]{1,0:T(8,128)(2,1)}, u32[]{:S(2)}, u32[]{:S(2)}) collective-permute-start(bf16[592,1536]{1,0:T(8,128)(2,1)} %pad_maximum_fusion.10), channel_id=1, source_target_pairs={{0,1},{1,0},{2,3},{3,2},{4,5},{5,4},{6,7},{7,6},{8,9},{9,8},{10,11... | collective-permute-start | bytes 5455880 | tf_op jit(solution)/shard_map/ppermute | solution.py:350
  89.8 645.7 %reduce-scatter.4.cloned.1.call-start = ((), (), s32[]{:S(2)}) async-start(), calls=%async_computation.6 | async-start | bytes 10616832 | tf_op jit(solution)/shard_map/reduce_scatter | solution.py:760
  235.2 23.1 %collective-permute-start.8 = (bf16[296,1536]{1,0:T(8,128)(2,1)S(1)}, bf16[296,1536]{1,0:T(8,128)(2,1)S(1)}, u32[]{:S(2)}, u32[]{:S(2)}) collective-permute-start(bf16[296,1536]{1,0:T(8,128)(2,1)S(1)} %pad_maximum_fusion.25.refs_2_), channel_id=1, source_target_pairs={{0,2},{1,3},{2,0},{3,1},{4,6},{5,7},{6,4},{7,5},{8,10},{9,11},{10,... | collective-permute-start | bytes 2727944 | tf_op jit(solution)/shard_map/ppermute | solution.py:350
  238.3 38.6 %collective-permute-start.3 = (bf16[296,1536]{1,0:T(8,128)(2,1)S(1)}, bf16[296,1536]{1,0:T(8,128)(2,1)S(1)}, u32[]{:S(2)}, u32[]{:S(2)}) collective-permute-start(bf16[296,1536]{1,0:T(8,128)(2,1)S(1)} %pad_maximum_fusion.24), channel_id=1, source_target_pairs={{0,2},{1,3},{2,0},{3,1},{4,6},{5,7},{6,4},{7,5},{8,10},{9,11},{10,... | collective-permute-start | bytes 2727944 | tf_op jit(solution)/shard_map/ppermute | solution.py:350
  283.2 23.2 %collective-permute-start.7 = (bf16[296,1536]{1,0:T(8,128)(2,1)S(1)}, bf16[296,1536]{1,0:T(8,128)(2,1)S(1)}, u32[]{:S(2)}, u32[]{:S(2)}) collective-permute-start(bf16[296,1536]{1,0:T(8,128)(2,1)S(1)} %get-tuple-element.301), channel_id=1, source_target_pairs={{0,2},{1,3},{2,0},{3,1},{4,6},{5,7},{6,4},{7,5},{8,10},{9,11},{10,... | collective-permute-start | bytes 2727944 | tf_op jit(solution)/shard_map/ppermute | solution.py:350
  284.7 39.5 %collective-permute-start.10 = (bf16[296,1536]{1,0:T(8,128)(2,1)S(1)}, bf16[296,1536]{1,0:T(8,128)(2,1)S(1)}, u32[]{:S(2)}, u32[]{:S(2)}) collective-permute-start(bf16[296,1536]{1,0:T(8,128)(2,1)S(1)} %get-tuple-element.300.refs_1_), channel_id=1, source_target_pairs={{0,2},{1,3},{2,0},{3,1},{4,6},{5,7},{6,4},{7,5},{8,10},{9,11},{10,... | collective-permute-start | bytes 2727944 | tf_op jit(solution)/shard_map/ppermute | solution.py:350
  465.8 38.8 %collective-permute-start.16 = (bf16[296,1536]{1,0:T(8,128)(2,1)S(1)}, bf16[296,1536]{1,0:T(8,128)(2,1)S(1)}, u32[]{:S(2)}, u32[]{:S(2)}) collective-permute-start(bf16[296,1536]{1,0:T(8,128)(2,1)S(1)} %pad_maximum_fusion.27.refs_2_), channel_id=1, source_target_pairs={{0,2},{1,3},{2,0},{3,1},{4,6},{5,7},{6,4},{7,5},{8,10},{9,11},{10,... | collective-permute-start | bytes 2727944 | tf_op jit(solution)/shard_map/ppermute | solution.py:350
  490.2 33.4 %collective-permute-start.15 = (bf16[296,1536]{1,0:T(8,128)(2,1)S(1)}, bf16[296,1536]{1,0:T(8,128)(2,1)S(1)}, u32[]{:S(2)}, u32[]{:S(2)}) collective-permute-start(bf16[296,1536]{1,0:T(8,128)(2,1)S(1)} %get-tuple-element.239.refs_1_), channel_id=1, source_target_pairs={{0,2},{1,3},{2,0},{3,1},{4,6},{5,7},{6,4},{7,5},{8,10},{9,11},{10,... | collective-permute-start | bytes 2727944 | tf_op jit(solution)/shard_map/ppermute | solution.py:350
  523.8 23.2 %collective-permute-start.17 = (bf16[592,1536]{1,0:T(8,128)(2,1)S(1)}, bf16[592,1536]{1,0:T(8,128)(2,1)S(1)}, u32[]{:S(2)}, u32[]{:S(2)}) collective-permute-start(bf16[592,1536]{1,0:T(8,128)(2,1)S(1)} %pad_maximum_fusion.15), channel_id=1, source_target_pairs={{0,1},{1,0},{2,3},{3,2},{4,5},{5,4},{6,7},{7,6},{8,9},{9,8},{10,11... | collective-permute-start | bytes 5455880 | tf_op jit(solution)/shard_map/ppermute | solution.py:350
  571.4 337.1 %reduce-scatter.6.cloned.1.call-start = ((), (), s32[]{:S(2)}) async-start(), calls=%async_computation.7 | async-start | bytes 10616832 | tf_op jit(solution)/shard_map/reduce_scatter | solution.py:760
  639.6 26.4 %collective-permute-start.21 = (bf16[296,1536]{1,0:T(8,128)(2,1)S(1)}, bf16[296,1536]{1,0:T(8,128)(2,1)S(1)}, u32[]{:S(2)}, u32[]{:S(2)}) collective-permute-start(bf16[296,1536]{1,0:T(8,128)(2,1)S(1)} %pad_maximum_fusion.28.refs_2_), channel_id=1, source_target_pairs={{0,2},{1,3},{2,0},{3,1},{4,6},{5,7},{6,4},{7,5},{8,10},{9,11},{10,... | collective-permute-start | bytes 2727944 | tf_op jit(solution)/shard_map/ppermute | solution.py:350
  660.6 396.8 %reduce-scatter.8.cloned.1.call-start = ((), (), s32[]{:S(2)}) async-start(), calls=%async_computation.8 | async-start | bytes 7962624 | tf_op jit(solution)/shard_map/reduce_scatter | solution.py:760
  675.0 32.3 %collective-permute-start.23 = (bf16[296,1536]{1,0:T(8,128)(2,1)S(1)}, bf16[296,1536]{1,0:T(8,128)(2,1)S(1)}, u32[]{:S(2)}, u32[]{:S(2)}) collective-permute-start(bf16[296,1536]{1,0:T(8,128)(2,1)S(1)} %fusion.26.refs_2_), channel_id=1, source_target_pairs={{0,2},{1,3},{2,0},{3,1},{4,6},{5,7},{6,4},{7,5},{8,10},{9,11},{10,... | collective-permute-start | bytes 2727944 | tf_op jit(solution)/shard_map/ppermute | solution.py:350
  707.4 23.9 %collective-permute-start.25 = (bf16[592,1536]{1,0:T(8,128)(2,1)S(1)}, bf16[592,1536]{1,0:T(8,128)(2,1)S(1)}, u32[]{:S(2)}, u32[]{:S(2)}) collective-permute-start(bf16[592,1536]{1,0:T(8,128)(2,1)S(1)} %pad_maximum_fusion.19), channel_id=1, source_target_pairs={{0,1},{1,0},{2,3},{3,2},{4,5},{5,4},{6,7},{7,6},{8,9},{9,8},{10,11... | collective-permute-start | bytes 5455880 | tf_op jit(solution)/shard_map/ppermute | solution.py:350
  839.9 38.8 %collective-permute-start.32 = (bf16[4,2,48,1536]{3,2,1,0:T(8,128)(2,1)S(1)}, bf16[4,2,48,1536]{3,2,1,0:T(8,128)(2,1)S(1)}, u32[]{:S(2)}, u32[]{:S(2)}) collective-permute-start(bf16[4,2,48,1536]{3,2,1,0:T(8,128)(2,1)S(1)} %pad_maximum_fusion.23), channel_id=1, source_target_pairs={{0,4},{4,0},{8,12},{12,8},{16,20},{20,16},{24,28},{28,24},{1,5},{5... | collective-permute-start | bytes 3538952 | tf_op jit(solution)/shard_map/ppermute | solution.py:376
  849.6 42.7 %collective-permute-start.30 = (bf16[592,1536]{1,0:T(8,128)(2,1)}, bf16[592,1536]{1,0:T(8,128)(2,1)}, u32[]{:S(2)}, u32[]{:S(2)}) collective-permute-start(bf16[592,1536]{1,0:T(8,128)(2,1)} %get-tuple-element.106), channel_id=1, source_target_pairs={{0,1},{1,0},{2,3},{3,2},{4,5},{5,4},{6,7},{7,6},{8,9},{9,8},{10,11... | collective-permute-start | bytes 5455880 | tf_op jit(solution)/shard_map/ppermute | solution.py:350
  896.3 55.2 %collective-permute-start.31 = (bf16[296,1536]{1,0:T(8,128)(2,1)S(1)}, bf16[296,1536]{1,0:T(8,128)(2,1)}, u32[]{:S(2)}, u32[]{:S(2)}) collective-permute-start(bf16[296,1536]{1,0:T(8,128)(2,1)S(1)} %pad_maximum_fusion.31.refs_2_), channel_id=1, source_target_pairs={{0,2},{1,3},{2,0},{3,1},{4,6},{5,7},{6,4},{7,5},{8,10},{9,11},{10,... | collective-permute-start | bytes 2727944 | tf_op jit(solution)/shard_map/ppermute | solution.py:350
  900.9 50.7 %collective-permute-start.29 = (bf16[296,1536]{1,0:T(8,128)(2,1)}, bf16[296,1536]{1,0:T(8,128)(2,1)}, u32[]{:S(2)}, u32[]{:S(2)}) collective-permute-start(bf16[296,1536]{1,0:T(8,128)(2,1)} %pad_maximum_fusion.30), channel_id=1, source_target_pairs={{0,2},{1,3},{2,0},{3,1},{4,6},{5,7},{6,4},{7,5},{8,10},{9,11},{10,... | collective-permute-start | bytes 2727944 | tf_op jit(solution)/shard_map/ppermute | solution.py:350
  902.7 48.7 %collective-permute-start.33 = (bf16[2,48,1536]{2,1,0:T(8,128)(2,1)}, bf16[2,48,1536]{2,1,0:T(8,128)(2,1)}, u32[]{:S(2)}, u32[]{:S(2)}) collective-permute-start(bf16[2,48,1536]{2,1,0:T(8,128)(2,1)} %get-tuple-element.231), channel_id=1, source_target_pairs={{0,8},{4,12},{8,0},{12,4},{16,24},{20,28},{24,16},{28,20},{1,9},{5... | collective-permute-start | bytes 884744 | tf_op jit(solution)/shard_map/ppermute | solution.py:376
  902.7 48.7 %collective-permute-start.35 = (bf16[2,48,1536]{2,1,0:T(8,128)(2,1)}, bf16[2,48,1536]{2,1,0:T(8,128)(2,1)}, u32[]{:S(2)}, u32[]{:S(2)}) collective-permute-start(bf16[2,48,1536]{2,1,0:T(8,128)(2,1)} %get-tuple-element.232), channel_id=1, source_target_pairs={{0,24},{4,28},{8,16},{12,20},{16,8},{20,12},{24,0},{28,4},{1,25},{... | collective-permute-start | bytes 884744 | tf_op jit(solution)/shard_map/ppermute | solution.py:376
  904.7 46.7 %collective-permute-start.34 = (bf16[2,48,1536]{2,1,0:T(8,128)(2,1)}, bf16[2,48,1536]{2,1,0:T(8,128)(2,1)}, u32[]{:S(2)}, u32[]{:S(2)}) collective-permute-start(bf16[2,48,1536]{2,1,0:T(8,128)(2,1)} %get-tuple-element.233), channel_id=1, source_target_pairs={{0,16},{4,20},{8,24},{12,28},{16,0},{20,4},{24,8},{28,12},{1,17},{... | collective-permute-start | bytes 884744 | tf_op jit(solution)/shard_map/ppermute | solution.py:376
  (228 other events, 4288.0 us)
Sparse Core Ops, SparseCore 0:
  10.8 142.7 all-gather.3
  155.8 136.2 all-gather.5
  294.3 136.2 all-gather.7
  571.6 161.5 reduce-scatter.3
  736.6 168.2 reduce-scatter.5
  908.4 148.9 reduce-scatter.7
